TPU v7x, 256 devices: a whole 4x4x8 slice. The times are simulated.
256 devices in a mesh: gx: 8 (over z), gy: 32 (over y, x, core).
Axes of the slice: x: 4, y: 4, z: 8, core: 2. Of those that a mesh axis runs over, the one named last changes fastest.
Arguments:
- right_side: float32 [64, 64, 4096], P(None, 'gx', 'gy'), may hold values from -4 to 4
- alpha: float32 [64, 64, 4096], P(None, 'gx', 'gy'), may hold values from 0.0001 to 1
- beta: float32 [64, 64, 4096], P(None, 'gx', 'gy'), may hold values from 0.5 to 2
Outputs:
- solution_field: float32 [64, 64, 4096], P(None, 'gx', 'gy')
- residual: float32 [64, 64, 4096], P(None, 'gx', 'gy')
All inputs are finite; a program needn't handle non-finite values.
Results may differ from a plain program's by a relative error of at most 0.0003.
Values sent between devices are 32-bit elements; how exact they have to be, the bound alone decides.
No kernel may reach another device: no remote copies, remote signals or barrier semaphores. Data moves between devices by JAX's collectives and lax.ppermute only.
A program may use at most 128 MiB of HBM per device.

v0:
```python
import jax
import jax.numpy as jnp
from jax import lax
from jax.sharding import PartitionSpec as P

LEVELS = 4
SMOOTHS = 3
BOTTOM = 12


def extended(value, sides, width):
    for axis, dim in sides:
        devices, length = (lax.axis_size(axis), value.shape[dim])
        up = [(i, (i + 1) % devices) for i in range(devices - 1)]
        down = [(j, i) for i, j in up]
        last = lax.slice_in_dim(value, length - width, length, axis=dim)
        first = lax.slice_in_dim(value, 0, width, axis=dim)
        before = lax.ppermute(last, axis, up)
        after = lax.ppermute(first, axis, down)
        value = jnp.concatenate([before, value, after], axis=dim)
    return value


def partner_2(value, axis, stride):
    mask = 2**stride
    pairs = [(source, source ^ mask) for source in range(lax.axis_size(axis))]
    return lax.ppermute(value, axis, pairs)


def face_weights(padded_beta, factor):
    centre = padded_beta[:, 1:-1, 1:-1]
    along_z = jnp.pad(centre, ((1, 1), (0, 0), (0, 0)))
    face_z = factor * (0.5 * (along_z[1:] + along_z[:-1]))
    face_x = factor * (0.5 * (padded_beta[:, 1:, 1:-1] + padded_beta[:, :-1, 1:-1]))
    face_y = factor * (0.5 * (padded_beta[:, 1:-1, 1:] + padded_beta[:, 1:-1, :-1]))
    return (face_z, face_x, face_y)


def build_level(alpha_level, padded_beta, factor):
    face_z, face_x, face_y = face_weights(padded_beta, factor)
    diagonal = alpha_level + (
        face_z[1:]
        + face_z[:-1]
        + face_x[:, 1:]
        + face_x[:, :-1]
        + face_y[:, :, 1:]
        + face_y[:, :, :-1]
    )
    return (diagonal, face_z, face_x, face_y)


def apply_rims(padded, operator):
    diagonal, face_z, face_x, face_y = operator
    centre = padded[:, 1:-1, 1:-1]
    along_z = jnp.pad(centre, ((1, 1), (0, 0), (0, 0)))
    beside = face_z[:-1] * along_z[:-2] + face_z[1:] * along_z[2:]
    beside = beside + face_x[:, :-1] * padded[:, :-2, 1:-1] + face_x[:, 1:] * padded[:, 2:, 1:-1]
    beside = (
        beside + face_y[:, :, :-1] * padded[:, 1:-1, :-2] + face_y[:, :, 1:] * padded[:, 1:-1, 2:]
    )
    return diagonal * centre - beside


def zero_rims(field):
    return jnp.pad(field, ((0, 0), (1, 1), (1, 1)))


def remote_rims(field):
    return extended(field, (("gx", 1), ("gy", 2)), 1)


def coefficient_rims(beta_level):
    return extended(beta_level, (("gx", 1), ("gy", 2)), 1)


def coarsen(field):
    planes, across, along = field.shape
    return field.reshape(planes // 2, 2, across // 2, 2, along // 2, 2).mean(axis=(1, 3, 5))


def refine(field):
    planes, across, along = field.shape
    wide = jnp.broadcast_to(field[:, None, :, None, :, None], (planes, 2, across, 2, along, 2))
    return wide.reshape(2 * planes, 2 * across, 2 * along)


def relax_once(iterate, source, operator, weight, rims_fn):
    return iterate + weight * (source - apply_rims(rims_fn(iterate), operator)) / operator[0]


def bottom_sweeps(source, operator, rims_fn):

    def one_sweep(turn, iterate):
        return relax_once(iterate, source, operator, 0.8, rims_fn)

    return lax.fori_loop(0, BOTTOM, one_sweep, jnp.zeros_like(source))


def replicated_bottom(pieces, planes, width_x, width_y, factor):
    source_all, alpha_all, beta_all = pieces
    operator = build_level(alpha_all, zero_rims(beta_all), factor)
    iterate_all = bottom_sweeps(source_all, operator, zero_rims)
    start_x = lax.axis_index("gx") * width_x
    start_y = lax.axis_index("gy") * width_y
    return lax.dynamic_slice(
        iterate_all, (jnp.zeros((), jnp.int32), start_x, start_y), (planes, width_x, width_y)
    )


def body(right_side, alpha, beta):
    alpha_levels = [alpha]
    beta_levels = [beta]
    for height in range(1, LEVELS):
        alpha_levels.append(coarsen(alpha_levels[-1]))
        beta_levels.append(coarsen(beta_levels[-1]))
    operators = []
    for height in range(LEVELS - 1):
        operators.append(
            build_level(alpha_levels[height], coefficient_rims(beta_levels[height]), 0.25**height)
        )
    sources = []
    smoothed = []
    source = right_side
    for height in range(LEVELS - 1):
        iterate = 0.6 * source / operators[height][0]
        for turn in range(1, SMOOTHS):
            iterate = relax_once(
                iterate, source, operators[height], 0.6 + 0.15 * (turn % 3), remote_rims
            )
        sources.append(source)
        smoothed.append(iterate)
        source = coarsen(source - apply_rims(remote_rims(iterate), operators[height]))
    alpha_low = alpha_levels[-1]
    beta_low = beta_levels[-1]
    bottom_factor = 0.25 ** (LEVELS - 1)
    planes, width_x, width_y = source.shape
    pieces = (source, alpha_low, beta_low)
    for position in range(lax.axis_size("gy").bit_length() - 1):
        partner = partner_2((pieces[0], pieces[1], pieces[2]), "gy", position)
        is_lower = lax.axis_index("gy") // 2**position % 2 == 0
        pieces = tuple(
            (
                jnp.where(
                    is_lower, jnp.concatenate((mine, theirs), 2), jnp.concatenate((theirs, mine), 2)
                )
                for mine, theirs in zip(pieces, partner)
            )
        )
    for position in range(lax.axis_size("gx").bit_length() - 1):
        partner = partner_2((pieces[0], pieces[1], pieces[2]), "gx", position)
        is_lower = lax.axis_index("gx") // 2**position % 2 == 0
        pieces = tuple(
            (
                jnp.where(
                    is_lower, jnp.concatenate((mine, theirs), 1), jnp.concatenate((theirs, mine), 1)
                )
                for mine, theirs in zip(pieces, partner)
            )
        )
    iterate = replicated_bottom(pieces, planes, width_x, width_y, bottom_factor)
    for height in reversed(range(LEVELS - 1)):
        iterate = smoothed[height] + refine(iterate)
        for turn in range(SMOOTHS):
            iterate = relax_once(
                iterate, sources[height], operators[height], 0.6 + 0.15 * (turn % 3), remote_rims
            )
    residual = right_side - apply_rims(remote_rims(iterate), operators[0])
    return (iterate, residual)


def solution(mesh):
    return jax.shard_map(
        body,
        mesh=mesh,
        in_specs=(P(None, "gx", "gy"), P(None, "gx", "gy"), P(None, "gx", "gy")),
        out_specs=(P(None, "gx", "gy"), P(None, "gx", "gy")),
        check_vma=False,
    )
```

profile of v0, /device:TPU:7, one launch (start us, length us, event | category | flops | bytes accessed | tf_op | source)
XLA Modules:
  0.0 647.3 jit_solution(953877036055249246)
XLA Ops:
  7.4 18.9 %reshape.1649 = f32[32,2,4,2,64,2]{5,4,3,2,1,0:T(8,128)} reshape(f32[64,8,128]{2,1,0:T(8,128)} %param.7) | data formatting | bytes 524288 | tf_op jit(solution)/shard_map/reshape | solution.py:78
  26.2 7.0 %reduce_sum.104 = f32[32,4,64]{2,1,0:T(4,128)S(1)} reduce(f32[32,2,4,2,64,2]{5,4,3,2,1,0:T(8,128)} %reshape.1649, f32[]{:T(128)} %constant.190.clone.1), dimensions={1,3,5}, to_apply=%region_2.0 | reduce | flops 57344 | bytes 294916 | tf_op jit(solution)/shard_map/reduce_sum | solution.py:78
  42.8 18.1 %reshape.1648 = f32[32,2,4,2,64,2]{5,4,3,2,1,0:T(8,128)} reshape(f32[64,8,128]{2,1,0:T(8,128)S(1)} %copy-done) | data formatting | bytes 524288 | tf_op jit(solution)/shard_map/reshape | solution.py:78
  61.0 7.0 %reduce_sum.103 = f32[32,4,64]{2,1,0:T(4,128)S(1)} reduce(f32[32,2,4,2,64,2]{5,4,3,2,1,0:T(8,128)} %reshape.1648, f32[]{:T(128)} %constant.190.clone.1), dimensions={1,3,5}, to_apply=%region_1.0 | reduce | flops 57344 | bytes 294916 | tf_op jit(solution)/shard_map/reduce_sum | solution.py:78
  120.4 7.5 %collective-permute-start.6 = (f32[64,10,1]{2,1,0:T(8,128)S(1)}, f32[64,10,1]{2,1,0:T(8,128)S(1)}, u32[]{:S(2)}, u32[]{:S(2)}) collective-permute-start(f32[64,10,1]{2,1,0:T(8,128)S(1)} %get-tuple-element.165), channel_id=1, source_target_pairs={{0,1},{1,2},{2,3},{3,4},{4,5},{5,6},{6,7},{7,8},{8,9},{9,10},{10,1... | collective-permute-start | bytes 7688 | tf_op jit(solution)/shard_map/ppermute | solution.py:18
  133.9 6.7 %collective-permute-done.7 = f32[64,10,1]{2,1,0:T(8,128)S(1)} collective-permute-done((f32[64,10,1]{2,1,0:T(8,128)S(1)}, f32[64,10,1]{2,1,0:T(8,128)S(1)}, u32[]{:S(2)}, u32[]{:S(2)}) %collective-permute-start.7) | collective-permute-done | bytes 2592 | tf_op jit(solution)/shard_map/ppermute | solution.py:19
  149.3 5.8 collective-permute-start.19
  163.4 6.5 %collective-permute-done.11 = f32[64,10,1]{2,1,0:T(8,128)S(1)} collective-permute-done((f32[64,10,1]{2,1,0:T(8,128)S(1)}, f32[64,10,1]{2,1,0:T(8,128)S(1)}, u32[]{:S(2)}, u32[]{:S(2)}) %collective-permute-start.11) | collective-permute-done | bytes 2592 | tf_op jit(solution)/shard_map/ppermute | solution.py:19
  190.4 6.5 %collective-permute-done.15 = f32[64,10,1]{2,1,0:T(8,128)S(1)} collective-permute-done((f32[64,10,1]{2,1,0:T(8,128)S(1)}, f32[64,10,1]{2,1,0:T(8,128)S(1)}, u32[]{:S(2)}, u32[]{:S(2)}) %collective-permute-start.15) | collective-permute-done | bytes 2592 | tf_op jit(solution)/shard_map/ppermute | solution.py:19
  197.5 18.1 %reshape.1647 = f32[32,2,4,2,64,2]{5,4,3,2,1,0:T(8,128)} reshape(f32[64,8,128]{2,1,0:T(8,128)S(1)} %fusion.73) | data formatting | bytes 524288 | tf_op jit(solution)/shard_map/reshape | solution.py:78
  215.6 7.0 %reduce_sum.102 = f32[32,4,64]{2,1,0:T(4,128)S(1)} reduce(f32[32,2,4,2,64,2]{5,4,3,2,1,0:T(8,128)} %reshape.1647, f32[]{:T(128)} %constant.190.clone.1), dimensions={1,3,5}, to_apply=%region_0.0 | reduce | flops 57344 | bytes 294916 | tf_op jit(solution)/shard_map/reduce_sum | solution.py:78
  257.5 6.4 collective-permute-done.27
  306.7 6.9 %collective-permute-start.38 = (f32[16,4,1]{2,0,1:T(8,128)S(1)}, f32[16,4,1]{2,0,1:T(8,128)S(1)}, u32[]{:S(2)}, u32[]{:S(2)}) collective-permute-start(f32[16,4,1]{2,0,1:T(8,128)S(1)} %get-tuple-element.224), channel_id=1, source_target_pairs={{0,1},{1,2},{2,3},{3,4},{4,5},{5,6},{6,7},{7,8},{8,9},{9,10},{10,1... | collective-permute-start | bytes 776 | tf_op jit(solution)/shard_map/ppermute | solution.py:18
  407.3 11.1 %collective-permute-start.74 = (f32[16,4,1]{2,0,1:T(8,128)S(1)}, f32[16,4,1]{2,0,1:T(8,128)S(1)}, u32[]{:S(2)}, u32[]{:S(2)}) collective-permute-start(f32[16,4,1]{2,0,1:T(8,128)S(1)} %get-tuple-element.218), channel_id=1, source_target_pairs={{0,1},{1,2},{2,3},{3,4},{4,5},{5,6},{6,7},{7,8},{8,9},{9,10},{10,1... | collective-permute-start | bytes 776 | tf_op jit(solution)/shard_map/ppermute | solution.py:18
  439.9 5.4 collective-permute-done.79
  484.4 6.5 collective-permute-done.87
  503.9 6.5 collective-permute-done.91
  523.4 6.5 collective-permute-done.95
  530.2 6.6 %broadcast_in_dim.33 = f32[32,2,4,2,64,2]{5,4,3,2,1,0:T(8,128)} broadcast(f32[32,4,64]{2,1,0:T(4,128)S(1)} %fusion.119), dimensions={0,2,4} | broadcast | bytes 294912 | tf_op jit(solution)/shard_map/broadcast_in_dim | solution.py:83
  536.8 12.6 %reshape.1652 = f32[64,8,128]{2,1,0:T(8,128)S(1)} reshape(f32[32,2,4,2,64,2]{5,4,3,2,1,0:T(8,128)} %broadcast_in_dim.33) | data formatting | bytes 524288 | tf_op jit(solution)/shard_map/reshape | solution.py:84
  566.7 6.5 %collective-permute-done.99 = f32[64,10,1]{2,1,0:T(8,128)S(1)} collective-permute-done((f32[64,10,1]{2,1,0:T(8,128)S(1)}, f32[64,10,1]{2,1,0:T(8,128)S(1)}, u32[]{:S(2)}, u32[]{:S(2)}) %collective-permute-start.99) | collective-permute-done | bytes 2592 | tf_op jit(solution)/shard_map/ppermute | solution.py:19
  590.9 6.5 %collective-permute-done.103 = f32[64,10,1]{2,1,0:T(8,128)S(1)} collective-permute-done((f32[64,10,1]{2,1,0:T(8,128)S(1)}, f32[64,10,1]{2,1,0:T(8,128)S(1)}, u32[]{:S(2)}, u32[]{:S(2)}) %collective-permute-start.103) | collective-permute-done | bytes 2592 | tf_op jit(solution)/shard_map/ppermute | solution.py:19
  615.1 6.5 %collective-permute-done.107 = f32[64,10,1]{2,1,0:T(8,128)S(1)} collective-permute-done((f32[64,10,1]{2,1,0:T(8,128)S(1)}, f32[64,10,1]{2,1,0:T(8,128)S(1)}, u32[]{:S(2)}, u32[]{:S(2)}) %collective-permute-start.107) | collective-permute-done | bytes 2592 | tf_op jit(solution)/shard_map/ppermute | solution.py:19
  639.4 6.5 %collective-permute-done.111 = f32[64,10,1]{2,1,0:T(8,128)S(1)} collective-permute-done((f32[64,10,1]{2,1,0:T(8,128)S(1)}, f32[64,10,1]{2,1,0:T(8,128)S(1)}, u32[]{:S(2)}, u32[]{:S(2)}) %collective-permute-start.111) | collective-permute-done | bytes 2592 | tf_op jit(solution)/shard_map/ppermute | solution.py:19
  (428 shorter events, 443.6 us)
Async XLA Ops:
  1.8 92.6 %collective-permute-start = (f32[64,1,128]{2,1,0:T(1,128)S(1)}, f32[64,1,128]{2,1,0:T(1,128)S(1)}, u32[]{:S(2)}, u32[]{:S(2)}) collective-permute-start(f32[64,1,128]{2,1,0:T(1,128)S(1)} %get-tuple-element.184), channel_id=1, source_target_pairs={{32,0},{64,32},{96,64},{128,96},{160,128},{192,160},{224,192},{33,... | collective-permute-start | bytes 98312 | tf_op jit(solution)/shard_map/ppermute | solution.py:19
  3.1 91.3 %collective-permute-start.1 = (f32[64,1,128]{2,1,0:T(1,128)S(1)}, f32[64,1,128]{2,1,0:T(1,128)S(1)}, u32[]{:S(2)}, u32[]{:S(2)}) collective-permute-start(f32[64,1,128]{2,1,0:T(1,128)S(1)} %get-tuple-element.183), channel_id=1, source_target_pairs={{0,32},{32,64},{64,96},{96,128},{128,160},{160,192},{192,224},{1,3... | collective-permute-start | bytes 98312 | tf_op jit(solution)/shard_map/ppermute | solution.py:18
  33.3 96.6 %collective-permute-start.16 = (f32[32,1,64]{2,1,0:T(1,128)S(1)}, f32[32,1,64]{2,1,0:T(1,128)S(1)}, u32[]{:S(2)}, u32[]{:S(2)}) collective-permute-start(f32[32,1,64]{2,1,0:T(1,128)S(1)} %get-tuple-element.213), channel_id=1, source_target_pairs={{32,0},{64,32},{96,64},{128,96},{160,128},{192,160},{224,192},{33,... | collective-permute-start | bytes 24584 | tf_op jit(solution)/shard_map/ppermute | solution.py:19
  39.9 35.7 %collective-permute-start.32 = (f32[16,1,32]{2,0,1:T(8,128)S(1)}, f32[16,1,32]{2,0,1:T(8,128)S(1)}, u32[]{:S(2)}, u32[]{:S(2)}) collective-permute-start(f32[16,1,32]{2,0,1:T(8,128)S(1)} %get-tuple-element.245), channel_id=1, source_target_pairs={{32,0},{64,32},{96,64},{128,96},{160,128},{192,160},{224,192},{33,... | collective-permute-start | bytes 6152 | tf_op jit(solution)/shard_map/ppermute | solution.py:19
  41.5 26.6 %collective-permute-start.52 = (f32[8,1,16]{2,0,1:T(8,128)S(1)}, f32[8,1,16]{2,0,1:T(8,128)S(1)}, u32[]{:S(2)}, u32[]{:S(2)}) collective-permute-start(f32[8,1,16]{2,0,1:T(8,128)S(1)} %get-tuple-element.251), channel_id=1, source_target_pairs={{0,1},{1,0},{2,3},{3,2},{4,5},{5,4},{6,7},{7,6},{8,9},{9,8},{10,11... | collective-permute-start | bytes 1544 | tf_op jit(solution)/shard_map/ppermute | solution.py:27
  84.1 45.8 %collective-permute-start.17 = (f32[32,1,64]{2,1,0:T(1,128)S(1)}, f32[32,1,64]{2,1,0:T(1,128)S(1)}, u32[]{:S(2)}, u32[]{:S(2)}) collective-permute-start(f32[32,1,64]{2,1,0:T(1,128)S(1)} %get-tuple-element.212), channel_id=1, source_target_pairs={{0,32},{32,64},{64,96},{96,128},{128,160},{160,192},{192,224},{1,3... | collective-permute-start | bytes 24584 | tf_op jit(solution)/shard_map/ppermute | solution.py:18
  94.7 12.7 %collective-permute-start.2 = (f32[64,10,1]{2,1,0:T(8,128)S(1)}, f32[64,10,1]{2,1,0:T(8,128)S(1)}, u32[]{:S(2)}, u32[]{:S(2)}) collective-permute-start(f32[64,10,1]{2,1,0:T(8,128)S(1)} %get-tuple-element.167), channel_id=1, source_target_pairs={{1,0},{2,1},{3,2},{4,3},{5,4},{6,5},{7,6},{8,7},{9,8},{10,9},{11,1... | collective-permute-start | bytes 7688 | tf_op jit(solution)/shard_map/ppermute | solution.py:19
  115.0 71.3 %collective-permute-start.56 = (f32[8,1,256]{2,0,1:T(8,128)S(1)}, f32[8,1,256]{2,0,1:T(8,128)S(1)}, u32[]{:S(2)}, u32[]{:S(2)}) collective-permute-start(f32[8,1,256]{2,0,1:T(8,128)S(1)} %maximum_select_fusion.15), channel_id=1, source_target_pairs={{0,16},{1,17},{2,18},{3,19},{4,20},{5,21},{6,22},{7,23},{8,24},{9,... | collective-permute-start | bytes 24584 | tf_op jit(solution)/shard_map/ppermute | solution.py:27
  120.4 13.4 %collective-permute-start.6 = (f32[64,10,1]{2,1,0:T(8,128)S(1)}, f32[64,10,1]{2,1,0:T(8,128)S(1)}, u32[]{:S(2)}, u32[]{:S(2)}) collective-permute-start(f32[64,10,1]{2,1,0:T(8,128)S(1)} %get-tuple-element.165), channel_id=1, source_target_pairs={{0,1},{1,2},{2,3},{3,4},{4,5},{5,6},{6,7},{7,8},{8,9},{9,10},{10,1... | collective-permute-start | bytes 7688 | tf_op jit(solution)/shard_map/ppermute | solution.py:18
  127.9 12.6 %collective-permute-start.7 = (f32[64,10,1]{2,1,0:T(8,128)S(1)}, f32[64,10,1]{2,1,0:T(8,128)S(1)}, u32[]{:S(2)}, u32[]{:S(2)}) collective-permute-start(f32[64,10,1]{2,1,0:T(8,128)S(1)} %get-tuple-element.166), channel_id=1, source_target_pairs={{1,0},{2,1},{3,2},{4,3},{5,4},{6,5},{7,6},{8,7},{9,8},{10,9},{11,1... | collective-permute-start | bytes 7688 | tf_op jit(solution)/shard_map/ppermute | solution.py:19
  141.2 13.9 %collective-permute-start.8 = (f32[64,1,128]{2,1,0:T(1,128)S(1)}, f32[64,1,128]{2,1,0:T(1,128)S(1)}, u32[]{:S(2)}, u32[]{:S(2)}) collective-permute-start(f32[64,1,128]{2,1,0:T(1,128)S(1)} %get-tuple-element.179), channel_id=1, source_target_pairs={{0,32},{32,64},{64,96},{96,128},{128,160},{160,192},{192,224},{1,3... | collective-permute-start | bytes 98312 | tf_op jit(solution)/shard_map/ppermute | solution.py:18
  147.4 28.9 %collective-permute-start.18 = (f32[32,6,1]{2,1,0:T(8,128)S(1)}, f32[32,6,1]{2,1,0:T(8,128)S(1)}, u32[]{:S(2)}, u32[]{:S(2)}) collective-permute-start(f32[32,6,1]{2,1,0:T(8,128)S(1)} %get-tuple-element.197), channel_id=1, source_target_pairs={{1,0},{2,1},{3,2},{4,3},{5,4},{6,5},{7,6},{8,7},{9,8},{10,9},{11,1... | collective-permute-start | bytes 2312 | tf_op jit(solution)/shard_map/ppermute | solution.py:19
  149.3 26.9 %collective-permute-start.19 = (f32[32,6,1]{2,1,0:T(8,128)S(1)}, f32[32,6,1]{2,1,0:T(8,128)S(1)}, u32[]{:S(2)}, u32[]{:S(2)}) collective-permute-start(f32[32,6,1]{2,1,0:T(8,128)S(1)} %get-tuple-element.198), channel_id=1, source_target_pairs={{0,1},{1,2},{2,3},{3,4},{4,5},{5,6},{6,7},{7,8},{8,9},{9,10},{10,1... | collective-permute-start | bytes 2312 | tf_op jit(solution)/shard_map/ppermute | solution.py:18
  157.3 12.6 %collective-permute-start.11 = (f32[64,10,1]{2,1,0:T(8,128)S(1)}, f32[64,10,1]{2,1,0:T(8,128)S(1)}, u32[]{:S(2)}, u32[]{:S(2)}) collective-permute-start(f32[64,10,1]{2,1,0:T(8,128)S(1)} %get-tuple-element.164), channel_id=1, source_target_pairs={{1,0},{2,1},{3,2},{4,3},{5,4},{6,5},{7,6},{8,7},{9,8},{10,9},{11,1... | collective-permute-start | bytes 7688 | tf_op jit(solution)/shard_map/ppermute | solution.py:19
  184.3 12.6 %collective-permute-start.15 = (f32[64,10,1]{2,1,0:T(8,128)S(1)}, f32[64,10,1]{2,1,0:T(8,128)S(1)}, u32[]{:S(2)}, u32[]{:S(2)}) collective-permute-start(f32[64,10,1]{2,1,0:T(8,128)S(1)} %get-tuple-element.162), channel_id=1, source_target_pairs={{1,0},{2,1},{3,2},{4,3},{5,4},{6,5},{7,6},{8,7},{9,8},{10,9},{11,1... | collective-permute-start | bytes 7688 | tf_op jit(solution)/shard_map/ppermute | solution.py:19
  186.2 41.4 %collective-permute-start.57 = (f32[8,1,512]{2,0,1:T(8,128)S(1)}, f32[8,1,512]{2,0,1:T(8,128)S(1)}, u32[]{:S(2)}, u32[]{:S(2)}) collective-permute-start(f32[8,1,512]{2,0,1:T(8,128)S(1)} %maximum_select_fusion.10), channel_id=1, source_target_pairs={{0,32},{32,0},{64,96},{96,64},{128,160},{160,128},{192,224},{224,1... | collective-permute-start | bytes 49160 | tf_op jit(solution)/shard_map/ppermute | solution.py:27
  237.1 11.8 %collective-permute-start.59 = (f32[8,4,512]{2,0,1:T(8,128)S(1)}, f32[8,4,512]{2,0,1:T(8,128)S(1)}, u32[]{:S(2)}, u32[]{:S(2)}) collective-permute-start(f32[8,4,512]{2,0,1:T(8,128)S(1)} %maximum_select_fusion.4), channel_id=1, source_target_pairs={{0,128},{32,160},{64,192},{96,224},{128,0},{160,32},{192,64},{224,... | collective-permute-start | bytes 196616 | tf_op jit(solution)/shard_map/ppermute | solution.py:27
  273.2 13.2 %collective-permute-start.30 = (f32[32,6,1]{2,1,0:T(8,128)}, f32[32,6,1]{2,1,0:T(8,128)}, u32[]{:S(2)}, u32[]{:S(2)}) collective-permute-start(f32[32,6,1]{2,1,0:T(8,128)} %get-tuple-element.191), channel_id=1, source_target_pairs={{0,1},{1,2},{2,3},{3,4},{4,5},{5,6},{6,7},{7,8},{8,9},{9,10},{10,1... | collective-permute-start | bytes 2312 | tf_op jit(solution)/shard_map/ppermute | solution.py:18
  315.6 18.4 %collective-permute-start.45 = (f32[8,1,32]{2,0,1:T(8,128)S(1)}, f32[8,1,32]{2,0,1:T(8,128)S(1)}, u32[]{:S(2)}, u32[]{:S(2)}) collective-permute-start(f32[8,1,32]{2,0,1:T(8,128)S(1)} %maximum_select_fusion.19), channel_id=1, source_target_pairs={{0,2},{1,3},{2,0},{3,1},{4,6},{5,7},{6,4},{7,5},{8,10},{9,11},{10,... | collective-permute-start | bytes 3080 | tf_op jit(solution)/shard_map/ppermute | solution.py:27
  407.3 14.1 %collective-permute-start.74 = (f32[16,4,1]{2,0,1:T(8,128)S(1)}, f32[16,4,1]{2,0,1:T(8,128)S(1)}, u32[]{:S(2)}, u32[]{:S(2)}) collective-permute-start(f32[16,4,1]{2,0,1:T(8,128)S(1)} %get-tuple-element.218), channel_id=1, source_target_pairs={{0,1},{1,2},{2,3},{3,4},{4,5},{5,6},{6,7},{7,8},{8,9},{9,10},{10,1... | collective-permute-start | bytes 776 | tf_op jit(solution)/shard_map/ppermute | solution.py:18
  560.5 12.6 %collective-permute-start.99 = (f32[64,10,1]{2,1,0:T(8,128)S(1)}, f32[64,10,1]{2,1,0:T(8,128)S(1)}, u32[]{:S(2)}, u32[]{:S(2)}) collective-permute-start(f32[64,10,1]{2,1,0:T(8,128)S(1)} %get-tuple-element.160), channel_id=1, source_target_pairs={{1,0},{2,1},{3,2},{4,3},{5,4},{6,5},{7,6},{8,7},{9,8},{10,9},{11,1... | collective-permute-start | bytes 7688 | tf_op jit(solution)/shard_map/ppermute | solution.py:19
  584.8 12.6 %collective-permute-start.103 = (f32[64,10,1]{2,1,0:T(8,128)S(1)}, f32[64,10,1]{2,1,0:T(8,128)S(1)}, u32[]{:S(2)}, u32[]{:S(2)}) collective-permute-start(f32[64,10,1]{2,1,0:T(8,128)S(1)} %get-tuple-element.158), channel_id=1, source_target_pairs={{1,0},{2,1},{3,2},{4,3},{5,4},{6,5},{7,6},{8,7},{9,8},{10,9},{11,1... | collective-permute-start | bytes 7688 | tf_op jit(solution)/shard_map/ppermute | solution.py:19
  609.0 12.6 %collective-permute-start.107 = (f32[64,10,1]{2,1,0:T(8,128)S(1)}, f32[64,10,1]{2,1,0:T(8,128)S(1)}, u32[]{:S(2)}, u32[]{:S(2)}) collective-permute-start(f32[64,10,1]{2,1,0:T(8,128)S(1)} %get-tuple-element.156), channel_id=1, source_target_pairs={{1,0},{2,1},{3,2},{4,3},{5,4},{6,5},{7,6},{8,7},{9,8},{10,9},{11,1... | collective-permute-start | bytes 7688 | tf_op jit(solution)/shard_map/ppermute | solution.py:19
  633.3 12.6 %collective-permute-start.111 = (f32[64,10,1]{2,1,0:T(8,128)S(1)}, f32[64,10,1]{2,1,0:T(8,128)S(1)}, u32[]{:S(2)}, u32[]{:S(2)}) collective-permute-start(f32[64,10,1]{2,1,0:T(8,128)S(1)} %get-tuple-element.154), channel_id=1, source_target_pairs={{1,0},{2,1},{3,2},{4,3},{5,4},{6,5},{7,6},{8,7},{9,8},{10,9},{11,1... | collective-permute-start | bytes 7688 | tf_op jit(solution)/shard_map/ppermute | solution.py:19
  (100 other events, 762.0 us)
where the time goes:
time: 659 us; the launch traced here: 647 us
  starting transfers between devices  272 us (41%)
  waiting for transfers between devices  213 us (32%)
  local copies, waits for them, and re-layouts  102 us (15%)
  other arithmetic  56.1 us (9%)
    ppermute x44, waiting for transfers between devices, extended(): after = lax.ppermute(first, axis, down)  165 us
    ppermute x44, starting transfers between devices, extended(): before = lax.ppermute(last, axis, up)  164 us
    ppermute x44, starting transfers between devices, extended(): after = lax.ppermute(first, axis, down)  76.3 us
    reshape x4, local copies, waits for them, and re-layouts, coarsen(): field.reshape(planes // 2, 2, across // 2, 2, along // 2, 2)  59.4 us
    reduce_sum x12, other arithmetic, coarsen(): field.reshape(planes // 2, 2, across // 2, 2, along // 2, 2)  31.9 us
    ppermute x24, starting transfers between devices, partner_2(): return lax.ppermute(value, axis, pairs)  31.9 us
    ppermute x44, waiting for transfers between devices, extended(): before = lax.ppermute(last, axis, up)  28.4 us
    ppermute x24, waiting for transfers between devices, partner_2(): return lax.ppermute(value, axis, pairs)  19.5 us
  transfers between devices with their start and end apart: 112, of which 55 were waited for; matrix products, arithmetic and copies ran while one was open for 16% of the time, Pallas kernels for 0%

commit v1 on v0

v1 whole, which is shorter than its diff:
```python
import functools

import jax
import jax.numpy as jnp
from jax import lax
from jax.experimental import pallas as pl
from jax.experimental.pallas import tpu as pltpu
from jax.sharding import PartitionSpec as P

F32 = jnp.float32
WEIGHTS = (0.6, 0.75, 0.9)
BOTTOM_WEIGHT = 0.8
BOTTOM = 12
YH = 20


def roll(x, shift, axis):
    shift %= x.shape[axis]
    return x if shift == 0 else pltpu.roll(x, shift, axis)


def iota(shape, axis):
    return lax.broadcasted_iota(jnp.int32, shape, axis)


def either(flag, a, b):
    return jnp.where(flag, a, b)


def only(flag, a):
    return jnp.where(flag, a, 0.0)


def matmul(a, b):
    return jnp.dot(a, b, precision=lax.Precision.HIGHEST, preferred_element_type=F32)


def indicator(mask):
    return jnp.where(mask, 1.0, 0.0).astype(F32)


def half_wrapped(i, low, high):
    return jnp.where(i < high, i // 2, jnp.where(i >= low, 64 + i // 2, -1))


class Level:
    def __init__(self, refs, factor, circular, unroll):
        self.f, self.a, self.b, self.ws, self.wl, self.wm, self.inv, self.diag, self.u, self.v = refs
        self.half = 0.5 * factor
        self.circular = circular
        self.planes, self.rows, self.lanes = self.f.shape
        self.unroll = unroll

    def build(self):
        shape = (self.rows, self.lanes)
        sub = iota(shape, 0)
        half = self.half
        self.b[self.planes] = jnp.zeros(shape, F32)
        self.u[self.planes] = jnp.zeros(shape, F32)
        self.v[self.planes] = jnp.zeros(shape, F32)

        def step(m, carry):
            before, b = carry
            after = self.b[m + 1]
            wl = half * (b + roll(b, -1, 1))
            beside = roll(b, -1, 0)
            if not self.circular:
                beside = only(sub < self.rows - 1, beside)
            ws = half * (b + beside)
            wm = half * (b + after)
            below = roll(ws, 1, 0)
            if not self.circular:
                below = jnp.where(sub == 0, half * b, below)
            diag = self.a[m] + (wl + roll(wl, 1, 1) + ws + below + wm + before)
            inv = jnp.where(b > 0.0, 1.0 / diag, 0.0)
            self.ws[m] = ws if self.circular else only(sub < self.rows - 1, ws)
            self.wl[m] = wl
            self.wm[m] = wm
            self.diag[m] = diag
            self.inv[m] = inv
            return wm, after

        first = self.b[0]
        lax.fori_loop(0, self.planes, step, (half * first, first), unroll=self.unroll)

    def start(self, weight):
        def step(m, carry):
            self.u[m] = (weight * self.f[m]) * self.inv[m]
            return carry

        lax.fori_loop(0, self.planes, step, 0, unroll=self.unroll)

    def beside(self, m, u, after, flow):
        wl, ws, wm = self.wl[m], self.ws[m], self.wm[m]
        along = wl * roll(u, -1, 1) + roll(wl * u, 1, 1)
        across = ws * roll(u, -1, 0) + roll(ws * u, 1, 0)
        return self.f[m] + (along + across + (wm * after + flow)), wm * u

    def sweep(self, weight, src, dst):
        def step(m, carry):
            flow, u = carry
            after = src[m + 1]
            total, flow = self.beside(m, u, after, flow)
            dst[m] = (1.0 - weight) * u + (weight * self.inv[m]) * total
            return flow, after

        first = src[0]
        lax.fori_loop(0, self.planes, step, (jnp.zeros_like(first), first), unroll=self.unroll)

    def sweeps_down(self):
        self.start(WEIGHTS[0])
        self.sweep(WEIGHTS[1], self.u, self.v)
        self.sweep(WEIGHTS[2], self.v, self.u)

    def sweeps_up(self):
        self.sweep(WEIGHTS[0], self.u, self.v)
        self.sweep(WEIGHTS[1], self.v, self.u)
        self.sweep(WEIGHTS[2], self.u, self.v)

    def residual_pairs(self, src, dst, rows):
        def step(m, carry):
            flow, u = carry
            total = None
            for k in (2 * m, 2 * m + 1):
                after = src[k + 1]
                part, flow = self.beside(k, u, after, flow)
                part = (part - self.diag[k] * u)[:rows]
                total = part if total is None else total + part
                u = after
            dst[m] = total
            return flow, u

        first = src[0]
        lax.fori_loop(0, self.planes // 2, step, (jnp.zeros_like(first), first), unroll=max(self.unroll // 2, 1))

    def residual(self, src, dst, rows, lanes):
        def step(m, carry):
            flow, u = carry
            after = src[m + 1]
            part, flow = self.beside(m, u, after, flow)
            dst[m] = (part - self.diag[m] * u)[:rows, :lanes]
            return flow, after

        first = src[0]
        lax.fori_loop(0, self.planes, step, (jnp.zeros_like(first), first), unroll=self.unroll)


def sum_planes(src, dst, rows):
    def step(m, carry):
        dst[m] = src[2 * m][:rows] + src[2 * m + 1][:rows]
        return carry

    lax.fori_loop(0, dst.shape[0], step, 0, unroll=4)


def places():
    ix, iy = lax.axis_index("gx"), lax.axis_index("gy")
    nx, ny = lax.axis_size("gx"), lax.axis_size("gy")
    return ix, iy, ix % 2 == 0, iy % 2 == 0, ix < nx - 1, ix > 0, iy < ny - 1, iy > 0


def pack_kernel(f, a, b, ya, yb, xa, xb):
    ix, iy, even_x, even_y, *_ = places()
    lane, sub = iota((8, 128), 1), iota((8, 128), 0)

    def y_side(z, shift):
        return jnp.where(
            lane < YH,
            roll(f[z], shift, 1),
            jnp.where(lane < 2 * YH, roll(a[z], shift + YH, 1), roll(b[z], shift + 2 * YH, 1)),
        )

    def y_step(z, carry):
        low = jnp.where(lane < 64, y_side(z, 0), roll(y_side(z + 32, 0), 64, 1))
        high = jnp.where(lane < 64, y_side(z, YH), roll(y_side(z + 32, YH), 64, 1))
        ya[z] = either(even_y, high, low)
        yb[z] = either(even_y, low, high)
        return carry

    lax.fori_loop(0, 32, y_step, 0, unroll=2)

    def x_step(q, carry):
        extra_low = extra_high = jnp.zeros((8, 128), F32)
        for j in range(4):
            z = 4 * q + j
            fz, az, bz = f[z], a[z], b[z]
            low = jnp.where(sub < 3, fz, jnp.where(sub < 6, roll(az, 3, 0), roll(bz, 6, 0)))
            high = jnp.where(sub < 3, roll(fz, 3, 0), jnp.where(sub < 6, roll(az, 6, 0), roll(bz, 2, 0)))
            here = sub // 2 == j
            extra_low = jnp.where(here, roll(bz, 2 * j - 2, 0), extra_low)
            extra_high = jnp.where(here, roll(bz, 2 * j - 6, 0), extra_high)
            xa[z] = either(even_x, high, low)
            xb[z] = either(even_x, low, high)
        xa[64 + q] = either(even_x, extra_high, extra_low)
        xb[64 + q] = either(even_x, extra_low, extra_high)
        return carry

    lax.fori_loop(0, 16, x_step, 0)


def corner_kernel(ya, yb, ca, cb):
    ix, iy, even_x, even_y, *_ = places()
    sub = iota((8, 128), 0)

    def step(z, carry):
        right, left = either(even_y, ya[z], yb[z]), either(even_y, yb[z], ya[z])
        low = jnp.where(sub < 4, left, roll(right, 4, 0))
        high = jnp.where(sub < 4, roll(left, 4, 0), right)
        ca[z] = either(even_x, high, low)
        cb[z] = either(even_x, low, high)
        return carry

    lax.fori_loop(0, 32, step, 0, unroll=4)


def fine_down_kernel(
    f, a, b, xa, xb, ya, yb, ca, cb,
    pack, ra, rb, own_u, f_out, ws_out, wl_out, wm_out, inv_out, diag_out,
    fx, ax, bx, ws, wl, wm, inv, diag, u, v, pairs, wide, sems,
):
    ix, iy, even_x, even_y, has_right, has_left, has_above, has_below = places()
    lane, sub = iota((8, 128), 1), iota((8, 128), 0)

    def unpack(q, carry):
        for j in range(4):
            zz = 4 * q + j
            up = only(has_above, either(even_y, ya[zz], yb[zz]))
            down = only(has_below, either(even_y, yb[zz], ya[zz]))
            corner_r = only(has_right, either(even_x, ca[zz], cb[zz]))
            corner_l = only(has_left, either(even_x, cb[zz], ca[zz]))
            up_c = only(has_above, jnp.where(sub < 4, roll(corner_r, 4, 0), corner_l))
            down_c = only(has_below, jnp.where(sub < 4, corner_r, roll(corner_l, 4, 0)))
            for h in range(2):
                z, e = zz + 32 * h, 64 + q + 8 * h
                main_r = only(has_right, either(even_x, xa[z], xb[z]))
                main_l = only(has_left, either(even_x, xb[z], xa[z]))
                extra_r = only(has_right, either(even_x, xa[e], xb[e]))
                extra_l = only(has_left, either(even_x, xb[e], xa[e]))
                beside = (
                    jnp.where(sub < 3, main_r, only(sub >= 5, roll(main_l, 5, 0))),
                    jnp.where(sub < 3, roll(main_r, -3, 0), only(sub >= 5, roll(main_l, 2, 0))),
                    jnp.where(
                        sub < 2,
                        roll(main_r, 2, 0),
                        jnp.where(
                            sub < 4,
                            roll(extra_r, 2 - 2 * j, 0),
                            jnp.where(sub < 6, roll(main_l, 6, 0), roll(extra_l, 6 - 2 * j, 0)),
                        ),
                    ),
                )
                for n, (own, full) in enumerate(((f, fx), (a, ax), (b, bx))):
                    at = 64 * h + YH * n
                    full[z, 0:8, 0:128] = own[z]
                    full[z, 8:16, 0:128] = beside[n]
                    for rows, hi, lo in (((0, 8), up, down), ((8, 16), up_c, down_c)):
                        full[z, rows[0] : rows[1], 128:256] = jnp.where(
                            lane < YH, roll(hi, -at, 1), only(lane >= 128 - YH, roll(lo, 128 - YH - at, 1))
                        )
        return carry

    lax.fori_loop(0, 8, unpack, 0)
    level = Level((fx, ax, bx, ws, wl, wm, inv, diag, u, v), 1.0, True, 4)
    level.build()
    copies = [
        pltpu.make_async_copy(src, dst, sems.at[n])
        for n, (src, dst) in enumerate(
            ((fx, f_out), (ws, ws_out), (wl, wl_out), (wm, wm_out), (inv, inv_out), (diag, diag_out))
        )
    ]
    for copy in copies:
        copy.start()

    half = indicator(iota((256, 128), 0) // 2 == iota((256, 128), 1))

    def coarse():
        wide[...] = matmul(pairs[...].reshape(256, 256), half)
        return 0.125 * (wide[pl.ds(0, 128, stride=2), :] + wide[pl.ds(1, 128, stride=2), :])

    sum_planes(ax, pairs, 8)
    alpha = coarse()
    sum_planes(bx, pairs, 8)
    beta = coarse()
    level.sweeps_down()
    level.residual_pairs(u, pairs, 8)
    source = coarse()

    at = iota((128, 128), 1)
    pack[0:16] = jnp.where(at < 64, source, roll(alpha, 64, 1)).reshape(16, 8, 128)
    second = jnp.zeros((128, 128), F32)
    for end, part in (
        (112, roll(beta, -16, 1)),
        (104, roll(beta, 32, 1)),
        (96, roll(alpha, -32, 1)),
        (88, roll(alpha, 16, 1)),
        (80, roll(source, -48, 1)),
        (72, source),
        (64, beta),
    ):
        second = jnp.where(at < end, part, second)
    pack[16:32] = second.reshape(16, 8, 128)

    for z in range(32):
        own_u[z] = u[z, 0:8, :]
        own_u[z + 32] = u[z + 32, 0:8, :]
        one, two = u[z, 0:8, 0:128], u[z + 32, 0:8, 0:128]
        low = jnp.where(sub < 4, one, roll(two, 4, 0))
        high = jnp.where(sub < 4, roll(one, 4, 0), two)
        ra[z] = either(even_x, high, low)
        rb[z] = either(even_x, low, high)
    for t in range(2):
        low = high = jnp.zeros((8, 128), F32)
        for g in range(2):
            for k in range(16):
                edge = u[16 * (2 * t + g) + k, 0:8, 128:256]
                edge = roll(jnp.where(lane < 4, edge, roll(edge, 8, 1)), 8 * k, 1)
                here = (lane // 8 == k) & (sub // 4 == g)
                turned = roll(edge, 4, 0)
                low = jnp.where(here, turned if g else edge, low)
                high = jnp.where(here, edge if g else turned, high)
        ra[32 + t] = either(even_x, high, low)
        rb[32 + t] = either(even_x, low, high)
    for copy in copies:
        copy.wait()


def middle_down_kernel(
    pack, ga, gb, ra, rb,
    copies, sa, sb, f1, a1, b1, u1,
    b, ws, wl, wm, inv, diag, u, v, pairs, wide,
):
    ix, iy, even_x, even_y, has_right, has_left, has_above, has_below = places()
    lane, sub = iota((8, 128), 1), iota((8, 128), 0)

    def fields(one, two):
        def halo(right, left):
            return jnp.where(lane < 72, roll(two, right, 1), only(lane >= 120, roll(two, left, 1)))

        return (
            jnp.where(lane < 64, one, halo(0, 48)),
            jnp.where(lane < 64, roll(one, 64, 1), halo(-16, 32)),
            jnp.where(lane < 64, two, halo(-32, 16)),
        )

    def unpack(t, carry):
        own = fields(pack[t], pack[16 + t])
        right = fields(
            only(has_right, either(even_x, ga[t], gb[t])), only(has_right, either(even_x, ga[16 + t], gb[16 + t]))
        )
        left = fields(
            only(has_left, either(even_x, gb[t], ga[t])), only(has_left, either(even_x, gb[16 + t], ga[16 + t]))
        )
        for n, full in enumerate((f1, a1, b)):
            full[2 * t, 0:8] = jnp.where(sub < 4, own[n], roll(right[n], 4, 0))
            full[2 * t, 8:16] = only(sub >= 4, roll(left[n], 4, 0))
            full[2 * t + 1, 0:8] = jnp.where(sub < 4, roll(own[n], 4, 0), right[n])
            full[2 * t + 1, 8:16] = only(sub >= 4, left[n])
        return carry

    lax.fori_loop(0, 16, unpack, 0)
    level = Level((f1, a1, b, ws, wl, wm, inv, diag, u, v), 0.25, True, 4)
    level.build()
    level.sweeps_down()

    lanes_in, lanes_out = iota((128, 128), 0), iota((128, 128), 1)
    half = indicator((lanes_in // 2 == lanes_out) & (lanes_out < 32))

    def coarse():
        wide[...] = matmul(pairs[...].reshape(128, 128), half)
        rows = [wide[pl.ds(k, 16, stride=8), :] for k in range(4)]
        return 0.125 * (rows[0] + rows[1]), 0.125 * (rows[2] + rows[3])

    sum_planes(a1, pairs, 8)
    alpha = coarse()
    sum_planes(b, pairs, 8)
    beta = coarse()
    level.residual_pairs(u, pairs, 8)
    source = coarse()
    for k in range(2):
        block = source[k] + roll(alpha[k], 32, 1) + roll(beta[k], 64, 1)
        for d in range(8):
            copies[2 * d + k] = block

    def edges(z, carry):
        b1[z] = b[z]
        u1[z] = u[z]
        mine, far = u[z, 0:8], u[z, 8:16]
        turned = roll(mine, 4, 0)
        high = jnp.where(
            sub >= 4, turned, jnp.where(sub == 3, roll(far, 4, 0), roll(b[z, 8:16], 1, 0))
        )
        low = jnp.where(sub == 1, roll(b[z, 0:8], 5, 0), turned)
        sa[z] = either(even_x, high, low)
        sb[z] = either(even_x, low, high)
        return carry

    lax.fori_loop(0, 32, edges, 0, unroll=2)
    sa[32:66] = ra[...]
    sb[32:66] = rb[...]


def up_kernel(
    own, ya, yb, xa, xb, f1, a1, b1, u1, own_u,
    f0_in, ws0_in, wl0_in, wm0_in, inv0_in, diag0_in,
    field_out, residual_out,
    f0, ws0, wl0, wm0, inv0, diag0, u0, v0,
    bx1, ws1, wl1, wm1, inv1, diag1, ux1, v1,
    f2, a2, b2, ws2, wl2, wm2, inv2, diag2, u2, v2,
    f3, a3, b3, ws3, wl3, wm3, inv3, diag3, u3, v3,
    pairs, wide, spread, sems,
):
    ix, iy, even_x, even_y, has_right, has_left, has_above, has_below = places()
    lane, sub = iota((8, 128), 1), iota((8, 128), 0)
    copies = [
        pltpu.make_async_copy(src, dst, sems.at[n])
        for n, (src, dst) in enumerate(
            ((f0_in, f0), (ws0_in, ws0), (wl0_in, wl0), (wm0_in, wm0), (inv0_in, inv0), (diag0_in, diag0))
        )
    ]
    for copy in copies:
        copy.start()

    at = iota((16, 128), 1)
    for x in range(16):
        mine = own[x]
        up = only(has_above, either(even_y, ya[x], yb[x]))
        down = only(has_below, either(even_y, yb[x], ya[x]))
        for n, full in enumerate((f2, a2, b2)):
            full[x] = jnp.where(
                at < 32,
                roll(mine, -32 * n, 1),
                jnp.where(at < 64, roll(up, 32 - 32 * n, 1), only(at >= 96, roll(down, 96 - 32 * n, 1))),
            )
    level2 = Level((f2, a2, b2, ws2, wl2, wm2, inv2, diag2, u2, v2), 0.0625, False, 4)
    level2.build()
    level2.sweeps_down()

    lanes_in, lanes_out = iota((128, 128), 0), iota((128, 128), 1)
    half = indicator(half_wrapped(lanes_in, 96, 64) == lanes_out)
    twice = indicator(lanes_in == half_wrapped(lanes_out, 96, 64))

    def coarse():
        wide[0:128, :] = matmul(pairs[...].reshape(128, 128), half)
        halves = wide[pl.ds(0, 64, stride=2), :] + wide[pl.ds(1, 64, stride=2), :]
        return (0.125 * halves).reshape(8, 8, 128)

    sum_planes(a2, pairs, 16)
    a3[...] = coarse()
    sum_planes(b2, pairs, 16)
    b3[0:8] = coarse()
    level2.residual_pairs(u2, pairs, 16)
    f3[...] = coarse()
    level3 = Level((f3, a3, b3, ws3, wl3, wm3, inv3, diag3, u3, v3), 0.015625, False, 8)
    level3.build()
    level3.start(BOTTOM_WEIGHT)

    def two_sweeps(_, carry):
        level3.sweep(BOTTOM_WEIGHT, u3, v3)
        level3.sweep(BOTTOM_WEIGHT, v3, u3)
        return carry

    lax.fori_loop(0, (BOTTOM - 2) // 2, two_sweeps, 0)
    level3.sweep(BOTTOM_WEIGHT, u3, v3)

    fine = matmul(v3[0:8].reshape(64, 128), twice)
    wide[pl.ds(0, 64, stride=2), :] = fine
    wide[pl.ds(1, 64, stride=2), :] = fine
    for x in range(16):
        u2[x] = u2[x] + only(inv2[x] > 0.0, wide[16 * (x // 2) : 16 * (x // 2) + 16, :])
    level2.sweeps_up()

    def fill_1(z, carry):
        right = only(has_right, either(even_x, xa[z], xb[z]))
        left = only(has_left, either(even_x, xb[z], xa[z]))
        ux1[z, 0:8] = jnp.where(sub < 4, u1[z, 0:8], right)
        ux1[z, 8:16] = jnp.where(sub == 0, right, only(sub >= 3, left))
        bx1[z, 0:8] = b1[z, 0:8]
        bx1[z, 8:16] = jnp.where(
            sub == 0, roll(right, -1, 0), jnp.where(sub == 3, roll(left, 3, 0), b1[z, 8:16])
        )
        return carry

    lax.fori_loop(0, 32, fill_1, 0, unroll=2)
    level1 = Level((f1, a1, bx1, ws1, wl1, wm1, inv1, diag1, ux1, v1), 0.25, True, 4)
    level1.build()
    double = indicator(lanes_in == jnp.where(lanes_out < 96, lanes_out // 2, 64 + lanes_out // 2))
    for k in range(-3, 5):
        column = jnp.clip(2 * ix + k, 0, 15)
        fine = matmul(v2[column], double)
        for e in range(2):
            for x in range(2):
                spread[pl.ds(e * 16 + (2 * k + x) % 16, 16, stride=32), :] = fine

    def correct_1(z, carry):
        rows = spread[pl.ds(pl.multiple_of(16 * z, 16), 16), :]
        ux1[z] = ux1[z] + only(inv1[z] > 0.0, rows)
        return carry

    lax.fori_loop(0, 32, correct_1, 0, unroll=2)
    level1.sweeps_up()

    for z in range(32):
        parts = v1[z, 0:8], v1[z, 8:16]
        rows = jnp.where(sub < 6, parts[0], parts[1])
        spread[pl.ds(16 * z, 8, stride=2), :] = rows
        spread[pl.ds(16 * z + 1, 8, stride=2), :] = rows
    for copy in copies:
        copy.wait()
    for z in range(64):
        t, e = z % 32, z // 32
        right = only(has_right, either(even_x, xa[32 + t], xb[32 + t]))
        left = only(has_left, either(even_x, xb[32 + t], xa[32 + t]))
        u0[z, 0:8, :] = own_u[z]
        u0[z, 8:16, 0:128] = jnp.where(
            sub < 4, roll(right, 4, 0) if e else right, left if e else roll(left, 4, 0)
        )
        g, k = z // 16, z % 16
        t, e = 64 + g // 2, g % 2
        right = only(has_right, either(even_x, xa[t], xb[t]))
        left = only(has_left, either(even_x, xb[t], xa[t]))
        edge = jnp.where(sub < 4, roll(right, 4, 0) if e else right, left if e else roll(left, 4, 0))
        u0[z, 8:16, 128:256] = jnp.where(
            lane < 4, roll(edge, -8 * k, 1), only(lane >= 124, roll(edge, 120 - 8 * k, 1))
        )
    lanes_in, lanes_out = iota((128, 256), 0), iota((128, 256), 1)
    double = indicator(lanes_in == lanes_out // 2)

    def correct_0(z, carry):
        fine = matmul(spread[pl.ds(pl.multiple_of(64 * z, 64), 64), :], double)
        for k in range(4):
            rows = fine[16 * k : 16 * k + 16]
            for e in range(2):
                m = 8 * z + 2 * k + e
                u0[m] = u0[m] + only(inv0[m] > 0.0, rows)
        return carry

    lax.fori_loop(0, 8, correct_0, 0)
    level0 = Level((f0, None, u0, ws0, wl0, wm0, inv0, diag0, u0, v0), 1.0, True, 4)
    u0[64] = jnp.zeros((16, 256), F32)
    v0[64] = jnp.zeros((16, 256), F32)
    level0.sweeps_up()
    level0.residual(v0, residual_out, 8, 128)

    def out(z, carry):
        field_out[z] = v0[z, 0:8, 0:128]
        return carry

    lax.fori_loop(0, 64, out, 0, unroll=4)


def call(kernel, outs, scratch, any_in=0, any_out=0, n_in=0, sems=0):
    vmem = pl.BlockSpec(memory_space=pltpu.VMEM)
    anywhere = pl.BlockSpec(memory_space=pl.ANY)
    out_specs = [vmem] * (len(outs) - any_out) + [anywhere] * any_out
    scratch_shapes = [pltpu.VMEM(shape, F32) for shape in scratch]
    if sems:
        scratch_shapes.append(pltpu.SemaphoreType.DMA((sems,)))
    return pl.pallas_call(
        kernel,
        out_shape=[jax.ShapeDtypeStruct(shape, F32) for shape in outs],
        in_specs=[vmem] * (n_in - any_in) + [anywhere] * any_in,
        out_specs=out_specs,
        scratch_shapes=scratch_shapes,
        compiler_params=pltpu.CompilerParams(vmem_limit_bytes=48 * 1024 * 1024),
    )


def swaps(axis):
    size = lax.axis_size(axis)
    first = [(i, i ^ 1) for i in range(size)]
    second = [(i, i + 1 if i % 2 else i - 1) for i in range(size)]
    if axis == "gx":
        second = [(i, j % size) for i, j in second]
    else:
        second = [(i, j) for i, j in second if 0 <= j < size]
    return first, second


def swap(a, b, axis):
    first, second = swaps(axis)
    return lax.ppermute(a, axis, first), lax.ppermute(b, axis, second)


def body(right_side, alpha, beta):
    tiles = lambda n: (n, 8, 128)
    ya, yb, xa, xb = call(pack_kernel, [tiles(32), tiles(32), tiles(80), tiles(80)], [], n_in=3)(
        right_side, alpha, beta
    )
    ya, yb = swap(ya, yb, "gy")
    xa, xb = swap(xa, xb, "gx")
    ca, cb = call(corner_kernel, [tiles(32), tiles(32)], [], n_in=2)(ya, yb)
    ca, cb = swap(ca, cb, "gx")

    full, more = (64, 16, 256), (65, 16, 256)
    pack, ra, rb, own_u, *fine = call(
        fine_down_kernel,
        [tiles(32), tiles(34), tiles(34), (64, 8, 256)] + [full] * 6,
        [full, full, more, full, full, full, full, full, more, more, (32, 8, 256), (256, 128)],
        n_in=9,
        any_out=6,
        sems=6,
    )(right_side, alpha, beta, xa, xb, ya, yb, ca, cb)
    ga, gb = swap(pack, pack, "gx")

    full, more = (32, 16, 128), (33, 16, 128)
    copies, sa, sb, f1, a1, b1, u1 = call(
        middle_down_kernel,
        [(16, 16, 128), tiles(66), tiles(66)] + [full] * 4,
        [more, full, full, full, full, full, more, more, tiles(16), (128, 128)],
        n_in=5,
    )(pack, ga, gb, ra, rb)
    own = lax.all_to_all(copies, "gx", 0, 0, tiled=True)
    ya, yb = swap(own, own, "gy")
    xa, xb = swap(sa, sb, "gx")

    def level(planes, rows, lanes):
        one, two = (planes, rows, lanes), (planes + 1, rows, lanes)
        return [one, one, two, one, one, one, one, one, two, two]

    zero, first = level(64, 16, 256), level(32, 16, 128)
    return tuple(
        call(
            up_kernel,
            [tiles(64), tiles(64)],
            [zero[0]]
            + zero[3:]
            + first[2:]
            + level(16, 16, 128)
            + level(8, 8, 128)
            + [(8, 16, 128), (128, 128), (512, 128)],
            n_in=16,
            any_in=6,
            sems=6,
        )(own, ya, yb, xa, xb, f1, a1, b1, u1, own_u, *fine)
    )


def solution(mesh):
    return jax.shard_map(
        body,
        mesh=mesh,
        in_specs=(P(None, "gx", "gy"),) * 3,
        out_specs=(P(None, "gx", "gy"),) * 2,
        check_vma=False,
    )
```

time: 659 us -> 104 us (0.16)
  the two profiles are of different devices: /device:TPU:7 before, /device:TPU:24 now
where the time goes in v1:
time: 104 us
  Pallas kernels  40.8 us (39%)
  starting transfers between devices  28.4 us (27%)
  waiting for transfers between devices  21.2 us (20%)
  local copies, waits for them, and re-layouts  12.7 us (12%)
    ppermute x12, starting transfers between devices, swap(): return (lax.ppermute(a, axis, first), lax.ppermute(b, axis, second))  24.5 us
    pallas_call x1, Pallas kernels, body(): call(up_kernel, [tiles(64), tiles(64)], [zero[0]] + zero[3:] + first[2:]...  20.1 us
    ppermute x12, waiting for transfers between devices, swap(): return (lax.ppermute(a, axis, first), lax.ppermute(b, axis, second))  17.1 us
    unnamed x34, local copies, waits for them, and re-layouts  12.7 us
    pallas_call x1, Pallas kernels, body(): call(fine_down_kernel, [tiles(32), tiles(34), tiles(34), (64, 8, 256)] +...  11.6 us
    pallas_call x1, Pallas kernels, body(): call(middle_down_kernel, [(16, 16, 128), tiles(66), tiles(66)] + [full] *...  6.41 us
    all_to_all x1, waiting for transfers between devices, body(): own = lax.all_to_all(copies, 'gx', 0, 0, tiled=True)  4.07 us
    all_to_all x1, starting transfers between devices, body(): own = lax.all_to_all(copies, 'gx', 0, 0, tiled=True)  3.94 us
  transfers between devices with their start and end apart: 13, of which 7 were waited for; matrix products, arithmetic and copies ran while one was open for 0% of the time, Pallas kernels for 0%

profile of v1, /device:TPU:24, one launch (start us, length us, event | category | flops | bytes accessed | tf_op | source)
XLA Modules:
  0.0 103.9 jit_solution(2935570311140053897)
XLA Ops:
  2.5 0.9 copy-done.4
  3.5 2.6 %shard_map.50 = (f32[32,8,128]{2,1,0:T(8,128)S(1)}, f32[32,8,128]{2,1,0:T(8,128)S(1)}, f32[80,8,128]{2,1,0:T(8,128)S(1)}, f32[80,8,128]{2,1,0:T(8,128)S(1)}) custom-call(f32[64,8,128]{2,1,0:T(8,128)S(1)} %copy-done, f32[64,8,128]{2,1,0:T(8,128)S(1)} %copy-done.2, f32[64,8,128]{2,1,0:T(8,128)S(1)} %copy-done.4), custom_call_target="tpu_custom_call" | custom-call | tf_op jit(solution)/shard_map/pallas_call | solution.py:586
  6.1 2.0 %collective-permute-start = (f32[80,8,128]{2,1,0:T(8,128)S(1)}, f32[80,8,128]{2,1,0:T(8,128)S(1)}, u32[]{:S(2)}, u32[]{:S(2)}) collective-permute-start(f32[80,8,128]{2,1,0:T(8,128)S(1)} %get-tuple-element.25), channel_id=1, source_target_pairs={{0,32},{32,0},{64,96},{96,64},{128,160},{160,128},{192,224},{224,1... | collective-permute-start | bytes 983048 | tf_op jit(solution)/shard_map/ppermute | solution.py:581
  8.1 4.9 %collective-permute-start.1 = (f32[80,8,128]{2,1,0:T(8,128)S(1)}, f32[80,8,128]{2,1,0:T(8,128)S(1)}, u32[]{:S(2)}, u32[]{:S(2)}) collective-permute-start(f32[80,8,128]{2,1,0:T(8,128)S(1)} %get-tuple-element.26), channel_id=1, source_target_pairs={{0,224},{32,64},{64,32},{96,128},{128,96},{160,192},{192,160},{224... | collective-permute-start | bytes 983048 | tf_op jit(solution)/shard_map/ppermute | solution.py:581
  13.0 4.9 %collective-permute-start.3 = (f32[32,8,128]{2,1,0:T(8,128)S(1)}, f32[32,8,128]{2,1,0:T(8,128)S(1)}, u32[]{:S(2)}, u32[]{:S(2)}) collective-permute-start(f32[32,8,128]{2,1,0:T(8,128)S(1)} %get-tuple-element.28), channel_id=1, source_target_pairs={{1,2},{2,1},{3,4},{4,3},{5,6},{6,5},{7,8},{8,7},{9,10},{10,9},{11,... | collective-permute-start | bytes 393224 | tf_op jit(solution)/shard_map/ppermute | solution.py:581
  18.0 3.4 %collective-permute-done.3.yb = f32[32,8,128]{2,1,0:T(8,128)S(1)} collective-permute-done((f32[32,8,128]{2,1,0:T(8,128)S(1)}, f32[32,8,128]{2,1,0:T(8,128)S(1)}, u32[]{:S(2)}, u32[]{:S(2)}) %collective-permute-start.3) | collective-permute-done | bytes 131104 | tf_op jit(solution)/shard_map/ppermute | solution.py:581
  21.6 2.0 %collective-permute-start.5 = (f32[32,8,128]{2,1,0:T(8,128)S(1)}, f32[32,8,128]{2,1,0:T(8,128)S(1)}, u32[]{:S(2)}, u32[]{:S(2)}) collective-permute-start(f32[32,8,128]{2,1,0:T(8,128)S(1)} %get-tuple-element.30), channel_id=1, source_target_pairs={{0,224},{32,64},{64,32},{96,128},{128,96},{160,192},{192,160},{224... | collective-permute-start | bytes 393224 | tf_op jit(solution)/shard_map/ppermute | solution.py:581
  23.6 3.0 %collective-permute-done.4.ca = f32[32,8,128]{2,1,0:T(8,128)S(1)} collective-permute-done((f32[32,8,128]{2,1,0:T(8,128)S(1)}, f32[32,8,128]{2,1,0:T(8,128)S(1)}, u32[]{:S(2)}, u32[]{:S(2)}) %collective-permute-start.4) | collective-permute-done | bytes 131104 | tf_op jit(solution)/shard_map/ppermute | solution.py:581
  26.5 1.3 %collective-permute-done.5.cb = f32[32,8,128]{2,1,0:T(8,128)S(1)} collective-permute-done((f32[32,8,128]{2,1,0:T(8,128)S(1)}, f32[32,8,128]{2,1,0:T(8,128)S(1)}, u32[]{:S(2)}, u32[]{:S(2)}) %collective-permute-start.5) | collective-permute-done | bytes 131104 | tf_op jit(solution)/shard_map/ppermute | solution.py:581
  27.9 11.6 %shard_map.52 = (f32[32,8,128]{2,1,0:T(8,128)S(1)}, f32[34,8,128]{2,1,0:T(8,128)S(1)}, f32[34,8,128]{2,1,0:T(8,128)S(1)}, f32[64,8,256]{2,1,0:T(8,128)S(1)}, f32...) custom-call(f32[64,8,128]{2,1,0:T(8,128)S(1)} %copy-done.1, ...), custom_call_target="tpu_custom_call" | custom-call | tf_op jit(solution)/shard_map/pallas_call | solution.py:595
  40.3 1.9 %collective-permute-start.7 = (f32[32,8,128]{2,1,0:T(8,128)S(1)}, f32[32,8,128]{2,1,0:T(8,128)S(1)}, u32[]{:S(2)}, u32[]{:S(2)}) collective-permute-start(f32[32,8,128]{2,1,0:T(8,128)S(1)} %get-tuple-element.31.pack), channel_id=1, source_target_pairs={{0,224},{32,64},{64,32},{96,128},{128,96},{160,192},{192,160},{224... | collective-permute-start | bytes 393224 | tf_op jit(solution)/shard_map/ppermute | solution.py:581
  42.2 4.3 %collective-permute-done.7.gb = f32[32,8,128]{2,1,0:T(8,128)S(1)} collective-permute-done((f32[32,8,128]{2,1,0:T(8,128)S(1)}, f32[32,8,128]{2,1,0:T(8,128)S(1)}, u32[]{:S(2)}, u32[]{:S(2)}) %collective-permute-start.7) | collective-permute-done | bytes 131104 | tf_op jit(solution)/shard_map/ppermute | solution.py:581
  47.2 6.4 %shard_map.53 = (f32[16,16,128]{2,1,0:T(8,128)}, f32[66,8,128]{2,1,0:T(8,128)S(1)}, f32[66,8,128]{2,1,0:T(8,128)S(1)}, f32[32,16,128]{2,1,0:T(8,128)S(1)}, f32[3...) custom-call(f32[32,8,128]{2,1,0:T(8,128)S(1)} %get-tuple-element.31.pack, ...), custom_call_target="tpu_custom_call" | custom-call | tf_op jit(solution)/shard_map/pallas_call | solution.py:606
  57.8 3.9 %all-to-all-start = ((f32[16,16,128]{2,1,0:T(8,128)}), f32[16,16,128]{2,1,0:T(8,128)S(1)}, u32[]{:S(2)}, u32[]{:S(2)}) async-start(f32[16,16,128]{2,1,0:T(8,128)} %get-tuple-element.34), calls=%async_computation | async-start | bytes 262144 | tf_op jit(solution)/shard_map/all_to_all | solution.py:612
  61.8 2.0 %collective-permute-start.10 = (f32[66,8,128]{2,1,0:T(8,128)}, f32[66,8,128]{2,1,0:T(8,128)S(1)}, u32[]{:S(2)}, u32[]{:S(2)}) collective-permute-start(f32[66,8,128]{2,1,0:T(8,128)} %copy-done.16), channel_id=1, source_target_pairs={{0,32},{32,0},{64,96},{96,64},{128,160},{160,128},{192,224},{224,1... | collective-permute-start | bytes 811016 | tf_op jit(solution)/shard_map/ppermute | solution.py:581
  63.8 2.7 %collective-permute-start.11 = (f32[66,8,128]{2,1,0:T(8,128)}, f32[66,8,128]{2,1,0:T(8,128)}, u32[]{:S(2)}, u32[]{:S(2)}) collective-permute-start(f32[66,8,128]{2,1,0:T(8,128)} %copy-done.15), channel_id=1, source_target_pairs={{0,224},{32,64},{64,32},{96,128},{128,96},{160,192},{192,160},{224... | collective-permute-start | bytes 811016 | tf_op jit(solution)/shard_map/ppermute | solution.py:581
  66.5 4.1 %all-to-all-done.own = f32[16,16,128]{2,1,0:T(8,128)S(1)} async-done(((f32[16,16,128]{2,1,0:T(8,128)}), f32[16,16,128]{2,1,0:T(8,128)S(1)}, u32[]{:S(2)}, u32[]{:S(2)}) %all-to-all-start) | async-done | bytes 131104 | tf_op jit(solution)/shard_map/all_to_all | solution.py:612
  70.5 2.4 %collective-permute-start.9 = (f32[16,16,128]{2,1,0:T(8,128)S(1)}, f32[16,16,128]{2,1,0:T(8,128)S(1)}, u32[]{:S(2)}, u32[]{:S(2)}) collective-permute-start(f32[16,16,128]{2,1,0:T(8,128)S(1)} %all-to-all-done.own), channel_id=1, source_target_pairs={{1,2},{2,1},{3,4},{4,3},{5,6},{6,5},{7,8},{8,7},{9,10},{10,9},{11,... | collective-permute-start | bytes 393224 | tf_op jit(solution)/shard_map/ppermute | solution.py:581
  72.9 1.5 %collective-permute-start.8 = (f32[16,16,128]{2,1,0:T(8,128)S(1)}, f32[16,16,128]{2,1,0:T(8,128)S(1)}, u32[]{:S(2)}, u32[]{:S(2)}) collective-permute-start(f32[16,16,128]{2,1,0:T(8,128)S(1)} %all-to-all-done.own), channel_id=1, source_target_pairs={{0,1},{1,0},{2,3},{3,2},{4,5},{5,4},{6,7},{7,6},{8,9},{9,8},{10,11... | collective-permute-start | bytes 393224 | tf_op jit(solution)/shard_map/ppermute | solution.py:581
  74.4 4.5 %collective-permute-done.9.yb = f32[16,16,128]{2,1,0:T(8,128)S(1)} collective-permute-done((f32[16,16,128]{2,1,0:T(8,128)S(1)}, f32[16,16,128]{2,1,0:T(8,128)S(1)}, u32[]{:S(2)}, u32[]{:S(2)}) %collective-permute-start.9) | collective-permute-done | bytes 131104 | tf_op jit(solution)/shard_map/ppermute | solution.py:581
  78.9 1.0 %copy-done.6 = f32[64,8,256]{2,1,0:T(8,128)S(1)} copy-done((f32[64,8,256]{2,1,0:T(8,128)S(1)}, f32[64,8,256]{2,1,0:T(8,128)}, u32[]{:S(2)}) %copy-start.6) | copy-done | bytes 524312
  80.0 0.9 copy-done.8
  80.9 0.9 copy-done.10
  83.8 20.1 %shard_map.54 = (f32[64,8,128]{2,1,0:T(8,128)}, f32[64,8,128]{2,1,0:T(8,128)}) custom-call(f32[16,16,128]{2,1,0:T(8,128)S(1)} %all-to-all-done.own, f32[16,16,128]{2,1,0:T(8,128)S(1)} %collective-permute-done.8.ya, f32[16,16,128]{2,1,0:T(8,128)S(1)} %collective-permute-done.9.yb, f32[66,8,128]{2,1,0:T(8,128)S(1)} %collective-permute-done.10.xa, ...), custom_call_target="tpu_custom_call" | custom-call | tf_op jit(solution)/shard_map/pallas_call | solution.py:622
  (41 shorter events, 9.7 us)
Async XLA Ops:
  0.6 1.0 copy-start
  1.6 0.9 copy-start.2
  2.5 0.9 copy-start.4
  3.5 24.4 %copy-start.3 = (f32[64,8,128]{2,1,0:T(8,128)S(1)}, f32[64,8,128]{2,1,0:T(8,128)}, u32[]{:S(2)}) copy-start(f32[64,8,128]{2,1,0:T(8,128)} %a.3) | copy-start | bytes 786436
  6.1 21.8 %copy-start.1 = (f32[64,8,128]{2,1,0:T(8,128)S(1)}, f32[64,8,128]{2,1,0:T(8,128)}, u32[]{:S(2)}) copy-start(f32[64,8,128]{2,1,0:T(8,128)} %f.3) | copy-start | bytes 786436
  6.1 21.8 %collective-permute-start = (f32[80,8,128]{2,1,0:T(8,128)S(1)}, f32[80,8,128]{2,1,0:T(8,128)S(1)}, u32[]{:S(2)}, u32[]{:S(2)}) collective-permute-start(f32[80,8,128]{2,1,0:T(8,128)S(1)} %get-tuple-element.25), channel_id=1, source_target_pairs={{0,32},{32,0},{64,96},{96,64},{128,160},{160,128},{192,224},{224,1... | collective-permute-start | bytes 983048 | tf_op jit(solution)/shard_map/ppermute | solution.py:581
  8.1 19.8 %collective-permute-start.1 = (f32[80,8,128]{2,1,0:T(8,128)S(1)}, f32[80,8,128]{2,1,0:T(8,128)S(1)}, u32[]{:S(2)}, u32[]{:S(2)}) collective-permute-start(f32[80,8,128]{2,1,0:T(8,128)S(1)} %get-tuple-element.26), channel_id=1, source_target_pairs={{0,224},{32,64},{64,32},{96,128},{128,96},{160,192},{192,160},{224... | collective-permute-start | bytes 983048 | tf_op jit(solution)/shard_map/ppermute | solution.py:581
  13.0 5.0 %collective-permute-start.2 = (f32[32,8,128]{2,1,0:T(8,128)S(1)}, f32[32,8,128]{2,1,0:T(8,128)S(1)}, u32[]{:S(2)}, u32[]{:S(2)}) collective-permute-start(f32[32,8,128]{2,1,0:T(8,128)S(1)} %get-tuple-element.27), channel_id=1, source_target_pairs={{0,1},{1,0},{2,3},{3,2},{4,5},{5,4},{6,7},{7,6},{8,9},{9,8},{10,11... | collective-permute-start | bytes 393224 | tf_op jit(solution)/shard_map/ppermute | solution.py:581
  13.0 8.4 %collective-permute-start.3 = (f32[32,8,128]{2,1,0:T(8,128)S(1)}, f32[32,8,128]{2,1,0:T(8,128)S(1)}, u32[]{:S(2)}, u32[]{:S(2)}) collective-permute-start(f32[32,8,128]{2,1,0:T(8,128)S(1)} %get-tuple-element.28), channel_id=1, source_target_pairs={{1,2},{2,1},{3,4},{4,3},{5,6},{6,5},{7,8},{8,7},{9,10},{10,9},{11,... | collective-permute-start | bytes 393224 | tf_op jit(solution)/shard_map/ppermute | solution.py:581
  21.5 5.1 %collective-permute-start.4 = (f32[32,8,128]{2,1,0:T(8,128)S(1)}, f32[32,8,128]{2,1,0:T(8,128)S(1)}, u32[]{:S(2)}, u32[]{:S(2)}) collective-permute-start(f32[32,8,128]{2,1,0:T(8,128)S(1)} %get-tuple-element.29), channel_id=1, source_target_pairs={{0,32},{32,0},{64,96},{96,64},{128,160},{160,128},{192,224},{224,1... | collective-permute-start | bytes 393224 | tf_op jit(solution)/shard_map/ppermute | solution.py:581
  21.6 6.3 %collective-permute-start.5 = (f32[32,8,128]{2,1,0:T(8,128)S(1)}, f32[32,8,128]{2,1,0:T(8,128)S(1)}, u32[]{:S(2)}, u32[]{:S(2)}) collective-permute-start(f32[32,8,128]{2,1,0:T(8,128)S(1)} %get-tuple-element.30), channel_id=1, source_target_pairs={{0,224},{32,64},{64,32},{96,128},{128,96},{160,192},{192,160},{224... | collective-permute-start | bytes 393224 | tf_op jit(solution)/shard_map/ppermute | solution.py:581
  39.5 0.8 copy-start.5
  40.3 6.2 %collective-permute-start.7 = (f32[32,8,128]{2,1,0:T(8,128)S(1)}, f32[32,8,128]{2,1,0:T(8,128)S(1)}, u32[]{:S(2)}, u32[]{:S(2)}) collective-permute-start(f32[32,8,128]{2,1,0:T(8,128)S(1)} %get-tuple-element.31.pack), channel_id=1, source_target_pairs={{0,224},{32,64},{64,32},{96,128},{128,96},{160,192},{192,160},{224... | collective-permute-start | bytes 393224 | tf_op jit(solution)/shard_map/ppermute | solution.py:581
  42.2 5.0 %collective-permute-start.6 = (f32[32,8,128]{2,1,0:T(8,128)S(1)}, f32[32,8,128]{2,1,0:T(8,128)S(1)}, u32[]{:S(2)}, u32[]{:S(2)}) collective-permute-start(f32[32,8,128]{2,1,0:T(8,128)S(1)} %get-tuple-element.31.pack), channel_id=1, source_target_pairs={{0,32},{32,0},{64,96},{96,64},{128,160},{160,128},{192,224},{224,1... | collective-permute-start | bytes 393224 | tf_op jit(solution)/shard_map/ppermute | solution.py:581
  57.8 12.7 %all-to-all-start = ((f32[16,16,128]{2,1,0:T(8,128)}), f32[16,16,128]{2,1,0:T(8,128)S(1)}, u32[]{:S(2)}, u32[]{:S(2)}) async-start(f32[16,16,128]{2,1,0:T(8,128)} %get-tuple-element.34), calls=%async_computation | async-start | bytes 262144 | tf_op jit(solution)/shard_map/all_to_all | solution.py:612
  61.8 12.7 %collective-permute-start.10 = (f32[66,8,128]{2,1,0:T(8,128)}, f32[66,8,128]{2,1,0:T(8,128)S(1)}, u32[]{:S(2)}, u32[]{:S(2)}) collective-permute-start(f32[66,8,128]{2,1,0:T(8,128)} %copy-done.16), channel_id=1, source_target_pairs={{0,32},{32,0},{64,96},{96,64},{128,160},{160,128},{192,224},{224,1... | collective-permute-start | bytes 811016 | tf_op jit(solution)/shard_map/ppermute | solution.py:581
  63.8 10.7 %collective-permute-start.11 = (f32[66,8,128]{2,1,0:T(8,128)}, f32[66,8,128]{2,1,0:T(8,128)}, u32[]{:S(2)}, u32[]{:S(2)}) collective-permute-start(f32[66,8,128]{2,1,0:T(8,128)} %copy-done.15), channel_id=1, source_target_pairs={{0,224},{32,64},{64,32},{96,128},{128,96},{160,192},{192,160},{224... | collective-permute-start | bytes 811016 | tf_op jit(solution)/shard_map/ppermute | solution.py:581
  70.5 8.4 %collective-permute-start.9 = (f32[16,16,128]{2,1,0:T(8,128)S(1)}, f32[16,16,128]{2,1,0:T(8,128)S(1)}, u32[]{:S(2)}, u32[]{:S(2)}) collective-permute-start(f32[16,16,128]{2,1,0:T(8,128)S(1)} %all-to-all-done.own), channel_id=1, source_target_pairs={{1,2},{2,1},{3,4},{4,3},{5,6},{6,5},{7,8},{8,7},{9,10},{10,9},{11,... | collective-permute-start | bytes 393224 | tf_op jit(solution)/shard_map/ppermute | solution.py:581
  72.9 6.0 %collective-permute-start.8 = (f32[16,16,128]{2,1,0:T(8,128)S(1)}, f32[16,16,128]{2,1,0:T(8,128)S(1)}, u32[]{:S(2)}, u32[]{:S(2)}) collective-permute-start(f32[16,16,128]{2,1,0:T(8,128)S(1)} %all-to-all-done.own), channel_id=1, source_target_pairs={{0,1},{1,0},{2,3},{3,2},{4,5},{5,4},{6,7},{7,6},{8,9},{9,8},{10,11... | collective-permute-start | bytes 393224 | tf_op jit(solution)/shard_map/ppermute | solution.py:581
  78.9 1.0 %copy-start.6 = (f32[64,8,256]{2,1,0:T(8,128)S(1)}, f32[64,8,256]{2,1,0:T(8,128)}, u32[]{:S(2)}) copy-start(f32[64,8,256]{2,1,0:T(8,128)} %copy-done.5) | copy-start | bytes 1572868
  80.0 0.9 copy-start.8
  80.9 0.9 copy-start.10
  81.9 0.9 copy-start.12
  82.8 0.9 copy-start.14
  (6 other events, 4.2 us)

commit v2 on v1

--- a/solution.py
+++ b/solution.py
@@ -31,12 +31,18 @@
     return jnp.where(flag, a, 0.0)
 
 
-def matmul(a, b):
-    return jnp.dot(a, b, precision=lax.Precision.HIGHEST, preferred_element_type=F32)
+def matmul(a, chooser):
+    total = None
+    for _ in range(3):
+        part = a.astype(jnp.bfloat16)
+        product = jnp.dot(part, chooser, preferred_element_type=F32)
+        total = product if total is None else total + product
+        a = a - part.astype(F32)
+    return total
 
 
 def indicator(mask):
-    return jnp.where(mask, 1.0, 0.0).astype(F32)
+    return jnp.where(mask, 1.0, 0.0).astype(jnp.bfloat16)
 
 
 def half_wrapped(i, low, high):
@@ -55,7 +61,6 @@
         shape = (self.rows, self.lanes)
         sub = iota(shape, 0)
         half = self.half
-        self.b[self.planes] = jnp.zeros(shape, F32)
         self.u[self.planes] = jnp.zeros(shape, F32)
         self.v[self.planes] = jnp.zeros(shape, F32)
 
@@ -150,7 +155,7 @@
         dst[m] = src[2 * m][:rows] + src[2 * m + 1][:rows]
         return carry
 
-    lax.fori_loop(0, dst.shape[0], step, 0, unroll=4)
+    lax.fori_loop(0, dst.shape[0], step, 0, unroll=8)
 
 
 def places():
@@ -159,25 +164,9 @@
     return ix, iy, ix % 2 == 0, iy % 2 == 0, ix < nx - 1, ix > 0, iy < ny - 1, iy > 0
 
 
-def pack_kernel(f, a, b, ya, yb, xa, xb):
+def pack_x_kernel(f, a, b, xa, xb):
     ix, iy, even_x, even_y, *_ = places()
-    lane, sub = iota((8, 128), 1), iota((8, 128), 0)
-
-    def y_side(z, shift):
-        return jnp.where(
-            lane < YH,
-            roll(f[z], shift, 1),
-            jnp.where(lane < 2 * YH, roll(a[z], shift + YH, 1), roll(b[z], shift + 2 * YH, 1)),
-        )
-
-    def y_step(z, carry):
-        low = jnp.where(lane < 64, y_side(z, 0), roll(y_side(z + 32, 0), 64, 1))
-        high = jnp.where(lane < 64, y_side(z, YH), roll(y_side(z + 32, YH), 64, 1))
-        ya[z] = either(even_y, high, low)
-        yb[z] = either(even_y, low, high)
-        return carry
-
-    lax.fori_loop(0, 32, y_step, 0, unroll=2)
+    sub = iota((8, 128), 0)
 
     def x_step(q, carry):
         extra_low = extra_high = jnp.zeros((8, 128), F32)
@@ -195,7 +184,35 @@
         xb[64 + q] = either(even_x, extra_low, extra_high)
         return carry
 
-    lax.fori_loop(0, 16, x_step, 0)
+    lax.fori_loop(0, 16, x_step, 0, unroll=4)
+
+
+def pack_y_kernel(f_in, a_in, b_in, f, a, b, ya, yb, sems):
+    ix, iy, even_x, even_y, *_ = places()
+    lane = iota((8, 128), 1)
+    copies = [
+        pltpu.make_async_copy(src, dst, sems.at[n]) for n, (src, dst) in enumerate(((f_in, f), (a_in, a), (b_in, b)))
+    ]
+    for copy in copies:
+        copy.start()
+    for copy in copies:
+        copy.wait()
+
+    def y_side(z, shift):
+        return jnp.where(
+            lane < YH,
+            roll(f[z], shift, 1),
+            jnp.where(lane < 2 * YH, roll(a[z], shift + YH, 1), roll(b[z], shift + 2 * YH, 1)),
+        )
+
+    def y_step(z, carry):
+        low = jnp.where(lane < 64, y_side(z, 0), roll(y_side(z + 32, 0), 64, 1))
+        high = jnp.where(lane < 64, y_side(z, YH), roll(y_side(z + 32, YH), 64, 1))
+        ya[z] = either(even_y, high, low)
+        yb[z] = either(even_y, low, high)
+        return carry
+
+    lax.fori_loop(0, 32, y_step, 0, unroll=8)
 
 
 def corner_kernel(ya, yb, ca, cb):
@@ -213,10 +230,50 @@
     lax.fori_loop(0, 32, step, 0, unroll=4)
 
 
+class Rows:
+    def __init__(self, top, bottom):
+        self.top, self.bottom = top, bottom
+        self.shape = (top.shape[0], 16, top.shape[2])
+
+    def __getitem__(self, m):
+        return jnp.concatenate([self.top[m], self.bottom[m]], 0)
+
+
+def spread_columns(lane, high, low, at):
+    return jnp.where(lane < YH, roll(high, -at, 1), only(lane >= 128 - YH, roll(low, 128 - YH - at, 1)))
+
+
+def coarse_fine(pairs, wide):
+    half = indicator(iota((256, 128), 0) // 2 == iota((256, 128), 1))
+    wide[...] = matmul(pairs[...].reshape(256, 256), half)
+    return 0.125 * (wide[pl.ds(0, 128, stride=2), :] + wide[pl.ds(1, 128, stride=2), :])
+
+
+def own_rows_kernel(f, a, b, ya, yb, fx, ax, bx, alpha, beta, pairs, wide):
+    ix, iy, even_x, even_y, has_right, has_left, has_above, has_below = places()
+    lane = iota((8, 128), 1)
+
+    def unpack(z, carry):
+        up = only(has_above, either(even_y, ya[z], yb[z]))
+        down = only(has_below, either(even_y, yb[z], ya[z]))
+        for n, (own, full) in enumerate(((f, fx), (a, ax), (b, bx))):
+            for h in range(2):
+                full[z + 32 * h, :, 0:128] = own[z + 32 * h]
+                full[z + 32 * h, :, 128:256] = spread_columns(lane, up, down, 64 * h + YH * n)
+        return carry
+
+    lax.fori_loop(0, 32, unpack, 0, unroll=8)
+    bx[64] = jnp.zeros((8, 256), F32)
+    sum_planes(ax, pairs, 8)
+    alpha[...] = coarse_fine(pairs, wide)
+    sum_planes(bx, pairs, 8)
+    beta[...] = coarse_fine(pairs, wide)
+
+
 def fine_down_kernel(
-    f, a, b, xa, xb, ya, yb, ca, cb,
-    pack, ra, rb, own_u, f_out, ws_out, wl_out, wm_out, inv_out, diag_out,
-    fx, ax, bx, ws, wl, wm, inv, diag, u, v, pairs, wide, sems,
+    f, a, b, alpha_in, beta_in, xa, xb, ca, cb,
+    pack, ra, rb, own_u, fx, ws, wl, wm, inv, diag,
+    ax, bx, u, v, pairs, wide,
 ):
     ix, iy, even_x, even_y, has_right, has_left, has_above, has_below = places()
     lane, sub = iota((8, 128), 1), iota((8, 128), 0)
@@ -224,12 +281,10 @@
     def unpack(q, carry):
         for j in range(4):
             zz = 4 * q + j
-            up = only(has_above, either(even_y, ya[zz], yb[zz]))
-            down = only(has_below, either(even_y, yb[zz], ya[zz]))
             corner_r = only(has_right, either(even_x, ca[zz], cb[zz]))
             corner_l = only(has_left, either(even_x, cb[zz], ca[zz]))
-            up_c = only(has_above, jnp.where(sub < 4, roll(corner_r, 4, 0), corner_l))
-            down_c = only(has_below, jnp.where(sub < 4, corner_r, roll(corner_l, 4, 0)))
+            up = only(has_above, jnp.where(sub < 4, roll(corner_r, 4, 0), corner_l))
+            down = only(has_below, jnp.where(sub < 4, corner_r, roll(corner_l, 4, 0)))
             for h in range(2):
                 z, e = zz + 32 * h, 64 + q + 8 * h
                 main_r = only(has_right, either(even_x, xa[z], xb[z]))
@@ -249,41 +304,19 @@
                         ),
                     ),
                 )
-                for n, (own, full) in enumerate(((f, fx), (a, ax), (b, bx))):
-                    at = 64 * h + YH * n
-                    full[z, 0:8, 0:128] = own[z]
-                    full[z, 8:16, 0:128] = beside[n]
-                    for rows, hi, lo in (((0, 8), up, down), ((8, 16), up_c, down_c)):
-                        full[z, rows[0] : rows[1], 128:256] = jnp.where(
-                            lane < YH, roll(hi, -at, 1), only(lane >= 128 - YH, roll(lo, 128 - YH - at, 1))
-                        )
-        return carry
-
-    lax.fori_loop(0, 8, unpack, 0)
-    level = Level((fx, ax, bx, ws, wl, wm, inv, diag, u, v), 1.0, True, 4)
+                for n, full in enumerate((fx, ax, bx)):
+                    full[z, :, 0:128] = beside[n]
+                    full[z, :, 128:256] = spread_columns(lane, up, down, 64 * h + YH * n)
+        return carry
+
+    lax.fori_loop(0, 8, unpack, 0, unroll=2)
+    bx[64] = jnp.zeros((8, 256), F32)
+    level = Level((Rows(f, fx), Rows(a, ax), Rows(b, bx), ws, wl, wm, inv, diag, u, v), 1.0, True, 16)
     level.build()
-    copies = [
-        pltpu.make_async_copy(src, dst, sems.at[n])
-        for n, (src, dst) in enumerate(
-            ((fx, f_out), (ws, ws_out), (wl, wl_out), (wm, wm_out), (inv, inv_out), (diag, diag_out))
-        )
-    ]
-    for copy in copies:
-        copy.start()
-
-    half = indicator(iota((256, 128), 0) // 2 == iota((256, 128), 1))
-
-    def coarse():
-        wide[...] = matmul(pairs[...].reshape(256, 256), half)
-        return 0.125 * (wide[pl.ds(0, 128, stride=2), :] + wide[pl.ds(1, 128, stride=2), :])
-
-    sum_planes(ax, pairs, 8)
-    alpha = coarse()
-    sum_planes(bx, pairs, 8)
-    beta = coarse()
     level.sweeps_down()
     level.residual_pairs(u, pairs, 8)
-    source = coarse()
+    source = coarse_fine(pairs, wide)
+    alpha, beta = alpha_in[...], beta_in[...]
 
     at = iota((128, 128), 1)
     pack[0:16] = jnp.where(at < 64, source, roll(alpha, 64, 1)).reshape(16, 8, 128)
@@ -320,14 +353,12 @@
                 high = jnp.where(here, edge if g else turned, high)
         ra[32 + t] = either(even_x, high, low)
         rb[32 + t] = either(even_x, low, high)
-    for copy in copies:
-        copy.wait()
 
 
 def middle_down_kernel(
-    pack, ga, gb, ra, rb,
-    copies, sa, sb, f1, a1, b1, u1,
-    b, ws, wl, wm, inv, diag, u, v, pairs, wide,
+    pack, ga, gb,
+    copies, f1, a1, b, u,
+    ws, wl, wm, inv, diag, v, pairs, wide,
 ):
     ix, iy, even_x, even_y, has_right, has_left, has_above, has_below = places()
     lane, sub = iota((8, 128), 1), iota((8, 128), 0)
@@ -357,8 +388,9 @@
             full[2 * t + 1, 8:16] = only(sub >= 4, left[n])
         return carry
 
-    lax.fori_loop(0, 16, unpack, 0)
-    level = Level((f1, a1, b, ws, wl, wm, inv, diag, u, v), 0.25, True, 4)
+    lax.fori_loop(0, 16, unpack, 0, unroll=4)
+    b[32] = jnp.zeros((16, 128), F32)
+    level = Level((f1, a1, b, ws, wl, wm, inv, diag, u, v), 0.25, True, 16)
     level.build()
     level.sweeps_down()
 
@@ -381,9 +413,12 @@
         for d in range(8):
             copies[2 * d + k] = block
 
+
+def edges_kernel(_, ra, rb, b, u, sa, sb):
+    ix, iy, even_x, even_y, *_ = places()
+    sub = iota((8, 128), 0)
+
     def edges(z, carry):
-        b1[z] = b[z]
-        u1[z] = u[z]
         mine, far = u[z, 0:8], u[z, 8:16]
         turned = roll(mine, 4, 0)
         high = jnp.where(
@@ -394,31 +429,20 @@
         sb[z] = either(even_x, low, high)
         return carry
 
-    lax.fori_loop(0, 32, edges, 0, unroll=2)
+    lax.fori_loop(0, 32, edges, 0, unroll=8)
     sa[32:66] = ra[...]
     sb[32:66] = rb[...]
 
 
-def up_kernel(
-    own, ya, yb, xa, xb, f1, a1, b1, u1, own_u,
-    f0_in, ws0_in, wl0_in, wm0_in, inv0_in, diag0_in,
-    field_out, residual_out,
-    f0, ws0, wl0, wm0, inv0, diag0, u0, v0,
-    bx1, ws1, wl1, wm1, inv1, diag1, ux1, v1,
+def bottom_kernel(
+    own, ya, yb,
+    out,
     f2, a2, b2, ws2, wl2, wm2, inv2, diag2, u2, v2,
     f3, a3, b3, ws3, wl3, wm3, inv3, diag3, u3, v3,
-    pairs, wide, spread, sems,
+    pairs, wide,
 ):
     ix, iy, even_x, even_y, has_right, has_left, has_above, has_below = places()
     lane, sub = iota((8, 128), 1), iota((8, 128), 0)
-    copies = [
-        pltpu.make_async_copy(src, dst, sems.at[n])
-        for n, (src, dst) in enumerate(
-            ((f0_in, f0), (ws0_in, ws0), (wl0_in, wl0), (wm0_in, wm0), (inv0_in, inv0), (diag0_in, diag0))
-        )
-    ]
-    for copy in copies:
-        copy.start()
 
     at = iota((16, 128), 1)
     for x in range(16):
@@ -431,7 +455,9 @@
                 roll(mine, -32 * n, 1),
                 jnp.where(at < 64, roll(up, 32 - 32 * n, 1), only(at >= 96, roll(down, 96 - 32 * n, 1))),
             )
-    level2 = Level((f2, a2, b2, ws2, wl2, wm2, inv2, diag2, u2, v2), 0.0625, False, 4)
+    b2[16] = jnp.zeros((16, 128), F32)
+    b3[8] = jnp.zeros((8, 128), F32)
+    level2 = Level((f2, a2, b2, ws2, wl2, wm2, inv2, diag2, u2, v2), 0.0625, False, 16)
     level2.build()
     level2.sweeps_down()
 
@@ -468,6 +494,40 @@
     for x in range(16):
         u2[x] = u2[x] + only(inv2[x] > 0.0, wide[16 * (x // 2) : 16 * (x // 2) + 16, :])
     level2.sweeps_up()
+    out[...] = v2[0:16]
+
+
+def ready_kernel(xa, xb, own_u, u0):
+    ix, iy, even_x, even_y, has_right, has_left, has_above, has_below = places()
+    lane, sub = iota((8, 128), 1), iota((8, 128), 0)
+
+    for z in range(64):
+        t, e = z % 32, z // 32
+        right = only(has_right, either(even_x, xa[32 + t], xb[32 + t]))
+        left = only(has_left, either(even_x, xb[32 + t], xa[32 + t]))
+        u0[z, 0:8, :] = own_u[z]
+        u0[z, 8:16, 0:128] = jnp.where(
+            sub < 4, roll(right, 4, 0) if e else right, left if e else roll(left, 4, 0)
+        )
+        g, k = z // 16, z % 16
+        t, e = 32 + g // 2, g % 2
+        right = only(has_right, either(even_x, xa[32 + t], xb[32 + t]))
+        left = only(has_left, either(even_x, xb[32 + t], xa[32 + t]))
+        edge = jnp.where(sub < 4, roll(right, 4, 0) if e else right, left if e else roll(left, 4, 0))
+        u0[z, 8:16, 128:256] = jnp.where(
+            lane < 4, roll(edge, -8 * k, 1), only(lane >= 124, roll(edge, 120 - 8 * k, 1))
+        )
+    u0[64] = jnp.zeros((16, 256), F32)
+
+
+def up_kernel(
+    v2, xa, xb, f1, a1, b1, u1, u0_in, f0, f0x, ws0, wl0, wm0, inv0, diag0,
+    field_out, residual_out,
+    u0, v0, bx1, ws1, wl1, wm1, inv1, diag1, ux1, v1, spread,
+):
+    ix, iy, even_x, even_y, has_right, has_left, has_above, has_below = places()
+    sub = iota((8, 128), 0)
+    lanes_in, lanes_out = iota((128, 128), 0), iota((128, 128), 1)
 
     def fill_1(z, carry):
         right = only(has_right, either(even_x, xa[z], xb[z]))
@@ -480,23 +540,24 @@
         )
         return carry
 
-    lax.fori_loop(0, 32, fill_1, 0, unroll=2)
-    level1 = Level((f1, a1, bx1, ws1, wl1, wm1, inv1, diag1, ux1, v1), 0.25, True, 4)
+    lax.fori_loop(0, 32, fill_1, 0, unroll=8)
+    bx1[32] = jnp.zeros((16, 128), F32)
+    level1 = Level((f1, a1, bx1, ws1, wl1, wm1, inv1, diag1, ux1, v1), 0.25, True, 16)
     level1.build()
     double = indicator(lanes_in == jnp.where(lanes_out < 96, lanes_out // 2, 64 + lanes_out // 2))
-    for k in range(-3, 5):
-        column = jnp.clip(2 * ix + k, 0, 15)
-        fine = matmul(v2[column], double)
+    columns = [v2[jnp.clip(2 * ix + k, 0, 15)] for k in range(-3, 5)]
+    fine = matmul(jnp.concatenate(columns, 0), double)
+    for k in range(8):
         for e in range(2):
             for x in range(2):
-                spread[pl.ds(e * 16 + (2 * k + x) % 16, 16, stride=32), :] = fine
+                spread[pl.ds(e * 16 + (2 * (k - 3) + x) % 16, 16, stride=32), :] = fine[16 * k : 16 * k + 16]
 
     def correct_1(z, carry):
         rows = spread[pl.ds(pl.multiple_of(16 * z, 16), 16), :]
         ux1[z] = ux1[z] + only(inv1[z] > 0.0, rows)
         return carry
 
-    lax.fori_loop(0, 32, correct_1, 0, unroll=2)
+    lax.fori_loop(0, 32, correct_1, 0, unroll=8)
     level1.sweeps_up()
 
     for z in range(32):
@@ -504,24 +565,6 @@
         rows = jnp.where(sub < 6, parts[0], parts[1])
         spread[pl.ds(16 * z, 8, stride=2), :] = rows
         spread[pl.ds(16 * z + 1, 8, stride=2), :] = rows
-    for copy in copies:
-        copy.wait()
-    for z in range(64):
-        t, e = z % 32, z // 32
-        right = only(has_right, either(even_x, xa[32 + t], xb[32 + t]))
-        left = only(has_left, either(even_x, xb[32 + t], xa[32 + t]))
-        u0[z, 0:8, :] = own_u[z]
-        u0[z, 8:16, 0:128] = jnp.where(
-            sub < 4, roll(right, 4, 0) if e else right, left if e else roll(left, 4, 0)
-        )
-        g, k = z // 16, z % 16
-        t, e = 64 + g // 2, g % 2
-        right = only(has_right, either(even_x, xa[t], xb[t]))
-        left = only(has_left, either(even_x, xb[t], xa[t]))
-        edge = jnp.where(sub < 4, roll(right, 4, 0) if e else right, left if e else roll(left, 4, 0))
-        u0[z, 8:16, 128:256] = jnp.where(
-            lane < 4, roll(edge, -8 * k, 1), only(lane >= 124, roll(edge, 120 - 8 * k, 1))
-        )
     lanes_in, lanes_out = iota((128, 256), 0), iota((128, 256), 1)
     double = indicator(lanes_in == lanes_out // 2)
 
@@ -531,11 +574,11 @@
             rows = fine[16 * k : 16 * k + 16]
             for e in range(2):
                 m = 8 * z + 2 * k + e
-                u0[m] = u0[m] + only(inv0[m] > 0.0, rows)
-        return carry
-
-    lax.fori_loop(0, 8, correct_0, 0)
-    level0 = Level((f0, None, u0, ws0, wl0, wm0, inv0, diag0, u0, v0), 1.0, True, 4)
+                u0[m] = u0_in[m] + only(inv0[m] > 0.0, rows)
+        return carry
+
+    lax.fori_loop(0, 8, correct_0, 0, unroll=4)
+    level0 = Level((Rows(f0, f0x), None, u0, ws0, wl0, wm0, inv0, diag0, u0, v0), 1.0, True, 16)
     u0[64] = jnp.zeros((16, 256), F32)
     v0[64] = jnp.zeros((16, 256), F32)
     level0.sweeps_up()
@@ -548,20 +591,21 @@
     lax.fori_loop(0, 64, out, 0, unroll=4)
 
 
-def call(kernel, outs, scratch, any_in=0, any_out=0, n_in=0, sems=0):
+def call(kernel, outs, scratch, n_in, any_in=0, sems=0, cost=1):
     vmem = pl.BlockSpec(memory_space=pltpu.VMEM)
-    anywhere = pl.BlockSpec(memory_space=pl.ANY)
-    out_specs = [vmem] * (len(outs) - any_out) + [anywhere] * any_out
+    anywhere = pl.BlockSpec(memory_space=pltpu.HBM)
     scratch_shapes = [pltpu.VMEM(shape, F32) for shape in scratch]
     if sems:
         scratch_shapes.append(pltpu.SemaphoreType.DMA((sems,)))
+    need = sum(4 * p * r * n for p, r, n in ((1,) * (3 - len(shape)) + shape for shape in scratch))
     return pl.pallas_call(
         kernel,
         out_shape=[jax.ShapeDtypeStruct(shape, F32) for shape in outs],
         in_specs=[vmem] * (n_in - any_in) + [anywhere] * any_in,
-        out_specs=out_specs,
+        out_specs=[vmem] * len(outs),
         scratch_shapes=scratch_shapes,
-        compiler_params=pltpu.CompilerParams(vmem_limit_bytes=48 * 1024 * 1024),
+        cost_estimate=pl.CostEstimate(flops=0, bytes_accessed=cost * 3_000_000, transcendentals=0),
+        compiler_params=pltpu.CompilerParams(vmem_limit_bytes=need + 4 * 1024 * 1024),
     )
 
 
@@ -582,56 +626,62 @@
 
 
 def body(right_side, alpha, beta):
-    tiles = lambda n: (n, 8, 128)
-    ya, yb, xa, xb = call(pack_kernel, [tiles(32), tiles(32), tiles(80), tiles(80)], [], n_in=3)(
+    def tiles(n):
+        return (n, 8, 128)
+
+    f, a, b, ya, yb = call(pack_y_kernel, [tiles(64)] * 3 + [tiles(32)] * 2, [], 3, any_in=3, sems=3)(
         right_side, alpha, beta
     )
     ya, yb = swap(ya, yb, "gy")
+    xa, xb = call(pack_x_kernel, [tiles(80), tiles(80)], [], 3, cost=50)(f, a, b)
     xa, xb = swap(xa, xb, "gx")
-    ca, cb = call(corner_kernel, [tiles(32), tiles(32)], [], n_in=2)(ya, yb)
+    ca, cb = call(corner_kernel, [tiles(32), tiles(32)], [], 2)(ya, yb)
     ca, cb = swap(ca, cb, "gx")
+    top, top_more = (64, 8, 256), (65, 8, 256)
+    f, a, b, alpha, beta = call(
+        own_rows_kernel, [top, top, top_more, (128, 128), (128, 128)], [(32, 8, 256), (256, 128)], 5, cost=50
+    )(f, a, b, ya, yb)
 
     full, more = (64, 16, 256), (65, 16, 256)
     pack, ra, rb, own_u, *fine = call(
         fine_down_kernel,
-        [tiles(32), tiles(34), tiles(34), (64, 8, 256)] + [full] * 6,
-        [full, full, more, full, full, full, full, full, more, more, (32, 8, 256), (256, 128)],
-        n_in=9,
-        any_out=6,
-        sems=6,
-    )(right_side, alpha, beta, xa, xb, ya, yb, ca, cb)
+        [tiles(32), tiles(34), tiles(34), top, top] + [full] * 5,
+        [top, top_more, more, more, (32, 8, 256), (256, 128)],
+        9,
+    )(f, a, b, alpha, beta, xa, xb, ca, cb)
     ga, gb = swap(pack, pack, "gx")
 
     full, more = (32, 16, 128), (33, 16, 128)
-    copies, sa, sb, f1, a1, b1, u1 = call(
+    copies, f1, a1, b1, u1 = call(
         middle_down_kernel,
-        [(16, 16, 128), tiles(66), tiles(66)] + [full] * 4,
-        [more, full, full, full, full, full, more, more, tiles(16), (128, 128)],
-        n_in=5,
-    )(pack, ga, gb, ra, rb)
+        [(16, 16, 128), full, full, more, more],
+        [full, full, full, full, full, more, tiles(16), (128, 128)],
+        3,
+    )(pack, ga, gb)
     own = lax.all_to_all(copies, "gx", 0, 0, tiled=True)
     ya, yb = swap(own, own, "gy")
-    xa, xb = swap(sa, sb, "gx")
+    sa, sb = call(edges_kernel, [tiles(66), tiles(66)], [], 5, cost=50)(own, ra, rb, b1, u1)
+    sa, sb = swap(sa, sb, "gx")
+    (u0,) = call(ready_kernel, [(65, 16, 256)], [], 3)(sa, sb, own_u)
 
     def level(planes, rows, lanes):
         one, two = (planes, rows, lanes), (planes + 1, rows, lanes)
         return [one, one, two, one, one, one, one, one, two, two]
 
-    zero, first = level(64, 16, 256), level(32, 16, 128)
+    (u2,) = call(
+        bottom_kernel,
+        [(16, 16, 128)],
+        level(16, 16, 128) + level(8, 8, 128) + [(8, 16, 128), (128, 128)],
+        3,
+        cost=50,
+    )(own, ya, yb)
     return tuple(
         call(
             up_kernel,
             [tiles(64), tiles(64)],
-            [zero[0]]
-            + zero[3:]
-            + first[2:]
-            + level(16, 16, 128)
-            + level(8, 8, 128)
-            + [(8, 16, 128), (128, 128), (512, 128)],
-            n_in=16,
-            any_in=6,
-            sems=6,
-        )(own, ya, yb, xa, xb, f1, a1, b1, u1, own_u, *fine)
+            [(65, 16, 256)] * 2 + level(32, 16, 128)[2:] + [(512, 128)],
+            15,
+        )(u2, sa, sb, f1, a1, b1, u1, u0, f, *fine)
     )
 
 

time: 104 us -> 73.7 us (0.71)
  Pallas kernels: 40.8 us -> 20 us
  blocking collectives: 0 us -> 13.6 us
  local copies, waits for them, and re-layouts: 12.7 us -> 2.84 us
  starting transfers between devices: 28.4 us -> 19.3 us
  waiting for transfers between devices: 21.2 us -> 17 us
    pallas_call x5 -> x10, Pallas kernels: 40.8 us -> 20 us  [the longest x1 6.97 us: body(): call(up_kernel, [tiles(64), tiles(64)], [(65, 16, 256)] * 2 + level(32, 1...]
    all_to_all x0 -> x1, blocking collectives: none -> 13.6 us  [body(): own = lax.all_to_all(copies, 'gx', 0, 0, tiled=True)]
    unnamed x34 -> x6, local copies, waits for them, and re-layouts: 12.7 us -> 2.84 us
    ppermute x12, starting transfers between devices: 24.5 us -> 19.3 us  [swap(): return (lax.ppermute(a, axis, first), lax.ppermute(b, axis, second))]
    all_to_all x1 -> x0, waiting for transfers between devices: 4.07 us -> none  [body(): own = lax.all_to_all(copies, 'gx', 0, 0, tiled=True)]
    all_to_all x1 -> x0, starting transfers between devices: 3.94 us -> none  [body(): own = lax.all_to_all(copies, 'gx', 0, 0, tiled=True)]
  transfers between devices with their start and end apart: 13 -> 12, of which waited for: 7 -> 6; matrix products, arithmetic and copies ran while one was open for 0% -> 0% of each run, Pallas kernels for 0% -> 5%
where the time goes in v2:
time: 73.7 us; the launch traced here: 73.5 us
  Pallas kernels  20 us (27%)
  starting transfers between devices  19.3 us (26%)
  waiting for transfers between devices  17 us (23%)
  blocking collectives  13.6 us (18%)
  local copies, waits for them, and re-layouts  2.84 us (4%)
  between operations  0.76 us (1%)
    ppermute x12, starting transfers between devices, swap(): return (lax.ppermute(a, axis, first), lax.ppermute(b, axis, second))  19.3 us
    ppermute x12, waiting for transfers between devices, swap(): return (lax.ppermute(a, axis, first), lax.ppermute(b, axis, second))  17 us
    all_to_all x1, blocking collectives, body(): own = lax.all_to_all(copies, 'gx', 0, 0, tiled=True)  13.6 us
    pallas_call x1, Pallas kernels, body(): call(up_kernel, [tiles(64), tiles(64)], [(65, 16, 256)] * 2 + level(32, 1...  6.97 us
    pallas_call x1, Pallas kernels, body(): call(fine_down_kernel, [tiles(32), tiles(34), tiles(34), top, top] + [ful...  5.39 us
    unnamed x6, local copies, waits for them, and re-layouts  2.84 us
    pallas_call x1, Pallas kernels, body(): call(middle_down_kernel, [(16, 16, 128), full, full, more, more], [full,...  2.44 us
    pallas_call x1, Pallas kernels, body(): call(bottom_kernel, [(16, 16, 128)], level(16, 16, 128) + level(8, 8, 128...  2.34 us
  transfers between devices with their start and end apart: 12, of which 6 were waited for; matrix products, arithmetic and copies ran while one was open for 0% of the time, Pallas kernels for 5%

profile of v2, /device:TPU:24, one launch (start us, length us, event | category | flops | bytes accessed | tf_op | source)
XLA Modules:
  0.0 73.5 jit_solution(18378125293699393561)
XLA Ops:
  0.6 0.9 %copy-done = f32[64,8,128]{2,1,0:T(8,128)S(1)} copy-done((f32[64,8,128]{2,1,0:T(8,128)S(1)}, f32[64,8,128]{2,1,0:T(8,128)}, u32[]{:S(2)}) %copy-start) | copy-done | bytes 262168
  1.6 0.9 %copy-done.1 = f32[64,8,128]{2,1,0:T(8,128)S(1)} copy-done((f32[64,8,128]{2,1,0:T(8,128)S(1)}, f32[64,8,128]{2,1,0:T(8,128)}, u32[]{:S(2)}) %copy-start.1) | copy-done | bytes 262168
  2.5 0.9 %copy-done.2 = f32[64,8,128]{2,1,0:T(8,128)S(1)} copy-done((f32[64,8,128]{2,1,0:T(8,128)S(1)}, f32[64,8,128]{2,1,0:T(8,128)}, u32[]{:S(2)}) %copy-start.2) | copy-done | bytes 262168
  3.5 0.9 %shard_map.50 = (f32[64,8,128]{2,1,0:T(8,128)S(1)}, f32[64,8,128]{2,1,0:T(8,128)S(1)}, f32[64,8,128]{2,1,0:T(8,128)S(1)}, f32[32,8,128]{2,1,0:T(8,128)S(1)}, f32[32,8,128]{2,1,0:T(8,128)S(1)}) custom-call(f32[64,8,128]{2,1,0:T(8,128)S(1)} %copy-done, f32[64,8,128]{2,1,0:T(8,128)S(1)} %copy-done.1, f32[64,8,128]{2,1,0:T(8,128)S(1)} %copy-done.2), custom_call_target="tpu_custom_call" | custom-call | bytes 3000000 | tf_op jit(solution)/shard_map/pallas_call | solution.py:632
  4.6 2.0 %collective-permute-start.2 = (f32[80,8,128]{2,1,0:T(8,128)S(1)}, f32[80,8,128]{2,1,0:T(8,128)S(1)}, u32[]{:S(2)}, u32[]{:S(2)}) collective-permute-start(f32[80,8,128]{2,1,0:T(8,128)S(1)} %get-tuple-element.43), channel_id=1, source_target_pairs={{0,32},{32,0},{64,96},{96,64},{128,160},{160,128},{192,224},{224,1... | collective-permute-start | bytes 983048 | tf_op jit(solution)/shard_map/ppermute | solution.py:625
  6.6 4.9 %collective-permute-start.3 = (f32[80,8,128]{2,1,0:T(8,128)S(1)}, f32[80,8,128]{2,1,0:T(8,128)S(1)}, u32[]{:S(2)}, u32[]{:S(2)}) collective-permute-start(f32[80,8,128]{2,1,0:T(8,128)S(1)} %get-tuple-element.44), channel_id=1, source_target_pairs={{0,224},{32,64},{64,32},{96,128},{128,96},{160,192},{192,160},{224... | collective-permute-start | bytes 983048 | tf_op jit(solution)/shard_map/ppermute | solution.py:625
  11.6 4.9 %collective-permute-start.1 = (f32[32,8,128]{2,1,0:T(8,128)S(1)}, f32[32,8,128]{2,1,0:T(8,128)S(1)}, u32[]{:S(2)}, u32[]{:S(2)}) collective-permute-start(f32[32,8,128]{2,1,0:T(8,128)S(1)} %get-tuple-element.37), channel_id=1, source_target_pairs={{1,2},{2,1},{3,4},{4,3},{5,6},{6,5},{7,8},{8,7},{9,10},{10,9},{11,... | collective-permute-start | bytes 393224 | tf_op jit(solution)/shard_map/ppermute | solution.py:625
  16.5 3.4 %collective-permute-done.1.yb = f32[32,8,128]{2,1,0:T(8,128)S(1)} collective-permute-done((f32[32,8,128]{2,1,0:T(8,128)S(1)}, f32[32,8,128]{2,1,0:T(8,128)S(1)}, u32[]{:S(2)}, u32[]{:S(2)}) %collective-permute-start.1) | collective-permute-done | bytes 131104 | tf_op jit(solution)/shard_map/ppermute | solution.py:625
  20.1 2.0 %collective-permute-start.5 = (f32[32,8,128]{2,1,0:T(8,128)S(1)}, f32[32,8,128]{2,1,0:T(8,128)S(1)}, u32[]{:S(2)}, u32[]{:S(2)}) collective-permute-start(f32[32,8,128]{2,1,0:T(8,128)S(1)} %get-tuple-element.46), channel_id=1, source_target_pairs={{0,224},{32,64},{64,32},{96,128},{128,96},{160,192},{192,160},{224... | collective-permute-start | bytes 393224 | tf_op jit(solution)/shard_map/ppermute | solution.py:625
  22.1 1.4 %shard_map.51 = (f32[64,8,256]{2,1,0:T(8,128)S(1)}, f32[64,8,256]{2,1,0:T(8,128)S(1)}, f32[65,8,256]{2,1,0:T(8,128)S(1)}, f32[128,128]{1,0:T(8,128)S(1)}, f32[128,128]{1,0:T(8,128)S(1)}) custom-call(f32[64,8,128]{2,1,0:T(8,128)S(1)} %get-tuple-element.33.f, f32[64,8,128]{2,1,0:T(8,128)S(1)} %get-tuple-element.34.a, f32[64,8,128]{2,1,0:T(8,128)S(1)} %get-tuple-element.35.b, ...), custom_call_target="tpu_custom_call" | custom-call | bytes 150000000 | tf_op jit(solution)/shard_map/pallas_call | solution.py:641
  23.5 1.6 %collective-permute-done.4.ca = f32[32,8,128]{2,1,0:T(8,128)S(1)} collective-permute-done((f32[32,8,128]{2,1,0:T(8,128)S(1)}, f32[32,8,128]{2,1,0:T(8,128)S(1)}, u32[]{:S(2)}, u32[]{:S(2)}) %collective-permute-start.4) | collective-permute-done | bytes 131104 | tf_op jit(solution)/shard_map/ppermute | solution.py:625
  25.1 1.3 %collective-permute-done.5.cb = f32[32,8,128]{2,1,0:T(8,128)S(1)} collective-permute-done((f32[32,8,128]{2,1,0:T(8,128)S(1)}, f32[32,8,128]{2,1,0:T(8,128)S(1)}, u32[]{:S(2)}, u32[]{:S(2)}) %collective-permute-start.5) | collective-permute-done | bytes 131104 | tf_op jit(solution)/shard_map/ppermute | solution.py:625
  26.4 5.4 %shard_map.54 = (f32[32,8,128]{2,1,0:T(8,128)S(1)}, f32[34,8,128]{2,1,0:T(8,128)S(1)}, f32[34,8,128]{2,1,0:T(8,128)S(1)}, f32[64,8,256]{2,1,0:T(8,128)S(1)}, f32...) custom-call(f32[64,8,256]{2,1,0:T(8,128)S(1)} %get-tuple-element.38., ...), custom_call_target="tpu_custom_call" | custom-call | bytes 3000000 | tf_op jit(solution)/shard_map/pallas_call | solution.py:646
  31.8 2.0 %collective-permute-start.7 = (f32[32,8,128]{2,1,0:T(8,128)S(1)}, f32[32,8,128]{2,1,0:T(8,128)S(1)}, u32[]{:S(2)}, u32[]{:S(2)}) collective-permute-start(f32[32,8,128]{2,1,0:T(8,128)S(1)} %get-tuple-element.47.pack), channel_id=1, source_target_pairs={{0,224},{32,64},{64,32},{96,128},{128,96},{160,192},{192,160},{224... | collective-permute-start | bytes 393224 | tf_op jit(solution)/shard_map/ppermute | solution.py:625
  33.8 4.3 %collective-permute-done.7.gb = f32[32,8,128]{2,1,0:T(8,128)S(1)} collective-permute-done((f32[32,8,128]{2,1,0:T(8,128)S(1)}, f32[32,8,128]{2,1,0:T(8,128)S(1)}, u32[]{:S(2)}, u32[]{:S(2)}) %collective-permute-start.7) | collective-permute-done | bytes 131104 | tf_op jit(solution)/shard_map/ppermute | solution.py:625
  38.1 0.7 collective-permute-done.6.ga
  38.8 2.4 %shard_map.55 = (f32[16,16,128]{2,1,0:T(8,128)S(1)}, f32[32,16,128]{2,1,0:T(8,128)S(1)}, f32[32,16,128]{2,1,0:T(8,128)S(1)}, f32[33,16,128]{2,1,0:T(8,128)S(1)}, f32[33,16,128]{2,1,0:T(8,128)S(1)}) custom-call(f32[32,8,128]{2,1,0:T(8,128)S(1)} %get-tuple-element.47.pack, f32[32,8,128]{2,1,0:T(8,128)S(1)} %collective-permute-done.6.ga, ...), custom_call_target="tpu_custom_call" | custom-call | bytes 3000000 | tf_op jit(solution)/shard_map/pallas_call | solution.py:655
  41.2 13.6 %all_to_all.5.own._ = f32[16,16,128]{2,1,0:T(8,128)S(1)} all-to-all(f32[16,16,128]{2,1,0:T(8,128)S(1)} %get-tuple-element.48), channel_id=1, replica_groups=mesh['gx'=8,'gy'=32] {'gx'}, dimensions={0} | all-to-all | bytes 262144 | tf_op jit(solution)/shard_map/all_to_all | solution.py:661
  54.9 0.6 collective-permute-start.10
  55.5 2.2 %collective-permute-start.9 = (f32[16,16,128]{2,1,0:T(8,128)S(1)}, f32[16,16,128]{2,1,0:T(8,128)S(1)}, u32[]{:S(2)}, u32[]{:S(2)}) collective-permute-start(f32[16,16,128]{2,1,0:T(8,128)S(1)} %all_to_all.5.own._), channel_id=1, source_target_pairs={{1,2},{2,1},{3,4},{4,3},{5,6},{6,5},{7,8},{8,7},{9,10},{10,9},{11,... | collective-permute-start | bytes 393224 | tf_op jit(solution)/shard_map/ppermute | solution.py:625
  57.8 0.4 collective-permute-start.8
  58.2 5.7 %collective-permute-done.9.yb = f32[16,16,128]{2,1,0:T(8,128)S(1)} collective-permute-done((f32[16,16,128]{2,1,0:T(8,128)S(1)}, f32[16,16,128]{2,1,0:T(8,128)S(1)}, u32[]{:S(2)}, u32[]{:S(2)}) %collective-permute-start.9) | collective-permute-done | bytes 131104 | tf_op jit(solution)/shard_map/ppermute | solution.py:625
  63.9 2.3 %shard_map.56.v2 = f32[16,16,128]{2,1,0:T(8,128)S(1)} custom-call(f32[16,16,128]{2,1,0:T(8,128)S(1)} %all_to_all.5.own._, f32[16,16,128]{2,1,0:T(8,128)S(1)} %collective-permute-done.8.ya, f32[16,16,128]{2,1,0:T(8,128)S(1)} %collective-permute-done.9.yb), custom_call_target="tpu_custom_call" | custom-call | bytes 150000000 | tf_op jit(solution)/shard_map/pallas_call | solution.py:671
  66.5 7.0 %shard_map.59 = (f32[64,8,128]{2,1,0:T(8,128)}, f32[64,8,128]{2,1,0:T(8,128)}) custom-call(f32[16,16,128]{2,1,0:T(8,128)S(1)} %shard_map.56.v2, f32[66,8,128]{2,1,0:T(8,128)S(1)} %collective-permute-done.10.xa, f32[66,8,128]{2,1,0:T(8,128)S(1)} %collective-permute-done.11.xb, f32[32,16,128]{2,1,0:T(8,128)S(1)} %get-tuple-element.55.f1, ...), custom_call_target="tpu_custom_call" | custom-call | bytes 3000000 | tf_op jit(solution)/shard_map/pallas_call | solution.py:679
  (17 shorter events, 0.7 us)
Async XLA Ops:
  0.6 1.0 %copy-start = (f32[64,8,128]{2,1,0:T(8,128)S(1)}, f32[64,8,128]{2,1,0:T(8,128)}, u32[]{:S(2)}) copy-start(f32[64,8,128]{2,1,0:T(8,128)} %f_in.1) | copy-start | bytes 786436
  1.6 0.9 %copy-start.1 = (f32[64,8,128]{2,1,0:T(8,128)S(1)}, f32[64,8,128]{2,1,0:T(8,128)}, u32[]{:S(2)}) copy-start(f32[64,8,128]{2,1,0:T(8,128)} %a_in.1) | copy-start | bytes 786436
  2.5 0.9 %copy-start.2 = (f32[64,8,128]{2,1,0:T(8,128)S(1)}, f32[64,8,128]{2,1,0:T(8,128)}, u32[]{:S(2)}) copy-start(f32[64,8,128]{2,1,0:T(8,128)} %b_in.1) | copy-start | bytes 786436
  4.6 21.8 %collective-permute-start.2 = (f32[80,8,128]{2,1,0:T(8,128)S(1)}, f32[80,8,128]{2,1,0:T(8,128)S(1)}, u32[]{:S(2)}, u32[]{:S(2)}) collective-permute-start(f32[80,8,128]{2,1,0:T(8,128)S(1)} %get-tuple-element.43), channel_id=1, source_target_pairs={{0,32},{32,0},{64,96},{96,64},{128,160},{160,128},{192,224},{224,1... | collective-permute-start | bytes 983048 | tf_op jit(solution)/shard_map/ppermute | solution.py:625
  6.6 19.8 %collective-permute-start.3 = (f32[80,8,128]{2,1,0:T(8,128)S(1)}, f32[80,8,128]{2,1,0:T(8,128)S(1)}, u32[]{:S(2)}, u32[]{:S(2)}) collective-permute-start(f32[80,8,128]{2,1,0:T(8,128)S(1)} %get-tuple-element.44), channel_id=1, source_target_pairs={{0,224},{32,64},{64,32},{96,128},{128,96},{160,192},{192,160},{224... | collective-permute-start | bytes 983048 | tf_op jit(solution)/shard_map/ppermute | solution.py:625
  11.6 5.0 %collective-permute-start = (f32[32,8,128]{2,1,0:T(8,128)S(1)}, f32[32,8,128]{2,1,0:T(8,128)S(1)}, u32[]{:S(2)}, u32[]{:S(2)}) collective-permute-start(f32[32,8,128]{2,1,0:T(8,128)S(1)} %get-tuple-element.36), channel_id=1, source_target_pairs={{0,1},{1,0},{2,3},{3,2},{4,5},{5,4},{6,7},{7,6},{8,9},{9,8},{10,11... | collective-permute-start | bytes 393224 | tf_op jit(solution)/shard_map/ppermute | solution.py:625
  11.6 8.4 %collective-permute-start.1 = (f32[32,8,128]{2,1,0:T(8,128)S(1)}, f32[32,8,128]{2,1,0:T(8,128)S(1)}, u32[]{:S(2)}, u32[]{:S(2)}) collective-permute-start(f32[32,8,128]{2,1,0:T(8,128)S(1)} %get-tuple-element.37), channel_id=1, source_target_pairs={{1,2},{2,1},{3,4},{4,3},{5,6},{6,5},{7,8},{8,7},{9,10},{10,9},{11,... | collective-permute-start | bytes 393224 | tf_op jit(solution)/shard_map/ppermute | solution.py:625
  20.0 5.1 %collective-permute-start.4 = (f32[32,8,128]{2,1,0:T(8,128)S(1)}, f32[32,8,128]{2,1,0:T(8,128)S(1)}, u32[]{:S(2)}, u32[]{:S(2)}) collective-permute-start(f32[32,8,128]{2,1,0:T(8,128)S(1)} %get-tuple-element.45), channel_id=1, source_target_pairs={{0,32},{32,0},{64,96},{96,64},{128,160},{160,128},{192,224},{224,1... | collective-permute-start | bytes 393224 | tf_op jit(solution)/shard_map/ppermute | solution.py:625
  20.1 6.3 %collective-permute-start.5 = (f32[32,8,128]{2,1,0:T(8,128)S(1)}, f32[32,8,128]{2,1,0:T(8,128)S(1)}, u32[]{:S(2)}, u32[]{:S(2)}) collective-permute-start(f32[32,8,128]{2,1,0:T(8,128)S(1)} %get-tuple-element.46), channel_id=1, source_target_pairs={{0,224},{32,64},{64,32},{96,128},{128,96},{160,192},{192,160},{224... | collective-permute-start | bytes 393224 | tf_op jit(solution)/shard_map/ppermute | solution.py:625
  31.8 6.3 %collective-permute-start.7 = (f32[32,8,128]{2,1,0:T(8,128)S(1)}, f32[32,8,128]{2,1,0:T(8,128)S(1)}, u32[]{:S(2)}, u32[]{:S(2)}) collective-permute-start(f32[32,8,128]{2,1,0:T(8,128)S(1)} %get-tuple-element.47.pack), channel_id=1, source_target_pairs={{0,224},{32,64},{64,32},{96,128},{128,96},{160,192},{192,160},{224... | collective-permute-start | bytes 393224 | tf_op jit(solution)/shard_map/ppermute | solution.py:625
  33.8 5.0 %collective-permute-start.6 = (f32[32,8,128]{2,1,0:T(8,128)S(1)}, f32[32,8,128]{2,1,0:T(8,128)S(1)}, u32[]{:S(2)}, u32[]{:S(2)}) collective-permute-start(f32[32,8,128]{2,1,0:T(8,128)S(1)} %get-tuple-element.47.pack), channel_id=1, source_target_pairs={{0,32},{32,0},{64,96},{96,64},{128,160},{160,128},{192,224},{224,1... | collective-permute-start | bytes 393224 | tf_op jit(solution)/shard_map/ppermute | solution.py:625
  54.9 11.4 %collective-permute-start.10 = (f32[66,8,128]{2,1,0:T(8,128)S(1)}, f32[66,8,128]{2,1,0:T(8,128)S(1)}, u32[]{:S(2)}, u32[]{:S(2)}) collective-permute-start(f32[66,8,128]{2,1,0:T(8,128)S(1)} %get-tuple-element.53), channel_id=1, source_target_pairs={{0,32},{32,0},{64,96},{96,64},{128,160},{160,128},{192,224},{224,1... | collective-permute-start | bytes 811016 | tf_op jit(solution)/shard_map/ppermute | solution.py:625
  55.5 10.8 %collective-permute-start.11 = (f32[66,8,128]{2,1,0:T(8,128)S(1)}, f32[66,8,128]{2,1,0:T(8,128)S(1)}, u32[]{:S(2)}, u32[]{:S(2)}) collective-permute-start(f32[66,8,128]{2,1,0:T(8,128)S(1)} %get-tuple-element.54), channel_id=1, source_target_pairs={{0,224},{32,64},{64,32},{96,128},{128,96},{160,192},{192,160},{224... | collective-permute-start | bytes 811016 | tf_op jit(solution)/shard_map/ppermute | solution.py:625
  55.5 8.4 %collective-permute-start.9 = (f32[16,16,128]{2,1,0:T(8,128)S(1)}, f32[16,16,128]{2,1,0:T(8,128)S(1)}, u32[]{:S(2)}, u32[]{:S(2)}) collective-permute-start(f32[16,16,128]{2,1,0:T(8,128)S(1)} %all_to_all.5.own._), channel_id=1, source_target_pairs={{1,2},{2,1},{3,4},{4,3},{5,6},{6,5},{7,8},{8,7},{9,10},{10,9},{11,... | collective-permute-start | bytes 393224 | tf_op jit(solution)/shard_map/ppermute | solution.py:625
  57.8 6.1 %collective-permute-start.8 = (f32[16,16,128]{2,1,0:T(8,128)S(1)}, f32[16,16,128]{2,1,0:T(8,128)S(1)}, u32[]{:S(2)}, u32[]{:S(2)}) collective-permute-start(f32[16,16,128]{2,1,0:T(8,128)S(1)} %all_to_all.5.own._), channel_id=1, source_target_pairs={{0,1},{1,0},{2,3},{3,2},{4,5},{5,4},{6,7},{7,6},{8,9},{9,8},{10,11... | collective-permute-start | bytes 393224 | tf_op jit(solution)/shard_map/ppermute | solution.py:625

commit v3 on v2

--- a/solution.py
+++ b/solution.py
@@ -164,55 +164,44 @@
     return ix, iy, ix % 2 == 0, iy % 2 == 0, ix < nx - 1, ix > 0, iy < ny - 1, iy > 0
 
 
-def pack_x_kernel(f, a, b, xa, xb):
+def pack_kernel(field, *refs):
+    own, *refs = refs
+    before, (xa, xb, ya, yb) = refs[:-4], refs[-4:]
     ix, iy, even_x, even_y, *_ = places()
-    sub = iota((8, 128), 0)
+    lane, sub = iota((8, 128), 1), iota((8, 128), 0)
+
+    def y_step(z, carry):
+        parts = []
+        for shift in (0, YH):
+            first = roll(own[z], shift + YH * field, 1)
+            second = roll(own[z + 32], shift + YH * field + 64, 1)
+            parts.append(jnp.where(lane < 64, first, second))
+        low, high = parts
+        here = (lane % 64 >= YH * field) & (lane % 64 < YH * (field + 1))
+        for out, value, old in ((ya, either(even_y, high, low), 2), (yb, either(even_y, low, high), 3)):
+            out[z] = jnp.where(here, value, before[old][z]) if before else only(here, value)
+        return carry
+
+    lax.fori_loop(0, 32, y_step, 0, unroll=8)
 
     def x_step(q, carry):
         extra_low = extra_high = jnp.zeros((8, 128), F32)
         for j in range(4):
             z = 4 * q + j
-            fz, az, bz = f[z], a[z], b[z]
-            low = jnp.where(sub < 3, fz, jnp.where(sub < 6, roll(az, 3, 0), roll(bz, 6, 0)))
-            high = jnp.where(sub < 3, roll(fz, 3, 0), jnp.where(sub < 6, roll(az, 6, 0), roll(bz, 2, 0)))
-            here = sub // 2 == j
-            extra_low = jnp.where(here, roll(bz, 2 * j - 2, 0), extra_low)
-            extra_high = jnp.where(here, roll(bz, 2 * j - 6, 0), extra_high)
-            xa[z] = either(even_x, high, low)
-            xb[z] = either(even_x, low, high)
-        xa[64 + q] = either(even_x, extra_high, extra_low)
-        xb[64 + q] = either(even_x, extra_low, extra_high)
+            value = own[z]
+            low, high = roll(value, 3 * field, 0), roll(value, (3, 6, 2)[field], 0)
+            for out, chosen, old in ((xa, either(even_x, high, low), 0), (xb, either(even_x, low, high), 1)):
+                out[z] = jnp.where(sub < 3 * field, before[old][z], chosen) if before else chosen
+            if field == 2:
+                here = sub // 2 == j
+                extra_low = jnp.where(here, roll(value, 2 * j - 2, 0), extra_low)
+                extra_high = jnp.where(here, roll(value, 2 * j - 6, 0), extra_high)
+        if field == 2:
+            xa[64 + q] = either(even_x, extra_high, extra_low)
+            xb[64 + q] = either(even_x, extra_low, extra_high)
         return carry
 
     lax.fori_loop(0, 16, x_step, 0, unroll=4)
-
-
-def pack_y_kernel(f_in, a_in, b_in, f, a, b, ya, yb, sems):
-    ix, iy, even_x, even_y, *_ = places()
-    lane = iota((8, 128), 1)
-    copies = [
-        pltpu.make_async_copy(src, dst, sems.at[n]) for n, (src, dst) in enumerate(((f_in, f), (a_in, a), (b_in, b)))
-    ]
-    for copy in copies:
-        copy.start()
-    for copy in copies:
-        copy.wait()
-
-    def y_side(z, shift):
-        return jnp.where(
-            lane < YH,
-            roll(f[z], shift, 1),
-            jnp.where(lane < 2 * YH, roll(a[z], shift + YH, 1), roll(b[z], shift + 2 * YH, 1)),
-        )
-
-    def y_step(z, carry):
-        low = jnp.where(lane < 64, y_side(z, 0), roll(y_side(z + 32, 0), 64, 1))
-        high = jnp.where(lane < 64, y_side(z, YH), roll(y_side(z + 32, YH), 64, 1))
-        ya[z] = either(even_y, high, low)
-        yb[z] = either(even_y, low, high)
-        return carry
-
-    lax.fori_loop(0, 32, y_step, 0, unroll=8)
 
 
 def corner_kernel(ya, yb, ca, cb):
@@ -249,7 +238,7 @@
     return 0.125 * (wide[pl.ds(0, 128, stride=2), :] + wide[pl.ds(1, 128, stride=2), :])
 
 
-def own_rows_kernel(f, a, b, ya, yb, fx, ax, bx, alpha, beta, pairs, wide):
+def own_rows_kernel(f, a, b, ya, yb, fx, ax, bx, ab, pairs, wide):
     ix, iy, even_x, even_y, has_right, has_left, has_above, has_below = places()
     lane = iota((8, 128), 1)
 
@@ -265,15 +254,15 @@
     lax.fori_loop(0, 32, unpack, 0, unroll=8)
     bx[64] = jnp.zeros((8, 256), F32)
     sum_planes(ax, pairs, 8)
-    alpha[...] = coarse_fine(pairs, wide)
+    ab[0:16] = coarse_fine(pairs, wide).reshape(16, 8, 128)
     sum_planes(bx, pairs, 8)
-    beta[...] = coarse_fine(pairs, wide)
+    ab[16:32] = coarse_fine(pairs, wide).reshape(16, 8, 128)
 
 
 def fine_down_kernel(
-    f, a, b, alpha_in, beta_in, xa, xb, ca, cb,
-    pack, ra, rb, own_u, fx, ws, wl, wm, inv, diag,
-    ax, bx, u, v, pairs, wide,
+    f, a, b, xa, xb, ca, cb,
+    source, u, fx, ws, wl, wm, inv, diag,
+    ax, bx, v, pairs, wide,
 ):
     ix, iy, even_x, even_y, has_right, has_left, has_above, has_below = places()
     lane, sub = iota((8, 128), 1), iota((8, 128), 0)
@@ -315,32 +304,22 @@
     level.build()
     level.sweeps_down()
     level.residual_pairs(u, pairs, 8)
-    source = coarse_fine(pairs, wide)
-    alpha, beta = alpha_in[...], beta_in[...]
-
-    at = iota((128, 128), 1)
-    pack[0:16] = jnp.where(at < 64, source, roll(alpha, 64, 1)).reshape(16, 8, 128)
-    second = jnp.zeros((128, 128), F32)
-    for end, part in (
-        (112, roll(beta, -16, 1)),
-        (104, roll(beta, 32, 1)),
-        (96, roll(alpha, -32, 1)),
-        (88, roll(alpha, 16, 1)),
-        (80, roll(source, -48, 1)),
-        (72, source),
-        (64, beta),
-    ):
-        second = jnp.where(at < end, part, second)
-    pack[16:32] = second.reshape(16, 8, 128)
-
-    for z in range(32):
-        own_u[z] = u[z, 0:8, :]
-        own_u[z + 32] = u[z + 32, 0:8, :]
+    source[...] = coarse_fine(pairs, wide).reshape(16, 8, 128)
+
+
+def u_edges_kernel(u, ra, rb):
+    ix, iy, even_x, even_y, *_ = places()
+    lane, sub = iota((8, 128), 1), iota((8, 128), 0)
+
+    def main(z, carry):
         one, two = u[z, 0:8, 0:128], u[z + 32, 0:8, 0:128]
         low = jnp.where(sub < 4, one, roll(two, 4, 0))
         high = jnp.where(sub < 4, roll(one, 4, 0), two)
         ra[z] = either(even_x, high, low)
         rb[z] = either(even_x, low, high)
+        return carry
+
+    lax.fori_loop(0, 32, main, 0, unroll=8)
     for t in range(2):
         low = high = jnp.zeros((8, 128), F32)
         for g in range(2):
@@ -356,36 +335,26 @@
 
 
 def middle_down_kernel(
-    pack, ga, gb,
+    source_in, ga, gb, ab, aba, abb,
     copies, f1, a1, b, u,
     ws, wl, wm, inv, diag, v, pairs, wide,
 ):
     ix, iy, even_x, even_y, has_right, has_left, has_above, has_below = places()
-    lane, sub = iota((8, 128), 1), iota((8, 128), 0)
-
-    def fields(one, two):
-        def halo(right, left):
-            return jnp.where(lane < 72, roll(two, right, 1), only(lane >= 120, roll(two, left, 1)))
-
-        return (
-            jnp.where(lane < 64, one, halo(0, 48)),
-            jnp.where(lane < 64, roll(one, 64, 1), halo(-16, 32)),
-            jnp.where(lane < 64, two, halo(-32, 16)),
-        )
+    sub = iota((8, 128), 0)
 
     def unpack(t, carry):
-        own = fields(pack[t], pack[16 + t])
-        right = fields(
-            only(has_right, either(even_x, ga[t], gb[t])), only(has_right, either(even_x, ga[16 + t], gb[16 + t]))
-        )
-        left = fields(
-            only(has_left, either(even_x, gb[t], ga[t])), only(has_left, either(even_x, gb[16 + t], ga[16 + t]))
-        )
-        for n, full in enumerate((f1, a1, b)):
-            full[2 * t, 0:8] = jnp.where(sub < 4, own[n], roll(right[n], 4, 0))
-            full[2 * t, 8:16] = only(sub >= 4, roll(left[n], 4, 0))
-            full[2 * t + 1, 0:8] = jnp.where(sub < 4, roll(own[n], 4, 0), right[n])
-            full[2 * t + 1, 8:16] = only(sub >= 4, left[n])
+        for own, one, two, at, full in (
+            (source_in, ga, gb, 0, f1),
+            (ab, aba, abb, 0, a1),
+            (ab, aba, abb, 16, b),
+        ):
+            mine = own[at + t]
+            right = only(has_right, either(even_x, one[at + t], two[at + t]))
+            left = only(has_left, either(even_x, two[at + t], one[at + t]))
+            full[2 * t, 0:8] = jnp.where(sub < 4, mine, roll(right, 4, 0))
+            full[2 * t, 8:16] = only(sub >= 4, roll(left, 4, 0))
+            full[2 * t + 1, 0:8] = jnp.where(sub < 4, roll(mine, 4, 0), right)
+            full[2 * t + 1, 8:16] = only(sub >= 4, left)
         return carry
 
     lax.fori_loop(0, 16, unpack, 0, unroll=4)
@@ -414,7 +383,7 @@
             copies[2 * d + k] = block
 
 
-def edges_kernel(_, ra, rb, b, u, sa, sb):
+def edges_kernel(_, b, u, sa, sb):
     ix, iy, even_x, even_y, *_ = places()
     sub = iota((8, 128), 0)
 
@@ -430,8 +399,6 @@
         return carry
 
     lax.fori_loop(0, 32, edges, 0, unroll=8)
-    sa[32:66] = ra[...]
-    sb[32:66] = rb[...]
 
 
 def bottom_kernel(
@@ -497,27 +464,28 @@
     out[...] = v2[0:16]
 
 
-def ready_kernel(xa, xb, own_u, u0):
+def ready_kernel(copies_in, xa, xb, own_u, copies, u0):
     ix, iy, even_x, even_y, has_right, has_left, has_above, has_below = places()
     lane, sub = iota((8, 128), 1), iota((8, 128), 0)
 
     for z in range(64):
         t, e = z % 32, z // 32
-        right = only(has_right, either(even_x, xa[32 + t], xb[32 + t]))
-        left = only(has_left, either(even_x, xb[32 + t], xa[32 + t]))
-        u0[z, 0:8, :] = own_u[z]
+        right = only(has_right, either(even_x, xa[t], xb[t]))
+        left = only(has_left, either(even_x, xb[t], xa[t]))
+        u0[z, 0:8, :] = own_u[z, 0:8, :]
         u0[z, 8:16, 0:128] = jnp.where(
             sub < 4, roll(right, 4, 0) if e else right, left if e else roll(left, 4, 0)
         )
         g, k = z // 16, z % 16
         t, e = 32 + g // 2, g % 2
-        right = only(has_right, either(even_x, xa[32 + t], xb[32 + t]))
-        left = only(has_left, either(even_x, xb[32 + t], xa[32 + t]))
+        right = only(has_right, either(even_x, xa[t], xb[t]))
+        left = only(has_left, either(even_x, xb[t], xa[t]))
         edge = jnp.where(sub < 4, roll(right, 4, 0) if e else right, left if e else roll(left, 4, 0))
         u0[z, 8:16, 128:256] = jnp.where(
             lane < 4, roll(edge, -8 * k, 1), only(lane >= 124, roll(edge, 120 - 8 * k, 1))
         )
     u0[64] = jnp.zeros((16, 256), F32)
+    copies[...] = copies_in[...]
 
 
 def up_kernel(
@@ -591,20 +559,18 @@
     lax.fori_loop(0, 64, out, 0, unroll=4)
 
 
-def call(kernel, outs, scratch, n_in, any_in=0, sems=0, cost=1):
+def call(kernel, outs, scratch, n_in, cost=1):
     vmem = pl.BlockSpec(memory_space=pltpu.VMEM)
-    anywhere = pl.BlockSpec(memory_space=pltpu.HBM)
-    scratch_shapes = [pltpu.VMEM(shape, F32) for shape in scratch]
-    if sems:
-        scratch_shapes.append(pltpu.SemaphoreType.DMA((sems,)))
     need = sum(4 * p * r * n for p, r, n in ((1,) * (3 - len(shape)) + shape for shape in scratch))
     return pl.pallas_call(
         kernel,
         out_shape=[jax.ShapeDtypeStruct(shape, F32) for shape in outs],
-        in_specs=[vmem] * (n_in - any_in) + [anywhere] * any_in,
+        in_specs=[vmem] * n_in,
         out_specs=[vmem] * len(outs),
-        scratch_shapes=scratch_shapes,
-        cost_estimate=pl.CostEstimate(flops=0, bytes_accessed=cost * 3_000_000, transcendentals=0),
+        scratch_shapes=[pltpu.VMEM(shape, F32) for shape in scratch],
+        cost_estimate=pl.CostEstimate(
+            flops=cost * 1_000_000_000, bytes_accessed=cost * 3_000_000, transcendentals=0
+        ),
         compiler_params=pltpu.CompilerParams(vmem_limit_bytes=need + 4 * 1024 * 1024),
     )
 
@@ -613,10 +579,7 @@
     size = lax.axis_size(axis)
     first = [(i, i ^ 1) for i in range(size)]
     second = [(i, i + 1 if i % 2 else i - 1) for i in range(size)]
-    if axis == "gx":
-        second = [(i, j % size) for i, j in second]
-    else:
-        second = [(i, j) for i, j in second if 0 <= j < size]
+    second = [(i, j % size) for i, j in second]
     return first, second
 
 
@@ -629,40 +592,47 @@
     def tiles(n):
         return (n, 8, 128)
 
-    f, a, b, ya, yb = call(pack_y_kernel, [tiles(64)] * 3 + [tiles(32)] * 2, [], 3, any_in=3, sems=3)(
-        right_side, alpha, beta
-    )
+    f, a, b = right_side, alpha, beta
+    sizes = [tiles(64), tiles(64), tiles(32), tiles(32)]
+    packs = call(functools.partial(pack_kernel, 0), sizes, [], 1)(f)
+    packs = call(functools.partial(pack_kernel, 1), sizes, [], 5)(a, *packs)
+    sizes = [tiles(80), tiles(80), tiles(32), tiles(32)]
+    xa, xb, ya, yb = call(functools.partial(pack_kernel, 2), sizes, [], 5)(b, *packs)
+    xa, xb = swap(xa, xb, "gx")
     ya, yb = swap(ya, yb, "gy")
-    xa, xb = call(pack_x_kernel, [tiles(80), tiles(80)], [], 3, cost=50)(f, a, b)
-    xa, xb = swap(xa, xb, "gx")
     ca, cb = call(corner_kernel, [tiles(32), tiles(32)], [], 2)(ya, yb)
     ca, cb = swap(ca, cb, "gx")
     top, top_more = (64, 8, 256), (65, 8, 256)
-    f, a, b, alpha, beta = call(
-        own_rows_kernel, [top, top, top_more, (128, 128), (128, 128)], [(32, 8, 256), (256, 128)], 5, cost=50
+    f, a, b, ab = call(
+        own_rows_kernel, [top, top, top_more, tiles(32)], [(32, 8, 256), (256, 128)], 5, cost=3
     )(f, a, b, ya, yb)
+    aba, abb = swap(ab, ab, "gx")
 
     full, more = (64, 16, 256), (65, 16, 256)
-    pack, ra, rb, own_u, *fine = call(
+    source, u, *fine = call(
         fine_down_kernel,
-        [tiles(32), tiles(34), tiles(34), top, top] + [full] * 5,
-        [top, top_more, more, more, (32, 8, 256), (256, 128)],
-        9,
-    )(f, a, b, alpha, beta, xa, xb, ca, cb)
-    ga, gb = swap(pack, pack, "gx")
+        [tiles(16), more, top] + [full] * 5,
+        [top, top_more, more, (32, 8, 256), (256, 128)],
+        7,
+        cost=50,
+    )(f, a, b, xa, xb, ca, cb)
+    ga, gb = swap(source, source, "gx")
+    ra, rb = call(u_edges_kernel, [tiles(34), tiles(34)], [], 1, cost=50)(u)
+    ra, rb = swap(ra, rb, "gx")
 
     full, more = (32, 16, 128), (33, 16, 128)
     copies, f1, a1, b1, u1 = call(
         middle_down_kernel,
         [(16, 16, 128), full, full, more, more],
         [full, full, full, full, full, more, tiles(16), (128, 128)],
-        3,
-    )(pack, ga, gb)
+        6,
+        cost=50,
+    )(source, ga, gb, ab, aba, abb)
+    copies, u0 = call(ready_kernel, [(16, 16, 128), (65, 16, 256)], [], 4)(copies, ra, rb, u)
     own = lax.all_to_all(copies, "gx", 0, 0, tiled=True)
     ya, yb = swap(own, own, "gy")
-    sa, sb = call(edges_kernel, [tiles(66), tiles(66)], [], 5, cost=50)(own, ra, rb, b1, u1)
+    sa, sb = call(edges_kernel, [tiles(32), tiles(32)], [], 3, cost=50)(own, b1, u1)
     sa, sb = swap(sa, sb, "gx")
-    (u0,) = call(ready_kernel, [(65, 16, 256)], [], 3)(sa, sb, own_u)
 
     def level(planes, rows, lanes):
         one, two = (planes, rows, lanes), (planes + 1, rows, lanes)

time: 73.7 us -> 70 us (0.950)
  waiting for transfers between devices: 17 us -> 13.4 us
  starting transfers between devices: 19.3 us -> 21.5 us
  blocking collectives: 13.6 us -> 12.1 us
  local copies, waits for them, and re-layouts: 2.84 us -> 1.94 us
    ppermute x12 -> x16, waiting for transfers between devices: 17 us -> 13.4 us  [swap(): return (lax.ppermute(a, axis, first), lax.ppermute(b, axis, second))]
    ppermute x12 -> x16, starting transfers between devices: 19.3 us -> 21.5 us  [swap(): return (lax.ppermute(a, axis, first), lax.ppermute(b, axis, second))]
    all_to_all x1, blocking collectives: 13.6 us -> 12.1 us  [body(): own = lax.all_to_all(copies, 'gx', 0, 0, tiled=True)]
    unnamed x6 -> x8, local copies, waits for them, and re-layouts: 2.84 us -> 1.94 us
    pallas_call x6 -> x8, Pallas kernels: 8.17 us -> 8.41 us  [the longest x1 5.06 us: body(): call(fine_down_kernel, [tiles(16), more, top] + [full] * 5, [top, top_mor...]
  transfers between devices with their start and end apart: 12 -> 16, of which waited for: 6 -> 5; matrix products, arithmetic and copies ran while one was open for 0% -> 0% of each run, Pallas kernels for 5% -> 16%
where the time goes in v3:
time: 70 us; the launch traced here: 69.3 us
  starting transfers between devices  21.5 us (31%)
  Pallas kernels  19.7 us (28%)
  waiting for transfers between devices  13.4 us (19%)
  blocking collectives  12.1 us (17%)
  local copies, waits for them, and re-layouts  1.94 us (3%)
  between operations  0.77 us (1%)
    ppermute x16, starting transfers between devices, swap(): return (lax.ppermute(a, axis, first), lax.ppermute(b, axis, second))  21.5 us
    ppermute x16, waiting for transfers between devices, swap(): return (lax.ppermute(a, axis, first), lax.ppermute(b, axis, second))  13.4 us
    all_to_all x1, blocking collectives, body(): own = lax.all_to_all(copies, 'gx', 0, 0, tiled=True)  12.1 us
    pallas_call x1, Pallas kernels, body(): call(up_kernel, [tiles(64), tiles(64)], [(65, 16, 256)] * 2 + level(32, 1...  6.88 us
    pallas_call x1, Pallas kernels, body(): call(fine_down_kernel, [tiles(16), more, top] + [full] * 5, [top, top_mor...  5.06 us
    pallas_call x1, Pallas kernels, body(): call(bottom_kernel, [(16, 16, 128)], level(16, 16, 128) + level(8, 8, 128...  2.34 us
    pallas_call x1, Pallas kernels, body(): call(middle_down_kernel, [(16, 16, 128), full, full, more, more], [full,...  1.95 us
    unnamed x8, local copies, waits for them, and re-layouts  1.94 us
  transfers between devices with their start and end apart: 16, of which 5 were waited for; matrix products, arithmetic and copies ran while one was open for 0% of the time, Pallas kernels for 16%

profile of v3, /device:TPU:24, one launch (start us, length us, event | category | flops | bytes accessed | tf_op | source)
XLA Modules:
  0.0 69.3 jit_solution(6718351523894766988)
XLA Ops:
  0.6 0.9 %copy-done = f32[64,8,128]{2,1,0:T(8,128)S(1)} copy-done((f32[64,8,128]{2,1,0:T(8,128)S(1)}, f32[64,8,128]{2,1,0:T(8,128)}, u32[]{:S(2)}) %copy-start) | copy-done | bytes 262168
  2.0 0.5 copy-done.2
  2.5 0.5 shard_map.51
  3.0 0.5 copy-done.3
  3.5 0.5 shard_map.52
  4.1 3.0 %collective-permute-start.1 = (f32[32,8,128]{2,1,0:T(8,128)S(1)}, f32[32,8,128]{2,1,0:T(8,128)S(1)}, u32[]{:S(2)}, u32[]{:S(2)}) collective-permute-start(f32[32,8,128]{2,1,0:T(8,128)S(1)} %get-tuple-element.48), channel_id=1, source_target_pairs={{0,31},{1,2},{2,1},{3,4},{4,3},{5,6},{6,5},{7,8},{8,7},{9,10},{10,... | collective-permute-start | bytes 393224 | tf_op jit(solution)/shard_map/ppermute | solution.py:588
  7.1 1.9 %collective-permute-start.2 = (f32[80,8,128]{2,1,0:T(8,128)S(1)}, f32[80,8,128]{2,1,0:T(8,128)S(1)}, u32[]{:S(2)}, u32[]{:S(2)}) collective-permute-start(f32[80,8,128]{2,1,0:T(8,128)S(1)} %get-tuple-element.52), channel_id=1, source_target_pairs={{0,32},{32,0},{64,96},{96,64},{128,160},{160,128},{192,224},{224,1... | collective-permute-start | bytes 983048 | tf_op jit(solution)/shard_map/ppermute | solution.py:588
  9.1 4.9 %collective-permute-start.3 = (f32[80,8,128]{2,1,0:T(8,128)S(1)}, f32[80,8,128]{2,1,0:T(8,128)S(1)}, u32[]{:S(2)}, u32[]{:S(2)}) collective-permute-start(f32[80,8,128]{2,1,0:T(8,128)S(1)} %get-tuple-element.53), channel_id=1, source_target_pairs={{0,224},{32,64},{64,32},{96,128},{128,96},{160,192},{192,160},{224... | collective-permute-start | bytes 983048 | tf_op jit(solution)/shard_map/ppermute | solution.py:588
  14.2 3.5 %collective-permute-start.5 = (f32[32,8,128]{2,1,0:T(8,128)S(1)}, f32[32,8,128]{2,1,0:T(8,128)S(1)}, u32[]{:S(2)}, u32[]{:S(2)}) collective-permute-start(f32[32,8,128]{2,1,0:T(8,128)S(1)} %get-tuple-element.55), channel_id=1, source_target_pairs={{0,224},{32,64},{64,32},{96,128},{128,96},{160,192},{192,160},{224... | collective-permute-start | bytes 393224 | tf_op jit(solution)/shard_map/ppermute | solution.py:588
  17.7 1.4 %shard_map.53 = (f32[64,8,256]{2,1,0:T(8,128)S(1)}, f32[64,8,256]{2,1,0:T(8,128)S(1)}, f32[65,8,256]{2,1,0:T(8,128)S(1)}, f32[32,8,128]{2,1,0:T(8,128)S(1)}) custom-call(f32[64,8,128]{2,1,0:T(8,128)S(1)} %copy-done.1, f32[64,8,128]{2,1,0:T(8,128)S(1)} %copy-done.2, f32[64,8,128]{2,1,0:T(8,128)S(1)} %copy-done.3, f32[32,8,128]{2,1,0:T(8,128)S(1)} %collective-permute-done.ya, ...), custom_call_target="tpu_custom_call" | custom-call | flops 3000000000 | bytes 9000000 | tf_op jit(solution)/shard_map/pallas_call | solution.py:606
  19.2 0.9 %collective-permute-start.8 = (f32[32,8,128]{2,1,0:T(8,128)S(1)}, f32[32,8,128]{2,1,0:T(8,128)S(1)}, u32[]{:S(2)}, u32[]{:S(2)}) collective-permute-start(f32[32,8,128]{2,1,0:T(8,128)S(1)} %get-tuple-element.57.ab), channel_id=1, source_target_pairs={{0,32},{32,0},{64,96},{96,64},{128,160},{160,128},{192,224},{224,1... | collective-permute-start | bytes 393224 | tf_op jit(solution)/shard_map/ppermute | solution.py:588
  20.1 4.3 %collective-permute-done.5.cb = f32[32,8,128]{2,1,0:T(8,128)S(1)} collective-permute-done((f32[32,8,128]{2,1,0:T(8,128)S(1)}, f32[32,8,128]{2,1,0:T(8,128)S(1)}, u32[]{:S(2)}, u32[]{:S(2)}) %collective-permute-start.5) | collective-permute-done | bytes 131104 | tf_op jit(solution)/shard_map/ppermute | solution.py:588
  24.5 5.1 %shard_map.55 = (f32[16,8,128]{2,1,0:T(8,128)S(1)}, f32[65,16,256]{2,1,0:T(8,128)S(1)}, f32[64,8,256]{2,1,0:T(8,128)S(1)}, f32[64,16,256]{2,1,0:T(8,128)S(1)}, f...) custom-call(f32[64,8,256]{2,1,0:T(8,128)S(1)} %get-tuple-element.49., ...), custom_call_target="tpu_custom_call" | custom-call | flops 49999998976 | bytes 150000000 | tf_op jit(solution)/shard_map/pallas_call | solution.py:612
  29.5 3.0 %collective-permute-start.7 = (f32[16,8,128]{2,1,0:T(8,128)S(1)}, f32[16,8,128]{2,1,0:T(8,128)S(1)}, u32[]{:S(2)}, u32[]{:S(2)}) collective-permute-start(f32[16,8,128]{2,1,0:T(8,128)S(1)} %get-tuple-element.56.source_in), channel_id=1, source_target_pairs={{0,224},{32,64},{64,32},{96,128},{128,96},{160,192},{192,160},{224... | collective-permute-start | bytes 196616 | tf_op jit(solution)/shard_map/ppermute | solution.py:588
  32.9 2.1 %collective-permute-start.10 = (f32[34,8,128]{2,1,0:T(8,128)S(1)}, f32[34,8,128]{2,1,0:T(8,128)S(1)}, u32[]{:S(2)}, u32[]{:S(2)}) collective-permute-start(f32[34,8,128]{2,1,0:T(8,128)S(1)} %get-tuple-element.60), channel_id=1, source_target_pairs={{0,32},{32,0},{64,96},{96,64},{128,160},{160,128},{192,224},{224,1... | collective-permute-start | bytes 417800 | tf_op jit(solution)/shard_map/ppermute | solution.py:588
  35.3 0.4 collective-permute-done.7.gb
  35.7 1.1 %collective-permute-done.6.ga = f32[16,8,128]{2,1,0:T(8,128)S(1)} collective-permute-done((f32[16,8,128]{2,1,0:T(8,128)S(1)}, f32[16,8,128]{2,1,0:T(8,128)S(1)}, u32[]{:S(2)}, u32[]{:S(2)}) %collective-permute-start.6) | collective-permute-done | bytes 65568 | tf_op jit(solution)/shard_map/ppermute | solution.py:588
  36.8 1.9 %shard_map.56 = (f32[16,16,128]{2,1,0:T(8,128)S(1)}, f32[32,16,128]{2,1,0:T(8,128)S(1)}, f32[32,16,128]{2,1,0:T(8,128)S(1)}, f32[33,16,128]{2,1,0:T(8,128)S(1)}, f32[33,16,128]{2,1,0:T(8,128)S(1)}) custom-call(f32[16,8,128]{2,1,0:T(8,128)S(1)} %get-tuple-element.56.source_in, f32[16,8,128]{2,1,0:T(8,128)S(1)} %collective-permute-done.6.ga, ...), custom_call_target="tpu_custom_call" | custom-call | flops 49999998976 | bytes 150000000 | tf_op jit(solution)/shard_map/pallas_call | solution.py:624
  38.8 2.4 %collective-permute-done.11.xb = f32[34,8,128]{2,1,0:T(8,128)S(1)} collective-permute-done((f32[34,8,128]{2,1,0:T(8,128)S(1)}, f32[34,8,128]{2,1,0:T(8,128)S(1)}, u32[]{:S(2)}, u32[]{:S(2)}) %collective-permute-start.11) | collective-permute-done | bytes 139296 | tf_op jit(solution)/shard_map/ppermute | solution.py:588
  41.5 12.1 %all_to_all.5.own._ = f32[16,16,128]{2,1,0:T(8,128)S(1)} all-to-all(f32[16,16,128]{2,1,0:T(8,128)S(1)} %get-tuple-element.62), channel_id=1, replica_groups=mesh['gx'=8,'gy'=32] {'gx'}, dimensions={0} | all-to-all | bytes 262144 | tf_op jit(solution)/shard_map/all_to_all | solution.py:632
  54.0 0.7 collective-permute-start.14
  55.1 5.0 %collective-permute-done.13.yb = f32[16,16,128]{2,1,0:T(8,128)S(1)} collective-permute-done((f32[16,16,128]{2,1,0:T(8,128)S(1)}, f32[16,16,128]{2,1,0:T(8,128)S(1)}, u32[]{:S(2)}, u32[]{:S(2)}) %collective-permute-start.13) | collective-permute-done | bytes 131104 | tf_op jit(solution)/shard_map/ppermute | solution.py:588
  60.0 2.3 %shard_map.59.v2 = f32[16,16,128]{2,1,0:T(8,128)S(1)} custom-call(f32[16,16,128]{2,1,0:T(8,128)S(1)} %all_to_all.5.own._, f32[16,16,128]{2,1,0:T(8,128)S(1)} %collective-permute-done.12.ya, f32[16,16,128]{2,1,0:T(8,128)S(1)} %collective-permute-done.13.yb), custom_call_target="tpu_custom_call" | custom-call | flops 49999998976 | bytes 150000000 | tf_op jit(solution)/shard_map/pallas_call | solution.py:641
  62.4 6.9 %shard_map.61 = (f32[64,8,128]{2,1,0:T(8,128)}, f32[64,8,128]{2,1,0:T(8,128)}) custom-call(f32[16,16,128]{2,1,0:T(8,128)S(1)} %shard_map.59.v2, f32[32,8,128]{2,1,0:T(8,128)S(1)} %collective-permute-done.14.xa, f32[32,8,128]{2,1,0:T(8,128)S(1)} %collective-permute-done.15.xb, f32[32,16,128]{2,1,0:T(8,128)S(1)} %get-tuple-element.67.f1, ...), custom_call_target="tpu_custom_call" | custom-call | flops 1000000000 | bytes 3000000 | tf_op jit(solution)/shard_map/pallas_call | solution.py:649
  (29 shorter events, 2.5 us)
Async XLA Ops:
  0.6 1.0 %copy-start = (f32[64,8,128]{2,1,0:T(8,128)S(1)}, f32[64,8,128]{2,1,0:T(8,128)}, u32[]{:S(2)}) copy-start(f32[64,8,128]{2,1,0:T(8,128)} %f.1) | copy-start | bytes 786436
  1.6 0.9 %copy-start.2 = (f32[64,8,128]{2,1,0:T(8,128)S(1)}, f32[64,8,128]{2,1,0:T(8,128)}, u32[]{:S(2)}) copy-start(f32[64,8,128]{2,1,0:T(8,128)} %a.1) | copy-start | bytes 786436
  2.5 0.9 %copy-start.3 = (f32[64,8,128]{2,1,0:T(8,128)S(1)}, f32[64,8,128]{2,1,0:T(8,128)}, u32[]{:S(2)}) copy-start(f32[64,8,128]{2,1,0:T(8,128)} %b.1) | copy-start | bytes 786436
  4.0 10.0 %collective-permute-start = (f32[32,8,128]{2,1,0:T(8,128)S(1)}, f32[32,8,128]{2,1,0:T(8,128)S(1)}, u32[]{:S(2)}, u32[]{:S(2)}) collective-permute-start(f32[32,8,128]{2,1,0:T(8,128)S(1)} %get-tuple-element.47), channel_id=1, source_target_pairs={{0,1},{1,0},{2,3},{3,2},{4,5},{5,4},{6,7},{7,6},{8,9},{9,8},{10,11... | collective-permute-start | bytes 393224 | tf_op jit(solution)/shard_map/ppermute | solution.py:588
  4.1 9.9 %collective-permute-start.1 = (f32[32,8,128]{2,1,0:T(8,128)S(1)}, f32[32,8,128]{2,1,0:T(8,128)S(1)}, u32[]{:S(2)}, u32[]{:S(2)}) collective-permute-start(f32[32,8,128]{2,1,0:T(8,128)S(1)} %get-tuple-element.48), channel_id=1, source_target_pairs={{0,31},{1,2},{2,1},{3,4},{4,3},{5,6},{6,5},{7,8},{8,7},{9,10},{10,... | collective-permute-start | bytes 393224 | tf_op jit(solution)/shard_map/ppermute | solution.py:588
  7.1 17.3 %collective-permute-start.2 = (f32[80,8,128]{2,1,0:T(8,128)S(1)}, f32[80,8,128]{2,1,0:T(8,128)S(1)}, u32[]{:S(2)}, u32[]{:S(2)}) collective-permute-start(f32[80,8,128]{2,1,0:T(8,128)S(1)} %get-tuple-element.52), channel_id=1, source_target_pairs={{0,32},{32,0},{64,96},{96,64},{128,160},{160,128},{192,224},{224,1... | collective-permute-start | bytes 983048 | tf_op jit(solution)/shard_map/ppermute | solution.py:588
  9.0 8.7 %copy-start.1 = (f32[64,8,128]{2,1,0:T(8,128)S(1)}, f32[64,8,128]{2,1,0:T(8,128)}, u32[]{:S(2)}) copy-start(f32[64,8,128]{2,1,0:T(8,128)} %f.1) | copy-start | bytes 786436
  9.1 15.4 %collective-permute-start.3 = (f32[80,8,128]{2,1,0:T(8,128)S(1)}, f32[80,8,128]{2,1,0:T(8,128)S(1)}, u32[]{:S(2)}, u32[]{:S(2)}) collective-permute-start(f32[80,8,128]{2,1,0:T(8,128)S(1)} %get-tuple-element.53), channel_id=1, source_target_pairs={{0,224},{32,64},{64,32},{96,128},{128,96},{160,192},{192,160},{224... | collective-permute-start | bytes 983048 | tf_op jit(solution)/shard_map/ppermute | solution.py:588
  14.1 5.1 %collective-permute-start.4 = (f32[32,8,128]{2,1,0:T(8,128)S(1)}, f32[32,8,128]{2,1,0:T(8,128)S(1)}, u32[]{:S(2)}, u32[]{:S(2)}) collective-permute-start(f32[32,8,128]{2,1,0:T(8,128)S(1)} %get-tuple-element.54), channel_id=1, source_target_pairs={{0,32},{32,0},{64,96},{96,64},{128,160},{160,128},{192,224},{224,1... | collective-permute-start | bytes 393224 | tf_op jit(solution)/shard_map/ppermute | solution.py:588
  14.2 10.3 %collective-permute-start.5 = (f32[32,8,128]{2,1,0:T(8,128)S(1)}, f32[32,8,128]{2,1,0:T(8,128)S(1)}, u32[]{:S(2)}, u32[]{:S(2)}) collective-permute-start(f32[32,8,128]{2,1,0:T(8,128)S(1)} %get-tuple-element.55), channel_id=1, source_target_pairs={{0,224},{32,64},{64,32},{96,128},{128,96},{160,192},{192,160},{224... | collective-permute-start | bytes 393224 | tf_op jit(solution)/shard_map/ppermute | solution.py:588
  19.1 15.9 %collective-permute-start.9 = (f32[32,8,128]{2,1,0:T(8,128)S(1)}, f32[32,8,128]{2,1,0:T(8,128)S(1)}, u32[]{:S(2)}, u32[]{:S(2)}) collective-permute-start(f32[32,8,128]{2,1,0:T(8,128)S(1)} %get-tuple-element.57.ab), channel_id=1, source_target_pairs={{0,224},{32,64},{64,32},{96,128},{128,96},{160,192},{192,160},{224... | collective-permute-start | bytes 393224 | tf_op jit(solution)/shard_map/ppermute | solution.py:588
  19.2 16.1 %collective-permute-start.8 = (f32[32,8,128]{2,1,0:T(8,128)S(1)}, f32[32,8,128]{2,1,0:T(8,128)S(1)}, u32[]{:S(2)}, u32[]{:S(2)}) collective-permute-start(f32[32,8,128]{2,1,0:T(8,128)S(1)} %get-tuple-element.57.ab), channel_id=1, source_target_pairs={{0,32},{32,0},{64,96},{96,64},{128,160},{160,128},{192,224},{224,1... | collective-permute-start | bytes 393224 | tf_op jit(solution)/shard_map/ppermute | solution.py:588
  29.5 6.2 %collective-permute-start.7 = (f32[16,8,128]{2,1,0:T(8,128)S(1)}, f32[16,8,128]{2,1,0:T(8,128)S(1)}, u32[]{:S(2)}, u32[]{:S(2)}) collective-permute-start(f32[16,8,128]{2,1,0:T(8,128)S(1)} %get-tuple-element.56.source_in), channel_id=1, source_target_pairs={{0,224},{32,64},{64,32},{96,128},{128,96},{160,192},{192,160},{224... | collective-permute-start | bytes 196616 | tf_op jit(solution)/shard_map/ppermute | solution.py:588
  32.6 4.3 %collective-permute-start.6 = (f32[16,8,128]{2,1,0:T(8,128)S(1)}, f32[16,8,128]{2,1,0:T(8,128)S(1)}, u32[]{:S(2)}, u32[]{:S(2)}) collective-permute-start(f32[16,8,128]{2,1,0:T(8,128)S(1)} %get-tuple-element.56.source_in), channel_id=1, source_target_pairs={{0,32},{32,0},{64,96},{96,64},{128,160},{160,128},{192,224},{224,1... | collective-permute-start | bytes 196616 | tf_op jit(solution)/shard_map/ppermute | solution.py:588
  32.9 5.9 %collective-permute-start.10 = (f32[34,8,128]{2,1,0:T(8,128)S(1)}, f32[34,8,128]{2,1,0:T(8,128)S(1)}, u32[]{:S(2)}, u32[]{:S(2)}) collective-permute-start(f32[34,8,128]{2,1,0:T(8,128)S(1)} %get-tuple-element.60), channel_id=1, source_target_pairs={{0,32},{32,0},{64,96},{96,64},{128,160},{160,128},{192,224},{224,1... | collective-permute-start | bytes 417800 | tf_op jit(solution)/shard_map/ppermute | solution.py:588
  35.0 6.3 %collective-permute-start.11 = (f32[34,8,128]{2,1,0:T(8,128)S(1)}, f32[34,8,128]{2,1,0:T(8,128)S(1)}, u32[]{:S(2)}, u32[]{:S(2)}) collective-permute-start(f32[34,8,128]{2,1,0:T(8,128)S(1)} %get-tuple-element.61), channel_id=1, source_target_pairs={{0,224},{32,64},{64,32},{96,128},{128,96},{160,192},{192,160},{224... | collective-permute-start | bytes 417800 | tf_op jit(solution)/shard_map/ppermute | solution.py:588
  53.5 6.5 %collective-permute-start.13 = (f32[16,16,128]{2,1,0:T(8,128)S(1)}, f32[16,16,128]{2,1,0:T(8,128)S(1)}, u32[]{:S(2)}, u32[]{:S(2)}) collective-permute-start(f32[16,16,128]{2,1,0:T(8,128)S(1)} %all_to_all.5.own._), channel_id=1, source_target_pairs={{0,31},{1,2},{2,1},{3,4},{4,3},{5,6},{6,5},{7,8},{8,7},{9,10},{10,... | collective-permute-start | bytes 393224 | tf_op jit(solution)/shard_map/ppermute | solution.py:588
  53.5 6.5 %collective-permute-start.12 = (f32[16,16,128]{2,1,0:T(8,128)S(1)}, f32[16,16,128]{2,1,0:T(8,128)S(1)}, u32[]{:S(2)}, u32[]{:S(2)}) collective-permute-start(f32[16,16,128]{2,1,0:T(8,128)S(1)} %all_to_all.5.own._), channel_id=1, source_target_pairs={{0,1},{1,0},{2,3},{3,2},{4,5},{5,4},{6,7},{7,6},{8,9},{9,8},{10,11... | collective-permute-start | bytes 393224 | tf_op jit(solution)/shard_map/ppermute | solution.py:588
  54.0 8.4 %collective-permute-start.14 = (f32[32,8,128]{2,1,0:T(8,128)S(1)}, f32[32,8,128]{2,1,0:T(8,128)S(1)}, u32[]{:S(2)}, u32[]{:S(2)}) collective-permute-start(f32[32,8,128]{2,1,0:T(8,128)S(1)} %get-tuple-element.65), channel_id=1, source_target_pairs={{0,32},{32,0},{64,96},{96,64},{128,160},{160,128},{192,224},{224,1... | collective-permute-start | bytes 393224 | tf_op jit(solution)/shard_map/ppermute | solution.py:588
  54.6 7.8 %collective-permute-start.15 = (f32[32,8,128]{2,1,0:T(8,128)S(1)}, f32[32,8,128]{2,1,0:T(8,128)S(1)}, u32[]{:S(2)}, u32[]{:S(2)}) collective-permute-start(f32[32,8,128]{2,1,0:T(8,128)S(1)} %get-tuple-element.66), channel_id=1, source_target_pairs={{0,224},{32,64},{64,32},{96,128},{128,96},{160,192},{192,160},{224... | collective-permute-start | bytes 393224 | tf_op jit(solution)/shard_map/ppermute | solution.py:588

commit v4 on v3

--- a/solution.py
+++ b/solution.py
@@ -57,7 +57,7 @@
         self.planes, self.rows, self.lanes = self.f.shape
         self.unroll = unroll
 
-    def build(self):
+    def build(self, weight=None):
         shape = (self.rows, self.lanes)
         sub = iota(shape, 0)
         half = self.half
@@ -83,17 +83,12 @@
             self.wm[m] = wm
             self.diag[m] = diag
             self.inv[m] = inv
+            if weight is not None:
+                self.u[m] = (weight * self.f[m]) * inv
             return wm, after
 
         first = self.b[0]
         lax.fori_loop(0, self.planes, step, (half * first, first), unroll=self.unroll)
-
-    def start(self, weight):
-        def step(m, carry):
-            self.u[m] = (weight * self.f[m]) * self.inv[m]
-            return carry
-
-        lax.fori_loop(0, self.planes, step, 0, unroll=self.unroll)
 
     def beside(self, m, u, after, flow):
         wl, ws, wm = self.wl[m], self.ws[m], self.wm[m]
@@ -113,7 +108,6 @@
         lax.fori_loop(0, self.planes, step, (jnp.zeros_like(first), first), unroll=self.unroll)
 
     def sweeps_down(self):
-        self.start(WEIGHTS[0])
         self.sweep(WEIGHTS[1], self.u, self.v)
         self.sweep(WEIGHTS[2], self.v, self.u)
 
@@ -162,6 +156,35 @@
     ix, iy = lax.axis_index("gx"), lax.axis_index("gy")
     nx, ny = lax.axis_size("gx"), lax.axis_size("gy")
     return ix, iy, ix % 2 == 0, iy % 2 == 0, ix < nx - 1, ix > 0, iy < ny - 1, iy > 0
+
+
+def pieces(plane):
+    for tile in range(3):
+        first = 3 * plane - 8 * tile
+        if -3 < first < 8:
+            yield tile, first, (max(first, 0) - first, min(first + 3, 8) - first)
+
+
+def pack_three(read, low_row, high_row, write):
+    sub = iota((8, 128), 0)
+    low = [jnp.zeros((8, 128), F32)] * 3
+    high = [jnp.zeros((8, 128), F32)] * 3
+    for plane in range(8):
+        rows = read(plane)
+        for tile, first, _ in pieces(plane):
+            here = (sub >= first) & (sub < first + 3)
+            low[tile] = jnp.where(here, roll(rows, first - low_row, 0), low[tile])
+            high[tile] = jnp.where(here, roll(rows, first - high_row, 0), high[tile])
+    for tile in range(3):
+        write(tile, low[tile], high[tile])
+
+
+def unpack_three(plane, into, tile_of, row):
+    sub = iota((8, 128), 0)
+    for tile, first, (low, high) in pieces(plane):
+        here = (sub >= row + low) & (sub < row + high)
+        into = jnp.where(here, roll(tile_of(tile), row - first, 0), into)
+    return into
 
 
 def pack_kernel(field, *refs):
@@ -238,7 +261,7 @@
     return 0.125 * (wide[pl.ds(0, 128, stride=2), :] + wide[pl.ds(1, 128, stride=2), :])
 
 
-def own_rows_kernel(f, a, b, ya, yb, fx, ax, bx, ab, pairs, wide):
+def own_rows_kernel(f, a, b, ya, yb, fx, ax, bx, ab, packed, pairs, wide):
     ix, iy, even_x, even_y, has_right, has_left, has_above, has_below = places()
     lane = iota((8, 128), 1)
 
@@ -257,11 +280,30 @@
     ab[0:16] = coarse_fine(pairs, wide).reshape(16, 8, 128)
     sum_planes(bx, pairs, 8)
     ab[16:32] = coarse_fine(pairs, wide).reshape(16, 8, 128)
+    for t in range(16):
+        packed[t] = jnp.where(lane < 64, ab[t], roll(ab[16 + t], 64, 1))
+    for t in range(4):
+        packed[16 + t] = halo_lanes([ab[t + 4 * q + 16 * n] for q in range(4) for n in range(2)])
+
+
+def halo_lanes(parts):
+    lane = iota((8, 128), 1)
+    packed = jnp.zeros((8, 128), F32)
+    for n, part in enumerate(parts):
+        pair = jnp.where(lane < 16 * n + 8, roll(part, 16 * n - 64, 1), roll(part, 16 * n + 8 - 120, 1))
+        packed = jnp.where(lane // 16 == n, pair, packed)
+    return packed
+
+
+def with_halo_lanes(own, packed, n):
+    lane = iota((8, 128), 1)
+    right, left = roll(packed, 64 - 16 * n, 1), roll(packed, 112 - 16 * n, 1)
+    return jnp.where(lane < 64, own, jnp.where(lane < 72, right, only(lane >= 120, left)))
 
 
 def fine_down_kernel(
     f, a, b, xa, xb, ca, cb,
-    source, u, fx, ws, wl, wm, inv, diag,
+    source, packed, u, fx, ws, wl, wm, inv, diag,
     ax, bx, v, pairs, wide,
 ):
     ix, iy, even_x, even_y, has_right, has_left, has_above, has_below = places()
@@ -301,25 +343,31 @@
     lax.fori_loop(0, 8, unpack, 0, unroll=2)
     bx[64] = jnp.zeros((8, 256), F32)
     level = Level((Rows(f, fx), Rows(a, ax), Rows(b, bx), ws, wl, wm, inv, diag, u, v), 1.0, True, 16)
-    level.build()
+    level.build(WEIGHTS[0])
     level.sweeps_down()
     level.residual_pairs(u, pairs, 8)
     source[...] = coarse_fine(pairs, wide).reshape(16, 8, 128)
+    for t in range(8):
+        packed[t] = jnp.where(lane < 64, source[t], roll(source[t + 8], 64, 1))
+    for t in range(2):
+        packed[8 + t] = halo_lanes([source[t + 2 * q] for q in range(8)])
 
 
 def u_edges_kernel(u, ra, rb):
     ix, iy, even_x, even_y, *_ = places()
     lane, sub = iota((8, 128), 1), iota((8, 128), 0)
 
-    def main(z, carry):
-        one, two = u[z, 0:8, 0:128], u[z + 32, 0:8, 0:128]
-        low = jnp.where(sub < 4, one, roll(two, 4, 0))
-        high = jnp.where(sub < 4, roll(one, 4, 0), two)
-        ra[z] = either(even_x, high, low)
-        rb[z] = either(even_x, low, high)
-        return carry
-
-    lax.fori_loop(0, 32, main, 0, unroll=8)
+    def put(at, low, high):
+        ra[at] = either(even_x, high, low)
+        rb[at] = either(even_x, low, high)
+
+    def main(g, carry):
+        pack_three(
+            lambda z: u[8 * g + z, 0:8, 0:128], 1, 4, lambda tile, low, high: put(3 * g + tile, low, high)
+        )
+        return carry
+
+    lax.fori_loop(0, 8, main, 0, unroll=2)
     for t in range(2):
         low = high = jnp.zeros((8, 128), F32)
         for g in range(2):
@@ -330,37 +378,42 @@
                 turned = roll(edge, 4, 0)
                 low = jnp.where(here, turned if g else edge, low)
                 high = jnp.where(here, edge if g else turned, high)
-        ra[32 + t] = either(even_x, high, low)
-        rb[32 + t] = either(even_x, low, high)
+        put(24 + t, low, high)
 
 
 def middle_down_kernel(
-    source_in, ga, gb, ab, aba, abb,
+    source_in, ga, gb, ab, aba, abb, _a, _b,
     copies, f1, a1, b, u,
     ws, wl, wm, inv, diag, v, pairs, wide,
 ):
     ix, iy, even_x, even_y, has_right, has_left, has_above, has_below = places()
     sub = iota((8, 128), 0)
 
-    def unpack(t, carry):
-        for own, one, two, at, full in (
-            (source_in, ga, gb, 0, f1),
-            (ab, aba, abb, 0, a1),
-            (ab, aba, abb, 16, b),
-        ):
-            mine = own[at + t]
-            right = only(has_right, either(even_x, one[at + t], two[at + t]))
-            left = only(has_left, either(even_x, two[at + t], one[at + t]))
-            full[2 * t, 0:8] = jnp.where(sub < 4, mine, roll(right, 4, 0))
-            full[2 * t, 8:16] = only(sub >= 4, roll(left, 4, 0))
-            full[2 * t + 1, 0:8] = jnp.where(sub < 4, roll(mine, 4, 0), right)
-            full[2 * t + 1, 8:16] = only(sub >= 4, left)
-        return carry
-
-    lax.fori_loop(0, 16, unpack, 0, unroll=4)
+    def right(one, two, at):
+        return only(has_right, either(even_x, one[at], two[at]))
+
+    def left(one, two, at):
+        return only(has_left, either(even_x, two[at], one[at]))
+
+    for t in range(16):
+        sides = []
+        for side in (right, left):
+            f = side(ga, gb, t % 8)
+            f = with_halo_lanes(roll(f, 64, 1) if t >= 8 else f, side(ga, gb, 8 + t % 2), t // 2)
+            both, halo = side(aba, abb, t), side(aba, abb, 16 + t % 4)
+            sides.append(
+                (f, with_halo_lanes(both, halo, t // 4 * 2), with_halo_lanes(roll(both, 64, 1), halo, t // 4 * 2 + 1))
+            )
+        for n, (own, full) in enumerate(((source_in[t], f1), (ab[t], a1), (ab[16 + t], b))):
+            high, low = sides[0][n], sides[1][n]
+            full[2 * t, 0:8] = jnp.where(sub < 4, own, roll(high, 4, 0))
+            full[2 * t, 8:16] = only(sub >= 4, roll(low, 4, 0))
+            full[2 * t + 1, 0:8] = jnp.where(sub < 4, roll(own, 4, 0), high)
+            full[2 * t + 1, 8:16] = only(sub >= 4, low)
+
     b[32] = jnp.zeros((16, 128), F32)
     level = Level((f1, a1, b, ws, wl, wm, inv, diag, u, v), 0.25, True, 16)
-    level.build()
+    level.build(WEIGHTS[0])
     level.sweeps_down()
 
     lanes_in, lanes_out = iota((128, 128), 0), iota((128, 128), 1)
@@ -377,28 +430,41 @@
     beta = coarse()
     level.residual_pairs(u, pairs, 8)
     source = coarse()
+    blocks = []
     for k in range(2):
-        block = source[k] + roll(alpha[k], 32, 1) + roll(beta[k], 64, 1)
+        blocks.append(source[k] + roll(alpha[k], 32, 1) + roll(beta[k], 64, 1))
+    parts = [blocks[0][:8], blocks[0][8:], blocks[1][:8]]
+    last = blocks[1][8:]
+    lane = iota((8, 128), 1)
+    for n, part in enumerate(parts):
+        part = jnp.where(lane < 96, part, roll(last, 96 - 32 * n, 1))
         for d in range(8):
-            copies[2 * d + k] = block
-
-
-def edges_kernel(_, b, u, sa, sb):
+            copies[3 * d + n] = part
+
+
+def edges_kernel(_, ra, rb, b, u, sa, sb):
     ix, iy, even_x, even_y, *_ = places()
-    sub = iota((8, 128), 0)
-
-    def edges(z, carry):
+    lane, sub = iota((8, 128), 1), iota((8, 128), 0)
+    sa[0:26] = ra[...]
+    sb[0:26] = rb[...]
+    high, low = [], []
+    for z in range(32):
         mine, far = u[z, 0:8], u[z, 8:16]
         turned = roll(mine, 4, 0)
-        high = jnp.where(
-            sub >= 4, turned, jnp.where(sub == 3, roll(far, 4, 0), roll(b[z, 8:16], 1, 0))
+        high.append(
+            jnp.where(sub >= 4, turned, jnp.where(sub == 3, roll(far, 4, 0), roll(b[z, 8:16], 1, 0)))
         )
-        low = jnp.where(sub == 1, roll(b[z, 0:8], 5, 0), turned)
-        sa[z] = either(even_x, high, low)
-        sb[z] = either(even_x, low, high)
-        return carry
-
-    lax.fori_loop(0, 32, edges, 0, unroll=8)
+        low.append(jnp.where(sub == 1, roll(b[z, 0:8], 5, 0), turned))
+
+    def packed(parts, t):
+        if t < 16:
+            return jnp.where(lane < 64, parts[t], roll(parts[t + 16], 64, 1))
+        return halo_lanes([parts[t - 16 + 4 * q] for q in range(8)])
+
+    for t in range(20):
+        h, l = packed(high, t), packed(low, t)
+        sa[26 + t] = either(even_x, h, l)
+        sb[26 + t] = either(even_x, l, h)
 
 
 def bottom_kernel(
@@ -411,21 +477,25 @@
     ix, iy, even_x, even_y, has_right, has_left, has_above, has_below = places()
     lane, sub = iota((8, 128), 1), iota((8, 128), 0)
 
-    at = iota((16, 128), 1)
-    for x in range(16):
-        mine = own[x]
-        up = only(has_above, either(even_y, ya[x], yb[x]))
-        down = only(has_below, either(even_y, yb[x], ya[x]))
-        for n, full in enumerate((f2, a2, b2)):
-            full[x] = jnp.where(
-                at < 32,
-                roll(mine, -32 * n, 1),
-                jnp.where(at < 64, roll(up, 32 - 32 * n, 1), only(at >= 96, roll(down, 96 - 32 * n, 1))),
-            )
+    def put(n, x, rows, own_part, up, down):
+        up, down = only(has_above, up), only(has_below, down)
+        (f2, a2, b2)[n][x, rows : rows + 8] = jnp.where(
+            lane < 32, own_part, jnp.where(lane < 64, roll(up, 32, 1), only(lane >= 96, roll(down, 96, 1)))
+        )
+
+    for d in range(8):
+        tiles = [
+            (own[3 * d + t], either(even_y, ya[3 * d + t], yb[3 * d + t]), either(even_y, yb[3 * d + t], ya[3 * d + t]))
+            for t in range(3)
+        ]
+        for n in range(3):
+            for t in range(3):
+                put(n, 2 * d + t // 2, 8 * (t % 2), *(roll(tile, -32 * n, 1) for tile in tiles[t]))
+            put(n, 2 * d + 1, 8, *(roll(tile, -96, 1) for tile in tiles[n]))
     b2[16] = jnp.zeros((16, 128), F32)
     b3[8] = jnp.zeros((8, 128), F32)
     level2 = Level((f2, a2, b2, ws2, wl2, wm2, inv2, diag2, u2, v2), 0.0625, False, 16)
-    level2.build()
+    level2.build(WEIGHTS[0])
     level2.sweeps_down()
 
     lanes_in, lanes_out = iota((128, 128), 0), iota((128, 128), 1)
@@ -444,8 +514,7 @@
     level2.residual_pairs(u2, pairs, 16)
     f3[...] = coarse()
     level3 = Level((f3, a3, b3, ws3, wl3, wm3, inv3, diag3, u3, v3), 0.015625, False, 8)
-    level3.build()
-    level3.start(BOTTOM_WEIGHT)
+    level3.build(BOTTOM_WEIGHT)
 
     def two_sweeps(_, carry):
         level3.sweep(BOTTOM_WEIGHT, u3, v3)
@@ -464,20 +533,18 @@
     out[...] = v2[0:16]
 
 
-def ready_kernel(copies_in, xa, xb, own_u, copies, u0):
+def ready_kernel(xa, xb, own_u, u0):
     ix, iy, even_x, even_y, has_right, has_left, has_above, has_below = places()
     lane, sub = iota((8, 128), 1), iota((8, 128), 0)
 
     for z in range(64):
-        t, e = z % 32, z // 32
-        right = only(has_right, either(even_x, xa[t], xb[t]))
-        left = only(has_left, either(even_x, xb[t], xa[t]))
         u0[z, 0:8, :] = own_u[z, 0:8, :]
-        u0[z, 8:16, 0:128] = jnp.where(
-            sub < 4, roll(right, 4, 0) if e else right, left if e else roll(left, 4, 0)
-        )
+        far, at = own_u[z, 8:16, 0:128], 3 * (z // 8)
+        far = unpack_three(z % 8, far, lambda t: only(has_right, either(even_x, xa[at + t], xb[at + t])), 1)
+        far = unpack_three(z % 8, far, lambda t: only(has_left, either(even_x, xb[at + t], xa[at + t])), 4)
+        u0[z, 8:16, 0:128] = far
         g, k = z // 16, z % 16
-        t, e = 32 + g // 2, g % 2
+        t, e = 24 + g // 2, g % 2
         right = only(has_right, either(even_x, xa[t], xb[t]))
         left = only(has_left, either(even_x, xb[t], xa[t]))
         edge = jnp.where(sub < 4, roll(right, 4, 0) if e else right, left if e else roll(left, 4, 0))
@@ -485,7 +552,6 @@
             lane < 4, roll(edge, -8 * k, 1), only(lane >= 124, roll(edge, 120 - 8 * k, 1))
         )
     u0[64] = jnp.zeros((16, 256), F32)
-    copies[...] = copies_in[...]
 
 
 def up_kernel(
@@ -497,18 +563,20 @@
     sub = iota((8, 128), 0)
     lanes_in, lanes_out = iota((128, 128), 0), iota((128, 128), 1)
 
-    def fill_1(z, carry):
-        right = only(has_right, either(even_x, xa[z], xb[z]))
-        left = only(has_left, either(even_x, xb[z], xa[z]))
+    def received(one, two, z):
+        main = either(even_x, one[26 + z % 16], two[26 + z % 16])
+        halo = either(even_x, one[42 + z % 4], two[42 + z % 4])
+        return with_halo_lanes(roll(main, 64, 1) if z >= 16 else main, halo, z // 4)
+
+    for z in range(32):
+        right = only(has_right, received(xa, xb, z))
+        left = only(has_left, received(xb, xa, z))
         ux1[z, 0:8] = jnp.where(sub < 4, u1[z, 0:8], right)
         ux1[z, 8:16] = jnp.where(sub == 0, right, only(sub >= 3, left))
         bx1[z, 0:8] = b1[z, 0:8]
         bx1[z, 8:16] = jnp.where(
             sub == 0, roll(right, -1, 0), jnp.where(sub == 3, roll(left, 3, 0), b1[z, 8:16])
         )
-        return carry
-
-    lax.fori_loop(0, 32, fill_1, 0, unroll=8)
     bx1[32] = jnp.zeros((16, 128), F32)
     level1 = Level((f1, a1, bx1, ws1, wl1, wm1, inv1, diag1, ux1, v1), 0.25, True, 16)
     level1.build()
@@ -603,36 +671,35 @@
     ca, cb = call(corner_kernel, [tiles(32), tiles(32)], [], 2)(ya, yb)
     ca, cb = swap(ca, cb, "gx")
     top, top_more = (64, 8, 256), (65, 8, 256)
-    f, a, b, ab = call(
-        own_rows_kernel, [top, top, top_more, tiles(32)], [(32, 8, 256), (256, 128)], 5, cost=3
+    f, a, b, ab, packed = call(
+        own_rows_kernel, [top, top, top_more, tiles(32), tiles(20)], [(32, 8, 256), (256, 128)], 5, cost=3
     )(f, a, b, ya, yb)
-    aba, abb = swap(ab, ab, "gx")
+    aba, abb = swap(packed, packed, "gx")
 
     full, more = (64, 16, 256), (65, 16, 256)
-    source, u, *fine = call(
+    source, packed, u, *fine = call(
         fine_down_kernel,
-        [tiles(16), more, top] + [full] * 5,
+        [tiles(16), tiles(10), more, top] + [full] * 5,
         [top, top_more, more, (32, 8, 256), (256, 128)],
         7,
         cost=50,
     )(f, a, b, xa, xb, ca, cb)
-    ga, gb = swap(source, source, "gx")
-    ra, rb = call(u_edges_kernel, [tiles(34), tiles(34)], [], 1, cost=50)(u)
-    ra, rb = swap(ra, rb, "gx")
+    ga, gb = swap(packed, packed, "gx")
+    ra, rb = call(u_edges_kernel, [tiles(26), tiles(26)], [], 1, cost=50)(u)
 
     full, more = (32, 16, 128), (33, 16, 128)
     copies, f1, a1, b1, u1 = call(
         middle_down_kernel,
-        [(16, 16, 128), full, full, more, more],
+        [tiles(24), full, full, more, more],
         [full, full, full, full, full, more, tiles(16), (128, 128)],
-        6,
+        8,
         cost=50,
-    )(source, ga, gb, ab, aba, abb)
-    copies, u0 = call(ready_kernel, [(16, 16, 128), (65, 16, 256)], [], 4)(copies, ra, rb, u)
+    )(source, ga, gb, ab, aba, abb, ra, rb)
     own = lax.all_to_all(copies, "gx", 0, 0, tiled=True)
     ya, yb = swap(own, own, "gy")
-    sa, sb = call(edges_kernel, [tiles(32), tiles(32)], [], 3, cost=50)(own, b1, u1)
+    sa, sb = call(edges_kernel, [tiles(46), tiles(46)], [], 5, cost=50)(own, ra, rb, b1, u1)
     sa, sb = swap(sa, sb, "gx")
+    (u0,) = call(ready_kernel, [(65, 16, 256)], [], 3)(sa, sb, u)
 
     def level(planes, rows, lanes):
         one, two = (planes, rows, lanes), (planes + 1, rows, lanes)

time: 70 us -> 69 us (0.986)
  waiting for transfers between devices: 13.4 us -> 5.52 us
  starting transfers between devices: 21.5 us -> 24.9 us
  Pallas kernels: 19.7 us -> 22.6 us
  blocking collectives: 12.1 us -> 13.1 us
    ppermute x16 -> x14, waiting for transfers between devices: 13.4 us -> 5.52 us  [swap(): return (lax.ppermute(a, axis, first), lax.ppermute(b, axis, second))]
    ppermute x16 -> x14, starting transfers between devices: 21.5 us -> 24.9 us  [swap(): return (lax.ppermute(a, axis, first), lax.ppermute(b, axis, second))]
    pallas_call x1, Pallas kernels: 2.34 us -> 4.44 us  [body(): call(bottom_kernel, [(16, 16, 128)], level(16, 16, 128) + level(8, 8, 128...]
    all_to_all x1, blocking collectives: 12.1 us -> 13.1 us  [body(): own = lax.all_to_all(copies, 'gx', 0, 0, tiled=True)]
  transfers between devices with their start and end apart: 16 -> 14, of which waited for: 5 -> 3; matrix products, arithmetic and copies ran while one was open for 0% -> 0% of each run, Pallas kernels for 16% -> 17%
where the time goes in v4:
time: 69 us; the launch traced here: 68.8 us
  starting transfers between devices  24.9 us (36%)
  Pallas kernels  22.6 us (33%)
  blocking collectives  13.1 us (19%)
  waiting for transfers between devices  5.52 us (8%)
  local copies, waits for them, and re-layouts  1.94 us (3%)
  between operations  0.8 us (1%)
    ppermute x14, starting transfers between devices, swap(): return (lax.ppermute(a, axis, first), lax.ppermute(b, axis, second))  24.9 us
    all_to_all x1, blocking collectives, body(): own = lax.all_to_all(copies, 'gx', 0, 0, tiled=True)  13.1 us
    pallas_call x1, Pallas kernels, body(): call(up_kernel, [tiles(64), tiles(64)], [(65, 16, 256)] * 2 + level(32, 1...  7.16 us
    ppermute x14, waiting for transfers between devices, swap(): return (lax.ppermute(a, axis, first), lax.ppermute(b, axis, second))  5.52 us
    pallas_call x1, Pallas kernels, body(): call(fine_down_kernel, [tiles(16), tiles(10), more, top] + [full] * 5, [t...  5.14 us
    pallas_call x1, Pallas kernels, body(): call(bottom_kernel, [(16, 16, 128)], level(16, 16, 128) + level(8, 8, 128...  4.44 us
    pallas_call x1, Pallas kernels, body(): call(middle_down_kernel, [tiles(24), full, full, more, more], [full, full...  2.19 us
    unnamed x8, local copies, waits for them, and re-layouts  1.94 us
  transfers between devices with their start and end apart: 14, of which 3 were waited for; matrix products, arithmetic and copies ran while one was open for 0% of the time, Pallas kernels for 17%

profile of v4, /device:TPU:24, one launch (start us, length us, event | category | flops | bytes accessed | tf_op | source)
XLA Modules:
  0.0 68.8 jit_solution(7280104169993704292)
XLA Ops:
  0.6 0.9 %copy-done = f32[64,8,128]{2,1,0:T(8,128)S(1)} copy-done((f32[64,8,128]{2,1,0:T(8,128)S(1)}, f32[64,8,128]{2,1,0:T(8,128)}, u32[]{:S(2)}) %copy-start) | copy-done | bytes 262168
  1.6 0.4 shard_map.50
  2.0 0.5 copy-done.2
  2.5 0.5 shard_map.51
  3.0 0.5 copy-done.3
  3.5 0.5 shard_map.52
  4.1 3.0 %collective-permute-start.1 = (f32[32,8,128]{2,1,0:T(8,128)S(1)}, f32[32,8,128]{2,1,0:T(8,128)S(1)}, u32[]{:S(2)}, u32[]{:S(2)}) collective-permute-start(f32[32,8,128]{2,1,0:T(8,128)S(1)} %get-tuple-element.48), channel_id=1, source_target_pairs={{0,31},{1,2},{2,1},{3,4},{4,3},{5,6},{6,5},{7,8},{8,7},{9,10},{10,... | collective-permute-start | bytes 393224 | tf_op jit(solution)/shard_map/ppermute | solution.py:656
  7.1 1.9 %collective-permute-start.2 = (f32[80,8,128]{2,1,0:T(8,128)S(1)}, f32[80,8,128]{2,1,0:T(8,128)S(1)}, u32[]{:S(2)}, u32[]{:S(2)}) collective-permute-start(f32[80,8,128]{2,1,0:T(8,128)S(1)} %get-tuple-element.52), channel_id=1, source_target_pairs={{0,32},{32,0},{64,96},{96,64},{128,160},{160,128},{192,224},{224,1... | collective-permute-start | bytes 983048 | tf_op jit(solution)/shard_map/ppermute | solution.py:656
  9.1 4.9 %collective-permute-start.3 = (f32[80,8,128]{2,1,0:T(8,128)S(1)}, f32[80,8,128]{2,1,0:T(8,128)S(1)}, u32[]{:S(2)}, u32[]{:S(2)}) collective-permute-start(f32[80,8,128]{2,1,0:T(8,128)S(1)} %get-tuple-element.53), channel_id=1, source_target_pairs={{0,224},{32,64},{64,32},{96,128},{128,96},{160,192},{192,160},{224... | collective-permute-start | bytes 983048 | tf_op jit(solution)/shard_map/ppermute | solution.py:656
  14.2 3.5 %collective-permute-start.5 = (f32[32,8,128]{2,1,0:T(8,128)S(1)}, f32[32,8,128]{2,1,0:T(8,128)S(1)}, u32[]{:S(2)}, u32[]{:S(2)}) collective-permute-start(f32[32,8,128]{2,1,0:T(8,128)S(1)} %get-tuple-element.55), channel_id=1, source_target_pairs={{0,224},{32,64},{64,32},{96,128},{128,96},{160,192},{192,160},{224... | collective-permute-start | bytes 393224 | tf_op jit(solution)/shard_map/ppermute | solution.py:656
  17.7 1.5 %shard_map.53 = (f32[64,8,256]{2,1,0:T(8,128)S(1)}, f32[64,8,256]{2,1,0:T(8,128)S(1)}, f32[65,8,256]{2,1,0:T(8,128)S(1)}, f32[32,8,128]{2,1,0:T(8,128)S(1)}, f32[20,8,128]{2,1,0:T(8,128)S(1)}) custom-call(f32[64,8,128]{2,1,0:T(8,128)S(1)} %copy-done.1, f32[64,8,128]{2,1,0:T(8,128)S(1)} %copy-done.2, f32[64,8,128]{2,1,0:T(8,128)S(1)} %copy-done.3, ...), custom_call_target="tpu_custom_call" | custom-call | flops 3000000000 | bytes 9000000 | tf_op jit(solution)/shard_map/pallas_call | solution.py:674
  19.3 5.7 %collective-permute-start.9 = (f32[20,8,128]{2,1,0:T(8,128)S(1)}, f32[20,8,128]{2,1,0:T(8,128)S(1)}, u32[]{:S(2)}, u32[]{:S(2)}) collective-permute-start(f32[20,8,128]{2,1,0:T(8,128)S(1)} %get-tuple-element.59), channel_id=1, source_target_pairs={{0,224},{32,64},{64,32},{96,128},{128,96},{160,192},{192,160},{224... | collective-permute-start | bytes 245768 | tf_op jit(solution)/shard_map/ppermute | solution.py:656
  25.0 5.1 %shard_map.55 = (f32[16,8,128]{2,1,0:T(8,128)S(1)}, f32[10,8,128]{2,1,0:T(8,128)S(1)}, f32[65,16,256]{2,1,0:T(8,128)S(1)}, f32[64,8,256]{2,1,0:T(8,128)S(1)}, f3...) custom-call(f32[64,8,256]{2,1,0:T(8,128)S(1)} %get-tuple-element.49., ...), custom_call_target="tpu_custom_call" | custom-call | flops 49999998976 | bytes 150000000 | tf_op jit(solution)/shard_map/pallas_call | solution.py:680
  30.2 2.0 %collective-permute-start.7 = (f32[10,8,128]{2,1,0:T(8,128)S(1)}, f32[10,8,128]{2,1,0:T(8,128)S(1)}, u32[]{:S(2)}, u32[]{:S(2)}) collective-permute-start(f32[10,8,128]{2,1,0:T(8,128)S(1)} %get-tuple-element.57), channel_id=1, source_target_pairs={{0,224},{32,64},{64,32},{96,128},{128,96},{160,192},{192,160},{224... | collective-permute-start | bytes 122888 | tf_op jit(solution)/shard_map/ppermute | solution.py:656
  32.5 1.7 %collective-permute-done.6.ga = f32[10,8,128]{2,1,0:T(8,128)S(1)} collective-permute-done((f32[10,8,128]{2,1,0:T(8,128)S(1)}, f32[10,8,128]{2,1,0:T(8,128)S(1)}, u32[]{:S(2)}, u32[]{:S(2)}) %collective-permute-start.6) | collective-permute-done | bytes 40992 | tf_op jit(solution)/shard_map/ppermute | solution.py:656
  34.2 1.3 %collective-permute-done.7.gb = f32[10,8,128]{2,1,0:T(8,128)S(1)} collective-permute-done((f32[10,8,128]{2,1,0:T(8,128)S(1)}, f32[10,8,128]{2,1,0:T(8,128)S(1)}, u32[]{:S(2)}, u32[]{:S(2)}) %collective-permute-start.7) | collective-permute-done | bytes 40992 | tf_op jit(solution)/shard_map/ppermute | solution.py:656
  35.5 2.2 %shard_map.57 = (f32[24,8,128]{2,1,0:T(8,128)S(1)}, f32[32,16,128]{2,1,0:T(8,128)S(1)}, f32[32,16,128]{2,1,0:T(8,128)S(1)}, f32[33,16,128]{2,1,0:T(8,128)S(1)}, f32[33,16,128]{2,1,0:T(8,128)S(1)}) custom-call(f32[16,8,128]{2,1,0:T(8,128)S(1)} %get-tuple-element.56.source_in, f32[10,8,128]{2,1,0:T(8,128)S(1)} %collective-permute-done.6.ga, ...), custom_call_target="tpu_custom_call" | custom-call | flops 49999998976 | bytes 150000000 | tf_op jit(solution)/shard_map/pallas_call | solution.py:691
  37.7 13.1 %all_to_all.5.own._ = f32[24,8,128]{2,1,0:T(8,128)S(1)} all-to-all(f32[24,8,128]{2,1,0:T(8,128)S(1)} %get-tuple-element.63), channel_id=1, replica_groups=mesh['gx'=8,'gy'=32] {'gx'}, dimensions={0} | all-to-all | bytes 196608 | tf_op jit(solution)/shard_map/all_to_all | solution.py:698
  50.8 2.3 %collective-permute-start.11 = (f32[24,8,128]{2,1,0:T(8,128)S(1)}, f32[24,8,128]{2,1,0:T(8,128)S(1)}, u32[]{:S(2)}, u32[]{:S(2)}) collective-permute-start(f32[24,8,128]{2,1,0:T(8,128)S(1)} %all_to_all.5.own._), channel_id=1, source_target_pairs={{0,31},{1,2},{2,1},{3,4},{4,3},{5,6},{6,5},{7,8},{8,7},{9,10},{10,... | collective-permute-start | bytes 294920 | tf_op jit(solution)/shard_map/ppermute | solution.py:656
  53.3 0.7 collective-permute-start.12
  53.9 0.4 collective-permute-start.13
  54.4 2.5 %collective-permute-done.11.yb = f32[24,8,128]{2,1,0:T(8,128)S(1)} collective-permute-done((f32[24,8,128]{2,1,0:T(8,128)S(1)}, f32[24,8,128]{2,1,0:T(8,128)S(1)}, u32[]{:S(2)}, u32[]{:S(2)}) %collective-permute-start.11) | collective-permute-done | bytes 98336 | tf_op jit(solution)/shard_map/ppermute | solution.py:656
  56.9 4.4 %shard_map.58.v2 = f32[16,16,128]{2,1,0:T(8,128)S(1)} custom-call(f32[24,8,128]{2,1,0:T(8,128)S(1)} %all_to_all.5.own._, f32[24,8,128]{2,1,0:T(8,128)S(1)} %collective-permute-done.10.ya, f32[24,8,128]{2,1,0:T(8,128)S(1)} %collective-permute-done.11.yb), custom_call_target="tpu_custom_call" | custom-call | flops 49999998976 | bytes 150000000 | tf_op jit(solution)/shard_map/pallas_call | solution.py:708
  61.7 7.2 %shard_map.61 = (f32[64,8,128]{2,1,0:T(8,128)}, f32[64,8,128]{2,1,0:T(8,128)}) custom-call(f32[16,16,128]{2,1,0:T(8,128)S(1)} %shard_map.58.v2, f32[46,8,128]{2,1,0:T(8,128)S(1)} %collective-permute-done.12.xa, f32[46,8,128]{2,1,0:T(8,128)S(1)} %collective-permute-done.13.xb, f32[32,16,128]{2,1,0:T(8,128)S(1)} %get-tuple-element.68.f1, ...), custom_call_target="tpu_custom_call" | custom-call | flops 1000000000 | bytes 3000000 | tf_op jit(solution)/shard_map/pallas_call | solution.py:716
  (25 shorter events, 1.3 us)
Async XLA Ops:
  0.6 1.0 %copy-start = (f32[64,8,128]{2,1,0:T(8,128)S(1)}, f32[64,8,128]{2,1,0:T(8,128)}, u32[]{:S(2)}) copy-start(f32[64,8,128]{2,1,0:T(8,128)} %f.1) | copy-start | bytes 786436
  1.6 0.9 %copy-start.2 = (f32[64,8,128]{2,1,0:T(8,128)S(1)}, f32[64,8,128]{2,1,0:T(8,128)}, u32[]{:S(2)}) copy-start(f32[64,8,128]{2,1,0:T(8,128)} %a.1) | copy-start | bytes 786436
  2.5 0.9 %copy-start.3 = (f32[64,8,128]{2,1,0:T(8,128)S(1)}, f32[64,8,128]{2,1,0:T(8,128)}, u32[]{:S(2)}) copy-start(f32[64,8,128]{2,1,0:T(8,128)} %b.1) | copy-start | bytes 786436
  4.0 10.0 %collective-permute-start = (f32[32,8,128]{2,1,0:T(8,128)S(1)}, f32[32,8,128]{2,1,0:T(8,128)S(1)}, u32[]{:S(2)}, u32[]{:S(2)}) collective-permute-start(f32[32,8,128]{2,1,0:T(8,128)S(1)} %get-tuple-element.47), channel_id=1, source_target_pairs={{0,1},{1,0},{2,3},{3,2},{4,5},{5,4},{6,7},{7,6},{8,9},{9,8},{10,11... | collective-permute-start | bytes 393224 | tf_op jit(solution)/shard_map/ppermute | solution.py:656
  4.1 9.9 %collective-permute-start.1 = (f32[32,8,128]{2,1,0:T(8,128)S(1)}, f32[32,8,128]{2,1,0:T(8,128)S(1)}, u32[]{:S(2)}, u32[]{:S(2)}) collective-permute-start(f32[32,8,128]{2,1,0:T(8,128)S(1)} %get-tuple-element.48), channel_id=1, source_target_pairs={{0,31},{1,2},{2,1},{3,4},{4,3},{5,6},{6,5},{7,8},{8,7},{9,10},{10,... | collective-permute-start | bytes 393224 | tf_op jit(solution)/shard_map/ppermute | solution.py:656
  7.1 17.8 %collective-permute-start.2 = (f32[80,8,128]{2,1,0:T(8,128)S(1)}, f32[80,8,128]{2,1,0:T(8,128)S(1)}, u32[]{:S(2)}, u32[]{:S(2)}) collective-permute-start(f32[80,8,128]{2,1,0:T(8,128)S(1)} %get-tuple-element.52), channel_id=1, source_target_pairs={{0,32},{32,0},{64,96},{96,64},{128,160},{160,128},{192,224},{224,1... | collective-permute-start | bytes 983048 | tf_op jit(solution)/shard_map/ppermute | solution.py:656
  9.0 8.7 %copy-start.1 = (f32[64,8,128]{2,1,0:T(8,128)S(1)}, f32[64,8,128]{2,1,0:T(8,128)}, u32[]{:S(2)}) copy-start(f32[64,8,128]{2,1,0:T(8,128)} %f.1) | copy-start | bytes 786436
  9.1 15.9 %collective-permute-start.3 = (f32[80,8,128]{2,1,0:T(8,128)S(1)}, f32[80,8,128]{2,1,0:T(8,128)S(1)}, u32[]{:S(2)}, u32[]{:S(2)}) collective-permute-start(f32[80,8,128]{2,1,0:T(8,128)S(1)} %get-tuple-element.53), channel_id=1, source_target_pairs={{0,224},{32,64},{64,32},{96,128},{128,96},{160,192},{192,160},{224... | collective-permute-start | bytes 983048 | tf_op jit(solution)/shard_map/ppermute | solution.py:656
  14.1 5.2 %collective-permute-start.4 = (f32[32,8,128]{2,1,0:T(8,128)S(1)}, f32[32,8,128]{2,1,0:T(8,128)S(1)}, u32[]{:S(2)}, u32[]{:S(2)}) collective-permute-start(f32[32,8,128]{2,1,0:T(8,128)S(1)} %get-tuple-element.54), channel_id=1, source_target_pairs={{0,32},{32,0},{64,96},{96,64},{128,160},{160,128},{192,224},{224,1... | collective-permute-start | bytes 393224 | tf_op jit(solution)/shard_map/ppermute | solution.py:656
  14.2 10.8 %collective-permute-start.5 = (f32[32,8,128]{2,1,0:T(8,128)S(1)}, f32[32,8,128]{2,1,0:T(8,128)S(1)}, u32[]{:S(2)}, u32[]{:S(2)}) collective-permute-start(f32[32,8,128]{2,1,0:T(8,128)S(1)} %get-tuple-element.55), channel_id=1, source_target_pairs={{0,224},{32,64},{64,32},{96,128},{128,96},{160,192},{192,160},{224... | collective-permute-start | bytes 393224 | tf_op jit(solution)/shard_map/ppermute | solution.py:656
  19.2 13.3 %collective-permute-start.8 = (f32[20,8,128]{2,1,0:T(8,128)S(1)}, f32[20,8,128]{2,1,0:T(8,128)S(1)}, u32[]{:S(2)}, u32[]{:S(2)}) collective-permute-start(f32[20,8,128]{2,1,0:T(8,128)S(1)} %get-tuple-element.59), channel_id=1, source_target_pairs={{0,32},{32,0},{64,96},{96,64},{128,160},{160,128},{192,224},{224,1... | collective-permute-start | bytes 245768 | tf_op jit(solution)/shard_map/ppermute | solution.py:656
  19.3 13.2 %collective-permute-start.9 = (f32[20,8,128]{2,1,0:T(8,128)S(1)}, f32[20,8,128]{2,1,0:T(8,128)S(1)}, u32[]{:S(2)}, u32[]{:S(2)}) collective-permute-start(f32[20,8,128]{2,1,0:T(8,128)S(1)} %get-tuple-element.59), channel_id=1, source_target_pairs={{0,224},{32,64},{64,32},{96,128},{128,96},{160,192},{192,160},{224... | collective-permute-start | bytes 245768 | tf_op jit(solution)/shard_map/ppermute | solution.py:656
  30.1 4.1 %collective-permute-start.6 = (f32[10,8,128]{2,1,0:T(8,128)S(1)}, f32[10,8,128]{2,1,0:T(8,128)S(1)}, u32[]{:S(2)}, u32[]{:S(2)}) collective-permute-start(f32[10,8,128]{2,1,0:T(8,128)S(1)} %get-tuple-element.57), channel_id=1, source_target_pairs={{0,32},{32,0},{64,96},{96,64},{128,160},{160,128},{192,224},{224,1... | collective-permute-start | bytes 122888 | tf_op jit(solution)/shard_map/ppermute | solution.py:656
  30.2 5.3 %collective-permute-start.7 = (f32[10,8,128]{2,1,0:T(8,128)S(1)}, f32[10,8,128]{2,1,0:T(8,128)S(1)}, u32[]{:S(2)}, u32[]{:S(2)}) collective-permute-start(f32[10,8,128]{2,1,0:T(8,128)S(1)} %get-tuple-element.57), channel_id=1, source_target_pairs={{0,224},{32,64},{64,32},{96,128},{128,96},{160,192},{192,160},{224... | collective-permute-start | bytes 122888 | tf_op jit(solution)/shard_map/ppermute | solution.py:656
  50.8 3.6 %collective-permute-start.10 = (f32[24,8,128]{2,1,0:T(8,128)S(1)}, f32[24,8,128]{2,1,0:T(8,128)S(1)}, u32[]{:S(2)}, u32[]{:S(2)}) collective-permute-start(f32[24,8,128]{2,1,0:T(8,128)S(1)} %all_to_all.5.own._), channel_id=1, source_target_pairs={{0,1},{1,0},{2,3},{3,2},{4,5},{5,4},{6,7},{7,6},{8,9},{9,8},{10,11... | collective-permute-start | bytes 294920 | tf_op jit(solution)/shard_map/ppermute | solution.py:656
  50.8 6.2 %collective-permute-start.11 = (f32[24,8,128]{2,1,0:T(8,128)S(1)}, f32[24,8,128]{2,1,0:T(8,128)S(1)}, u32[]{:S(2)}, u32[]{:S(2)}) collective-permute-start(f32[24,8,128]{2,1,0:T(8,128)S(1)} %all_to_all.5.own._), channel_id=1, source_target_pairs={{0,31},{1,2},{2,1},{3,4},{4,3},{5,6},{6,5},{7,8},{8,7},{9,10},{10,... | collective-permute-start | bytes 294920 | tf_op jit(solution)/shard_map/ppermute | solution.py:656
  53.3 8.1 %collective-permute-start.12 = (f32[46,8,128]{2,1,0:T(8,128)S(1)}, f32[46,8,128]{2,1,0:T(8,128)S(1)}, u32[]{:S(2)}, u32[]{:S(2)}) collective-permute-start(f32[46,8,128]{2,1,0:T(8,128)S(1)} %get-tuple-element.66), channel_id=1, source_target_pairs={{0,32},{32,0},{64,96},{96,64},{128,160},{160,128},{192,224},{224,1... | collective-permute-start | bytes 565256 | tf_op jit(solution)/shard_map/ppermute | solution.py:656
  53.9 7.4 %collective-permute-start.13 = (f32[46,8,128]{2,1,0:T(8,128)S(1)}, f32[46,8,128]{2,1,0:T(8,128)S(1)}, u32[]{:S(2)}, u32[]{:S(2)}) collective-permute-start(f32[46,8,128]{2,1,0:T(8,128)S(1)} %get-tuple-element.67), channel_id=1, source_target_pairs={{0,224},{32,64},{64,32},{96,128},{128,96},{160,192},{192,160},{224... | collective-permute-start | bytes 565256 | tf_op jit(solution)/shard_map/ppermute | solution.py:656

commit v5 on v4

--- a/solution.py
+++ b/solution.py
@@ -477,21 +477,20 @@
     ix, iy, even_x, even_y, has_right, has_left, has_above, has_below = places()
     lane, sub = iota((8, 128), 1), iota((8, 128), 0)
 
-    def put(n, x, rows, own_part, up, down):
-        up, down = only(has_above, up), only(has_below, down)
-        (f2, a2, b2)[n][x, rows : rows + 8] = jnp.where(
-            lane < 32, own_part, jnp.where(lane < 64, roll(up, 32, 1), only(lane >= 96, roll(down, 96, 1)))
-        )
-
+    high, middle, low = lane < 64, lane < 32, lane >= 96
     for d in range(8):
-        tiles = [
-            (own[3 * d + t], either(even_y, ya[3 * d + t], yb[3 * d + t]), either(even_y, yb[3 * d + t], ya[3 * d + t]))
-            for t in range(3)
-        ]
-        for n in range(3):
-            for t in range(3):
-                put(n, 2 * d + t // 2, 8 * (t % 2), *(roll(tile, -32 * n, 1) for tile in tiles[t]))
-            put(n, 2 * d + 1, 8, *(roll(tile, -96, 1) for tile in tiles[n]))
+        tiles = []
+        for t in range(3):
+            one, two = ya[3 * d + t], yb[3 * d + t]
+            tiles.append(
+                (own[3 * d + t], only(has_above, either(even_y, one, two)), only(has_below, either(even_y, two, one)))
+            )
+        for n, full in enumerate((f2, a2, b2)):
+            for t in range(4):
+                mine, up, down = tiles[n if t == 3 else t]
+                at = 96 if t == 3 else 32 * n
+                beside = jnp.where(high, roll(up, 32 - at, 1), only(low, roll(down, 96 - at, 1)))
+                full[2 * d + t // 2, 8 * (t % 2) : 8 * (t % 2) + 8] = jnp.where(middle, roll(mine, -at, 1), beside)
     b2[16] = jnp.zeros((16, 128), F32)
     b3[8] = jnp.zeros((8, 128), F32)
     level2 = Level((f2, a2, b2, ws2, wl2, wm2, inv2, diag2, u2, v2), 0.0625, False, 16)

time: 69 us -> 68.4 us (level)
  Pallas kernels: 22.6 us -> 20.5 us
  waiting for transfers between devices: 5.52 us -> 6.99 us
    pallas_call x1, Pallas kernels: 4.44 us -> 2.34 us  [body(): call(bottom_kernel, [(16, 16, 128)], level(16, 16, 128) + level(8, 8, 128...]
    ppermute x14, waiting for transfers between devices: 5.52 us -> 6.99 us  [swap(): return (lax.ppermute(a, axis, first), lax.ppermute(b, axis, second))]
  transfers between devices with their start and end apart: 14 -> 14, of which waited for: 3 -> 4; matrix products, arithmetic and copies ran while one was open for 0% -> 0% of each run, Pallas kernels for 17% -> 14%
where the time goes in v5:
time: 68.4 us; the launch traced here: 68.2 us
  starting transfers between devices  24.9 us (36%)
  Pallas kernels  20.5 us (30%)
  blocking collectives  13.1 us (19%)
  waiting for transfers between devices  6.99 us (10%)
  local copies, waits for them, and re-layouts  1.94 us (3%)
  between operations  0.79 us (1%)
    ppermute x14, starting transfers between devices, swap(): return (lax.ppermute(a, axis, first), lax.ppermute(b, axis, second))  24.9 us
    all_to_all x1, blocking collectives, body(): own = lax.all_to_all(copies, 'gx', 0, 0, tiled=True)  13.1 us
    pallas_call x1, Pallas kernels, body(): call(up_kernel, [tiles(64), tiles(64)], [(65, 16, 256)] * 2 + level(32, 1...  7.16 us
    ppermute x14, waiting for transfers between devices, swap(): return (lax.ppermute(a, axis, first), lax.ppermute(b, axis, second))  6.99 us
    pallas_call x1, Pallas kernels, body(): call(fine_down_kernel, [tiles(16), tiles(10), more, top] + [full] * 5, [t...  5.14 us
    pallas_call x1, Pallas kernels, body(): call(bottom_kernel, [(16, 16, 128)], level(16, 16, 128) + level(8, 8, 128...  2.34 us
    pallas_call x1, Pallas kernels, body(): call(middle_down_kernel, [tiles(24), full, full, more, more], [full, full...  2.19 us
    unnamed x8, local copies, waits for them, and re-layouts  1.94 us
  transfers between devices with their start and end apart: 14, of which 4 were waited for; matrix products, arithmetic and copies ran while one was open for 0% of the time, Pallas kernels for 14%

profile of v5, /device:TPU:24, one launch (start us, length us, event | category | flops | bytes accessed | tf_op | source)
XLA Modules:
  0.0 68.2 jit_solution(4231802065723249225)
XLA Ops:
  0.6 0.9 %copy-done = f32[64,8,128]{2,1,0:T(8,128)S(1)} copy-done((f32[64,8,128]{2,1,0:T(8,128)S(1)}, f32[64,8,128]{2,1,0:T(8,128)}, u32[]{:S(2)}) %copy-start) | copy-done | bytes 262168
  2.0 0.5 copy-done.2
  2.5 0.5 shard_map.51
  3.0 0.5 copy-done.3
  3.5 0.5 shard_map.52
  4.1 3.0 %collective-permute-start.1 = (f32[32,8,128]{2,1,0:T(8,128)S(1)}, f32[32,8,128]{2,1,0:T(8,128)S(1)}, u32[]{:S(2)}, u32[]{:S(2)}) collective-permute-start(f32[32,8,128]{2,1,0:T(8,128)S(1)} %get-tuple-element.48), channel_id=1, source_target_pairs={{0,31},{1,2},{2,1},{3,4},{4,3},{5,6},{6,5},{7,8},{8,7},{9,10},{10,... | collective-permute-start | bytes 393224 | tf_op jit(solution)/shard_map/ppermute | solution.py:655
  7.1 1.9 %collective-permute-start.2 = (f32[80,8,128]{2,1,0:T(8,128)S(1)}, f32[80,8,128]{2,1,0:T(8,128)S(1)}, u32[]{:S(2)}, u32[]{:S(2)}) collective-permute-start(f32[80,8,128]{2,1,0:T(8,128)S(1)} %get-tuple-element.52), channel_id=1, source_target_pairs={{0,32},{32,0},{64,96},{96,64},{128,160},{160,128},{192,224},{224,1... | collective-permute-start | bytes 983048 | tf_op jit(solution)/shard_map/ppermute | solution.py:655
  9.1 4.9 %collective-permute-start.3 = (f32[80,8,128]{2,1,0:T(8,128)S(1)}, f32[80,8,128]{2,1,0:T(8,128)S(1)}, u32[]{:S(2)}, u32[]{:S(2)}) collective-permute-start(f32[80,8,128]{2,1,0:T(8,128)S(1)} %get-tuple-element.53), channel_id=1, source_target_pairs={{0,224},{32,64},{64,32},{96,128},{128,96},{160,192},{192,160},{224... | collective-permute-start | bytes 983048 | tf_op jit(solution)/shard_map/ppermute | solution.py:655
  14.2 3.5 %collective-permute-start.5 = (f32[32,8,128]{2,1,0:T(8,128)S(1)}, f32[32,8,128]{2,1,0:T(8,128)S(1)}, u32[]{:S(2)}, u32[]{:S(2)}) collective-permute-start(f32[32,8,128]{2,1,0:T(8,128)S(1)} %get-tuple-element.55), channel_id=1, source_target_pairs={{0,224},{32,64},{64,32},{96,128},{128,96},{160,192},{192,160},{224... | collective-permute-start | bytes 393224 | tf_op jit(solution)/shard_map/ppermute | solution.py:655
  17.7 1.5 %shard_map.53 = (f32[64,8,256]{2,1,0:T(8,128)S(1)}, f32[64,8,256]{2,1,0:T(8,128)S(1)}, f32[65,8,256]{2,1,0:T(8,128)S(1)}, f32[32,8,128]{2,1,0:T(8,128)S(1)}, f32[20,8,128]{2,1,0:T(8,128)S(1)}) custom-call(f32[64,8,128]{2,1,0:T(8,128)S(1)} %copy-done.1, f32[64,8,128]{2,1,0:T(8,128)S(1)} %copy-done.2, f32[64,8,128]{2,1,0:T(8,128)S(1)} %copy-done.3, ...), custom_call_target="tpu_custom_call" | custom-call | flops 3000000000 | bytes 9000000 | tf_op jit(solution)/shard_map/pallas_call | solution.py:673
  19.3 5.7 %collective-permute-start.9 = (f32[20,8,128]{2,1,0:T(8,128)S(1)}, f32[20,8,128]{2,1,0:T(8,128)S(1)}, u32[]{:S(2)}, u32[]{:S(2)}) collective-permute-start(f32[20,8,128]{2,1,0:T(8,128)S(1)} %get-tuple-element.59), channel_id=1, source_target_pairs={{0,224},{32,64},{64,32},{96,128},{128,96},{160,192},{192,160},{224... | collective-permute-start | bytes 245768 | tf_op jit(solution)/shard_map/ppermute | solution.py:655
  25.0 5.1 %shard_map.55 = (f32[16,8,128]{2,1,0:T(8,128)S(1)}, f32[10,8,128]{2,1,0:T(8,128)S(1)}, f32[65,16,256]{2,1,0:T(8,128)S(1)}, f32[64,8,256]{2,1,0:T(8,128)S(1)}, f3...) custom-call(f32[64,8,256]{2,1,0:T(8,128)S(1)} %get-tuple-element.49., ...), custom_call_target="tpu_custom_call" | custom-call | flops 49999998976 | bytes 150000000 | tf_op jit(solution)/shard_map/pallas_call | solution.py:679
  30.2 2.0 %collective-permute-start.7 = (f32[10,8,128]{2,1,0:T(8,128)S(1)}, f32[10,8,128]{2,1,0:T(8,128)S(1)}, u32[]{:S(2)}, u32[]{:S(2)}) collective-permute-start(f32[10,8,128]{2,1,0:T(8,128)S(1)} %get-tuple-element.57), channel_id=1, source_target_pairs={{0,224},{32,64},{64,32},{96,128},{128,96},{160,192},{192,160},{224... | collective-permute-start | bytes 122888 | tf_op jit(solution)/shard_map/ppermute | solution.py:655
  32.5 1.7 %collective-permute-done.6.ga = f32[10,8,128]{2,1,0:T(8,128)S(1)} collective-permute-done((f32[10,8,128]{2,1,0:T(8,128)S(1)}, f32[10,8,128]{2,1,0:T(8,128)S(1)}, u32[]{:S(2)}, u32[]{:S(2)}) %collective-permute-start.6) | collective-permute-done | bytes 40992 | tf_op jit(solution)/shard_map/ppermute | solution.py:655
  34.2 1.3 %collective-permute-done.7.gb = f32[10,8,128]{2,1,0:T(8,128)S(1)} collective-permute-done((f32[10,8,128]{2,1,0:T(8,128)S(1)}, f32[10,8,128]{2,1,0:T(8,128)S(1)}, u32[]{:S(2)}, u32[]{:S(2)}) %collective-permute-start.7) | collective-permute-done | bytes 40992 | tf_op jit(solution)/shard_map/ppermute | solution.py:655
  35.5 2.2 %shard_map.57 = (f32[24,8,128]{2,1,0:T(8,128)S(1)}, f32[32,16,128]{2,1,0:T(8,128)S(1)}, f32[32,16,128]{2,1,0:T(8,128)S(1)}, f32[33,16,128]{2,1,0:T(8,128)S(1)}, f32[33,16,128]{2,1,0:T(8,128)S(1)}) custom-call(f32[16,8,128]{2,1,0:T(8,128)S(1)} %get-tuple-element.56.source_in, f32[10,8,128]{2,1,0:T(8,128)S(1)} %collective-permute-done.6.ga, ...), custom_call_target="tpu_custom_call" | custom-call | flops 49999998976 | bytes 150000000 | tf_op jit(solution)/shard_map/pallas_call | solution.py:690
  37.7 13.1 %all_to_all.5.own._ = f32[24,8,128]{2,1,0:T(8,128)S(1)} all-to-all(f32[24,8,128]{2,1,0:T(8,128)S(1)} %get-tuple-element.63), channel_id=1, replica_groups=mesh['gx'=8,'gy'=32] {'gx'}, dimensions={0} | all-to-all | bytes 196608 | tf_op jit(solution)/shard_map/all_to_all | solution.py:697
  50.8 2.3 %collective-permute-start.11 = (f32[24,8,128]{2,1,0:T(8,128)S(1)}, f32[24,8,128]{2,1,0:T(8,128)S(1)}, u32[]{:S(2)}, u32[]{:S(2)}) collective-permute-start(f32[24,8,128]{2,1,0:T(8,128)S(1)} %all_to_all.5.own._), channel_id=1, source_target_pairs={{0,31},{1,2},{2,1},{3,4},{4,3},{5,6},{6,5},{7,8},{8,7},{9,10},{10,... | collective-permute-start | bytes 294920 | tf_op jit(solution)/shard_map/ppermute | solution.py:655
  53.3 0.7 collective-permute-start.12
  53.9 0.4 collective-permute-start.13
  54.4 2.5 %collective-permute-done.11.yb = f32[24,8,128]{2,1,0:T(8,128)S(1)} collective-permute-done((f32[24,8,128]{2,1,0:T(8,128)S(1)}, f32[24,8,128]{2,1,0:T(8,128)S(1)}, u32[]{:S(2)}, u32[]{:S(2)}) %collective-permute-start.11) | collective-permute-done | bytes 98336 | tf_op jit(solution)/shard_map/ppermute | solution.py:655
  56.9 2.3 %shard_map.58.v2 = f32[16,16,128]{2,1,0:T(8,128)S(1)} custom-call(f32[24,8,128]{2,1,0:T(8,128)S(1)} %all_to_all.5.own._, f32[24,8,128]{2,1,0:T(8,128)S(1)} %collective-permute-done.10.ya, f32[24,8,128]{2,1,0:T(8,128)S(1)} %collective-permute-done.11.yb), custom_call_target="tpu_custom_call" | custom-call | flops 49999998976 | bytes 150000000 | tf_op jit(solution)/shard_map/pallas_call | solution.py:707
  59.3 1.5 %collective-permute-done.13.xb = f32[46,8,128]{2,1,0:T(8,128)S(1)} collective-permute-done((f32[46,8,128]{2,1,0:T(8,128)S(1)}, f32[46,8,128]{2,1,0:T(8,128)S(1)}, u32[]{:S(2)}, u32[]{:S(2)}) %collective-permute-start.13) | collective-permute-done | bytes 188448 | tf_op jit(solution)/shard_map/ppermute | solution.py:655
  61.0 7.2 %shard_map.61 = (f32[64,8,128]{2,1,0:T(8,128)}, f32[64,8,128]{2,1,0:T(8,128)}) custom-call(f32[16,16,128]{2,1,0:T(8,128)S(1)} %shard_map.58.v2, f32[46,8,128]{2,1,0:T(8,128)S(1)} %collective-permute-done.12.xa, f32[46,8,128]{2,1,0:T(8,128)S(1)} %collective-permute-done.13.xb, f32[32,16,128]{2,1,0:T(8,128)S(1)} %get-tuple-element.68.f1, ...), custom_call_target="tpu_custom_call" | custom-call | flops 1000000000 | bytes 3000000 | tf_op jit(solution)/shard_map/pallas_call | solution.py:715
  (25 shorter events, 1.7 us)
Async XLA Ops:
  0.6 1.0 %copy-start = (f32[64,8,128]{2,1,0:T(8,128)S(1)}, f32[64,8,128]{2,1,0:T(8,128)}, u32[]{:S(2)}) copy-start(f32[64,8,128]{2,1,0:T(8,128)} %f.1) | copy-start | bytes 786436
  1.6 0.9 %copy-start.2 = (f32[64,8,128]{2,1,0:T(8,128)S(1)}, f32[64,8,128]{2,1,0:T(8,128)}, u32[]{:S(2)}) copy-start(f32[64,8,128]{2,1,0:T(8,128)} %a.1) | copy-start | bytes 786436
  2.5 0.9 %copy-start.3 = (f32[64,8,128]{2,1,0:T(8,128)S(1)}, f32[64,8,128]{2,1,0:T(8,128)}, u32[]{:S(2)}) copy-start(f32[64,8,128]{2,1,0:T(8,128)} %b.1) | copy-start | bytes 786436
  4.0 10.0 %collective-permute-start = (f32[32,8,128]{2,1,0:T(8,128)S(1)}, f32[32,8,128]{2,1,0:T(8,128)S(1)}, u32[]{:S(2)}, u32[]{:S(2)}) collective-permute-start(f32[32,8,128]{2,1,0:T(8,128)S(1)} %get-tuple-element.47), channel_id=1, source_target_pairs={{0,1},{1,0},{2,3},{3,2},{4,5},{5,4},{6,7},{7,6},{8,9},{9,8},{10,11... | collective-permute-start | bytes 393224 | tf_op jit(solution)/shard_map/ppermute | solution.py:655
  4.1 9.9 %collective-permute-start.1 = (f32[32,8,128]{2,1,0:T(8,128)S(1)}, f32[32,8,128]{2,1,0:T(8,128)S(1)}, u32[]{:S(2)}, u32[]{:S(2)}) collective-permute-start(f32[32,8,128]{2,1,0:T(8,128)S(1)} %get-tuple-element.48), channel_id=1, source_target_pairs={{0,31},{1,2},{2,1},{3,4},{4,3},{5,6},{6,5},{7,8},{8,7},{9,10},{10,... | collective-permute-start | bytes 393224 | tf_op jit(solution)/shard_map/ppermute | solution.py:655
  7.1 17.8 %collective-permute-start.2 = (f32[80,8,128]{2,1,0:T(8,128)S(1)}, f32[80,8,128]{2,1,0:T(8,128)S(1)}, u32[]{:S(2)}, u32[]{:S(2)}) collective-permute-start(f32[80,8,128]{2,1,0:T(8,128)S(1)} %get-tuple-element.52), channel_id=1, source_target_pairs={{0,32},{32,0},{64,96},{96,64},{128,160},{160,128},{192,224},{224,1... | collective-permute-start | bytes 983048 | tf_op jit(solution)/shard_map/ppermute | solution.py:655
  9.0 8.7 %copy-start.1 = (f32[64,8,128]{2,1,0:T(8,128)S(1)}, f32[64,8,128]{2,1,0:T(8,128)}, u32[]{:S(2)}) copy-start(f32[64,8,128]{2,1,0:T(8,128)} %f.1) | copy-start | bytes 786436
  9.1 15.9 %collective-permute-start.3 = (f32[80,8,128]{2,1,0:T(8,128)S(1)}, f32[80,8,128]{2,1,0:T(8,128)S(1)}, u32[]{:S(2)}, u32[]{:S(2)}) collective-permute-start(f32[80,8,128]{2,1,0:T(8,128)S(1)} %get-tuple-element.53), channel_id=1, source_target_pairs={{0,224},{32,64},{64,32},{96,128},{128,96},{160,192},{192,160},{224... | collective-permute-start | bytes 983048 | tf_op jit(solution)/shard_map/ppermute | solution.py:655
  14.1 5.2 %collective-permute-start.4 = (f32[32,8,128]{2,1,0:T(8,128)S(1)}, f32[32,8,128]{2,1,0:T(8,128)S(1)}, u32[]{:S(2)}, u32[]{:S(2)}) collective-permute-start(f32[32,8,128]{2,1,0:T(8,128)S(1)} %get-tuple-element.54), channel_id=1, source_target_pairs={{0,32},{32,0},{64,96},{96,64},{128,160},{160,128},{192,224},{224,1... | collective-permute-start | bytes 393224 | tf_op jit(solution)/shard_map/ppermute | solution.py:655
  14.2 10.8 %collective-permute-start.5 = (f32[32,8,128]{2,1,0:T(8,128)S(1)}, f32[32,8,128]{2,1,0:T(8,128)S(1)}, u32[]{:S(2)}, u32[]{:S(2)}) collective-permute-start(f32[32,8,128]{2,1,0:T(8,128)S(1)} %get-tuple-element.55), channel_id=1, source_target_pairs={{0,224},{32,64},{64,32},{96,128},{128,96},{160,192},{192,160},{224... | collective-permute-start | bytes 393224 | tf_op jit(solution)/shard_map/ppermute | solution.py:655
  19.2 13.3 %collective-permute-start.8 = (f32[20,8,128]{2,1,0:T(8,128)S(1)}, f32[20,8,128]{2,1,0:T(8,128)S(1)}, u32[]{:S(2)}, u32[]{:S(2)}) collective-permute-start(f32[20,8,128]{2,1,0:T(8,128)S(1)} %get-tuple-element.59), channel_id=1, source_target_pairs={{0,32},{32,0},{64,96},{96,64},{128,160},{160,128},{192,224},{224,1... | collective-permute-start | bytes 245768 | tf_op jit(solution)/shard_map/ppermute | solution.py:655
  19.3 13.2 %collective-permute-start.9 = (f32[20,8,128]{2,1,0:T(8,128)S(1)}, f32[20,8,128]{2,1,0:T(8,128)S(1)}, u32[]{:S(2)}, u32[]{:S(2)}) collective-permute-start(f32[20,8,128]{2,1,0:T(8,128)S(1)} %get-tuple-element.59), channel_id=1, source_target_pairs={{0,224},{32,64},{64,32},{96,128},{128,96},{160,192},{192,160},{224... | collective-permute-start | bytes 245768 | tf_op jit(solution)/shard_map/ppermute | solution.py:655
  30.1 4.1 %collective-permute-start.6 = (f32[10,8,128]{2,1,0:T(8,128)S(1)}, f32[10,8,128]{2,1,0:T(8,128)S(1)}, u32[]{:S(2)}, u32[]{:S(2)}) collective-permute-start(f32[10,8,128]{2,1,0:T(8,128)S(1)} %get-tuple-element.57), channel_id=1, source_target_pairs={{0,32},{32,0},{64,96},{96,64},{128,160},{160,128},{192,224},{224,1... | collective-permute-start | bytes 122888 | tf_op jit(solution)/shard_map/ppermute | solution.py:655
  30.2 5.3 %collective-permute-start.7 = (f32[10,8,128]{2,1,0:T(8,128)S(1)}, f32[10,8,128]{2,1,0:T(8,128)S(1)}, u32[]{:S(2)}, u32[]{:S(2)}) collective-permute-start(f32[10,8,128]{2,1,0:T(8,128)S(1)} %get-tuple-element.57), channel_id=1, source_target_pairs={{0,224},{32,64},{64,32},{96,128},{128,96},{160,192},{192,160},{224... | collective-permute-start | bytes 122888 | tf_op jit(solution)/shard_map/ppermute | solution.py:655
  50.8 3.6 %collective-permute-start.10 = (f32[24,8,128]{2,1,0:T(8,128)S(1)}, f32[24,8,128]{2,1,0:T(8,128)S(1)}, u32[]{:S(2)}, u32[]{:S(2)}) collective-permute-start(f32[24,8,128]{2,1,0:T(8,128)S(1)} %all_to_all.5.own._), channel_id=1, source_target_pairs={{0,1},{1,0},{2,3},{3,2},{4,5},{5,4},{6,7},{7,6},{8,9},{9,8},{10,11... | collective-permute-start | bytes 294920 | tf_op jit(solution)/shard_map/ppermute | solution.py:655
  50.8 6.2 %collective-permute-start.11 = (f32[24,8,128]{2,1,0:T(8,128)S(1)}, f32[24,8,128]{2,1,0:T(8,128)S(1)}, u32[]{:S(2)}, u32[]{:S(2)}) collective-permute-start(f32[24,8,128]{2,1,0:T(8,128)S(1)} %all_to_all.5.own._), channel_id=1, source_target_pairs={{0,31},{1,2},{2,1},{3,4},{4,3},{5,6},{6,5},{7,8},{8,7},{9,10},{10,... | collective-permute-start | bytes 294920 | tf_op jit(solution)/shard_map/ppermute | solution.py:655
  53.3 6.0 %collective-permute-start.12 = (f32[46,8,128]{2,1,0:T(8,128)S(1)}, f32[46,8,128]{2,1,0:T(8,128)S(1)}, u32[]{:S(2)}, u32[]{:S(2)}) collective-permute-start(f32[46,8,128]{2,1,0:T(8,128)S(1)} %get-tuple-element.66), channel_id=1, source_target_pairs={{0,32},{32,0},{64,96},{96,64},{128,160},{160,128},{192,224},{224,1... | collective-permute-start | bytes 565256 | tf_op jit(solution)/shard_map/ppermute | solution.py:655
  53.9 6.8 %collective-permute-start.13 = (f32[46,8,128]{2,1,0:T(8,128)S(1)}, f32[46,8,128]{2,1,0:T(8,128)S(1)}, u32[]{:S(2)}, u32[]{:S(2)}) collective-permute-start(f32[46,8,128]{2,1,0:T(8,128)S(1)} %get-tuple-element.67), channel_id=1, source_target_pairs={{0,224},{32,64},{64,32},{96,128},{128,96},{160,192},{192,160},{224... | collective-permute-start | bytes 565256 | tf_op jit(solution)/shard_map/ppermute | solution.py:655

commit v6 on v5

--- a/solution.py
+++ b/solution.py
@@ -340,7 +340,7 @@
                     full[z, :, 128:256] = spread_columns(lane, up, down, 64 * h + YH * n)
         return carry
 
-    lax.fori_loop(0, 8, unpack, 0, unroll=2)
+    lax.fori_loop(0, 8, unpack, 0, unroll=4)
     bx[64] = jnp.zeros((8, 256), F32)
     level = Level((Rows(f, fx), Rows(a, ax), Rows(b, bx), ws, wl, wm, inv, diag, u, v), 1.0, True, 16)
     level.build(WEIGHTS[0])
@@ -612,7 +612,7 @@
                 u0[m] = u0_in[m] + only(inv0[m] > 0.0, rows)
         return carry
 
-    lax.fori_loop(0, 8, correct_0, 0, unroll=4)
+    lax.fori_loop(0, 8, correct_0, 0, unroll=8)
     level0 = Level((Rows(f0, f0x), None, u0, ws0, wl0, wm0, inv0, diag0, u0, v0), 1.0, True, 16)
     u0[64] = jnp.zeros((16, 256), F32)
     v0[64] = jnp.zeros((16, 256), F32)

time: 68.4 us -> 68.1 us (level)
  no operation moved by 1% of the time
where the time goes in v6:
time: 68.1 us; the launch traced here: 67.9 us
  starting transfers between devices  24.9 us (37%)
  Pallas kernels  20.3 us (30%)
  blocking collectives  13.1 us (19%)
  waiting for transfers between devices  6.99 us (10%)
  local copies, waits for them, and re-layouts  1.94 us (3%)
  between operations  0.79 us (1%)
    ppermute x14, starting transfers between devices, swap(): return (lax.ppermute(a, axis, first), lax.ppermute(b, axis, second))  24.9 us
    all_to_all x1, blocking collectives, body(): own = lax.all_to_all(copies, 'gx', 0, 0, tiled=True)  13.1 us
    pallas_call x1, Pallas kernels, body(): call(up_kernel, [tiles(64), tiles(64)], [(65, 16, 256)] * 2 + level(32, 1...  7.05 us
    ppermute x14, waiting for transfers between devices, swap(): return (lax.ppermute(a, axis, first), lax.ppermute(b, axis, second))  6.99 us
    pallas_call x1, Pallas kernels, body(): call(fine_down_kernel, [tiles(16), tiles(10), more, top] + [full] * 5, [t...  5 us
    pallas_call x1, Pallas kernels, body(): call(bottom_kernel, [(16, 16, 128)], level(16, 16, 128) + level(8, 8, 128...  2.33 us
    pallas_call x1, Pallas kernels, body(): call(middle_down_kernel, [tiles(24), full, full, more, more], [full, full...  2.19 us
    unnamed x8, local copies, waits for them, and re-layouts  1.94 us
  transfers between devices with their start and end apart: 14, of which 4 were waited for; matrix products, arithmetic and copies ran while one was open for 0% of the time, Pallas kernels for 14%

profile of v6, /device:TPU:24, one launch (start us, length us, event | category | flops | bytes accessed | tf_op | source)
XLA Modules:
  0.0 67.9 jit_solution(2140244208353756672)
XLA Ops:
  0.6 0.9 %copy-done = f32[64,8,128]{2,1,0:T(8,128)S(1)} copy-done((f32[64,8,128]{2,1,0:T(8,128)S(1)}, f32[64,8,128]{2,1,0:T(8,128)}, u32[]{:S(2)}) %copy-start) | copy-done | bytes 262168
  2.0 0.5 copy-done.2
  2.5 0.5 shard_map.51
  3.0 0.5 copy-done.3
  3.5 0.5 shard_map.52
  4.1 3.0 %collective-permute-start.1 = (f32[32,8,128]{2,1,0:T(8,128)S(1)}, f32[32,8,128]{2,1,0:T(8,128)S(1)}, u32[]{:S(2)}, u32[]{:S(2)}) collective-permute-start(f32[32,8,128]{2,1,0:T(8,128)S(1)} %get-tuple-element.48), channel_id=1, source_target_pairs={{0,31},{1,2},{2,1},{3,4},{4,3},{5,6},{6,5},{7,8},{8,7},{9,10},{10,... | collective-permute-start | bytes 393224 | tf_op jit(solution)/shard_map/ppermute | solution.py:655
  7.1 1.9 %collective-permute-start.2 = (f32[80,8,128]{2,1,0:T(8,128)S(1)}, f32[80,8,128]{2,1,0:T(8,128)S(1)}, u32[]{:S(2)}, u32[]{:S(2)}) collective-permute-start(f32[80,8,128]{2,1,0:T(8,128)S(1)} %get-tuple-element.52), channel_id=1, source_target_pairs={{0,32},{32,0},{64,96},{96,64},{128,160},{160,128},{192,224},{224,1... | collective-permute-start | bytes 983048 | tf_op jit(solution)/shard_map/ppermute | solution.py:655
  9.1 4.9 %collective-permute-start.3 = (f32[80,8,128]{2,1,0:T(8,128)S(1)}, f32[80,8,128]{2,1,0:T(8,128)S(1)}, u32[]{:S(2)}, u32[]{:S(2)}) collective-permute-start(f32[80,8,128]{2,1,0:T(8,128)S(1)} %get-tuple-element.53), channel_id=1, source_target_pairs={{0,224},{32,64},{64,32},{96,128},{128,96},{160,192},{192,160},{224... | collective-permute-start | bytes 983048 | tf_op jit(solution)/shard_map/ppermute | solution.py:655
  14.2 3.5 %collective-permute-start.5 = (f32[32,8,128]{2,1,0:T(8,128)S(1)}, f32[32,8,128]{2,1,0:T(8,128)S(1)}, u32[]{:S(2)}, u32[]{:S(2)}) collective-permute-start(f32[32,8,128]{2,1,0:T(8,128)S(1)} %get-tuple-element.55), channel_id=1, source_target_pairs={{0,224},{32,64},{64,32},{96,128},{128,96},{160,192},{192,160},{224... | collective-permute-start | bytes 393224 | tf_op jit(solution)/shard_map/ppermute | solution.py:655
  17.7 1.5 %shard_map.53 = (f32[64,8,256]{2,1,0:T(8,128)S(1)}, f32[64,8,256]{2,1,0:T(8,128)S(1)}, f32[65,8,256]{2,1,0:T(8,128)S(1)}, f32[32,8,128]{2,1,0:T(8,128)S(1)}, f32[20,8,128]{2,1,0:T(8,128)S(1)}) custom-call(f32[64,8,128]{2,1,0:T(8,128)S(1)} %copy-done.1, f32[64,8,128]{2,1,0:T(8,128)S(1)} %copy-done.2, f32[64,8,128]{2,1,0:T(8,128)S(1)} %copy-done.3, ...), custom_call_target="tpu_custom_call" | custom-call | flops 3000000000 | bytes 9000000 | tf_op jit(solution)/shard_map/pallas_call | solution.py:673
  19.3 5.7 %collective-permute-start.9 = (f32[20,8,128]{2,1,0:T(8,128)S(1)}, f32[20,8,128]{2,1,0:T(8,128)S(1)}, u32[]{:S(2)}, u32[]{:S(2)}) collective-permute-start(f32[20,8,128]{2,1,0:T(8,128)S(1)} %get-tuple-element.59), channel_id=1, source_target_pairs={{0,224},{32,64},{64,32},{96,128},{128,96},{160,192},{192,160},{224... | collective-permute-start | bytes 245768 | tf_op jit(solution)/shard_map/ppermute | solution.py:655
  25.0 5.0 %shard_map.55 = (f32[16,8,128]{2,1,0:T(8,128)S(1)}, f32[10,8,128]{2,1,0:T(8,128)S(1)}, f32[65,16,256]{2,1,0:T(8,128)S(1)}, f32[64,8,256]{2,1,0:T(8,128)S(1)}, f3...) custom-call(f32[64,8,256]{2,1,0:T(8,128)S(1)} %get-tuple-element.49., ...), custom_call_target="tpu_custom_call" | custom-call | flops 49999998976 | bytes 150000000 | tf_op jit(solution)/shard_map/pallas_call | solution.py:679
  30.1 2.0 %collective-permute-start.7 = (f32[10,8,128]{2,1,0:T(8,128)S(1)}, f32[10,8,128]{2,1,0:T(8,128)S(1)}, u32[]{:S(2)}, u32[]{:S(2)}) collective-permute-start(f32[10,8,128]{2,1,0:T(8,128)S(1)} %get-tuple-element.57), channel_id=1, source_target_pairs={{0,224},{32,64},{64,32},{96,128},{128,96},{160,192},{192,160},{224... | collective-permute-start | bytes 122888 | tf_op jit(solution)/shard_map/ppermute | solution.py:655
  32.4 1.7 %collective-permute-done.6.ga = f32[10,8,128]{2,1,0:T(8,128)S(1)} collective-permute-done((f32[10,8,128]{2,1,0:T(8,128)S(1)}, f32[10,8,128]{2,1,0:T(8,128)S(1)}, u32[]{:S(2)}, u32[]{:S(2)}) %collective-permute-start.6) | collective-permute-done | bytes 40992 | tf_op jit(solution)/shard_map/ppermute | solution.py:655
  34.1 1.3 %collective-permute-done.7.gb = f32[10,8,128]{2,1,0:T(8,128)S(1)} collective-permute-done((f32[10,8,128]{2,1,0:T(8,128)S(1)}, f32[10,8,128]{2,1,0:T(8,128)S(1)}, u32[]{:S(2)}, u32[]{:S(2)}) %collective-permute-start.7) | collective-permute-done | bytes 40992 | tf_op jit(solution)/shard_map/ppermute | solution.py:655
  35.4 2.2 %shard_map.57 = (f32[24,8,128]{2,1,0:T(8,128)S(1)}, f32[32,16,128]{2,1,0:T(8,128)S(1)}, f32[32,16,128]{2,1,0:T(8,128)S(1)}, f32[33,16,128]{2,1,0:T(8,128)S(1)}, f32[33,16,128]{2,1,0:T(8,128)S(1)}) custom-call(f32[16,8,128]{2,1,0:T(8,128)S(1)} %get-tuple-element.56.source_in, f32[10,8,128]{2,1,0:T(8,128)S(1)} %collective-permute-done.6.ga, ...), custom_call_target="tpu_custom_call" | custom-call | flops 49999998976 | bytes 150000000 | tf_op jit(solution)/shard_map/pallas_call | solution.py:690
  37.6 13.1 %all_to_all.5.own._ = f32[24,8,128]{2,1,0:T(8,128)S(1)} all-to-all(f32[24,8,128]{2,1,0:T(8,128)S(1)} %get-tuple-element.63), channel_id=1, replica_groups=mesh['gx'=8,'gy'=32] {'gx'}, dimensions={0} | all-to-all | bytes 196608 | tf_op jit(solution)/shard_map/all_to_all | solution.py:697
  50.6 2.3 %collective-permute-start.11 = (f32[24,8,128]{2,1,0:T(8,128)S(1)}, f32[24,8,128]{2,1,0:T(8,128)S(1)}, u32[]{:S(2)}, u32[]{:S(2)}) collective-permute-start(f32[24,8,128]{2,1,0:T(8,128)S(1)} %all_to_all.5.own._), channel_id=1, source_target_pairs={{0,31},{1,2},{2,1},{3,4},{4,3},{5,6},{6,5},{7,8},{8,7},{9,10},{10,... | collective-permute-start | bytes 294920 | tf_op jit(solution)/shard_map/ppermute | solution.py:655
  53.2 0.7 collective-permute-start.12
  53.8 0.4 collective-permute-start.13
  54.3 2.5 %collective-permute-done.11.yb = f32[24,8,128]{2,1,0:T(8,128)S(1)} collective-permute-done((f32[24,8,128]{2,1,0:T(8,128)S(1)}, f32[24,8,128]{2,1,0:T(8,128)S(1)}, u32[]{:S(2)}, u32[]{:S(2)}) %collective-permute-start.11) | collective-permute-done | bytes 98336 | tf_op jit(solution)/shard_map/ppermute | solution.py:655
  56.8 2.3 %shard_map.58.v2 = f32[16,16,128]{2,1,0:T(8,128)S(1)} custom-call(f32[24,8,128]{2,1,0:T(8,128)S(1)} %all_to_all.5.own._, f32[24,8,128]{2,1,0:T(8,128)S(1)} %collective-permute-done.10.ya, f32[24,8,128]{2,1,0:T(8,128)S(1)} %collective-permute-done.11.yb), custom_call_target="tpu_custom_call" | custom-call | flops 49999998976 | bytes 150000000 | tf_op jit(solution)/shard_map/pallas_call | solution.py:707
  59.1 1.5 %collective-permute-done.13.xb = f32[46,8,128]{2,1,0:T(8,128)S(1)} collective-permute-done((f32[46,8,128]{2,1,0:T(8,128)S(1)}, f32[46,8,128]{2,1,0:T(8,128)S(1)}, u32[]{:S(2)}, u32[]{:S(2)}) %collective-permute-start.13) | collective-permute-done | bytes 188448 | tf_op jit(solution)/shard_map/ppermute | solution.py:655
  60.9 7.0 %shard_map.61 = (f32[64,8,128]{2,1,0:T(8,128)}, f32[64,8,128]{2,1,0:T(8,128)}) custom-call(f32[16,16,128]{2,1,0:T(8,128)S(1)} %shard_map.58.v2, f32[46,8,128]{2,1,0:T(8,128)S(1)} %collective-permute-done.12.xa, f32[46,8,128]{2,1,0:T(8,128)S(1)} %collective-permute-done.13.xb, f32[32,16,128]{2,1,0:T(8,128)S(1)} %get-tuple-element.68.f1, ...), custom_call_target="tpu_custom_call" | custom-call | flops 1000000000 | bytes 3000000 | tf_op jit(solution)/shard_map/pallas_call | solution.py:715
  (25 shorter events, 1.7 us)
Async XLA Ops:
  0.6 1.0 %copy-start = (f32[64,8,128]{2,1,0:T(8,128)S(1)}, f32[64,8,128]{2,1,0:T(8,128)}, u32[]{:S(2)}) copy-start(f32[64,8,128]{2,1,0:T(8,128)} %f.1) | copy-start | bytes 786436
  1.6 0.9 %copy-start.2 = (f32[64,8,128]{2,1,0:T(8,128)S(1)}, f32[64,8,128]{2,1,0:T(8,128)}, u32[]{:S(2)}) copy-start(f32[64,8,128]{2,1,0:T(8,128)} %a.1) | copy-start | bytes 786436
  2.5 0.9 %copy-start.3 = (f32[64,8,128]{2,1,0:T(8,128)S(1)}, f32[64,8,128]{2,1,0:T(8,128)}, u32[]{:S(2)}) copy-start(f32[64,8,128]{2,1,0:T(8,128)} %b.1) | copy-start | bytes 786436
  4.0 10.0 %collective-permute-start = (f32[32,8,128]{2,1,0:T(8,128)S(1)}, f32[32,8,128]{2,1,0:T(8,128)S(1)}, u32[]{:S(2)}, u32[]{:S(2)}) collective-permute-start(f32[32,8,128]{2,1,0:T(8,128)S(1)} %get-tuple-element.47), channel_id=1, source_target_pairs={{0,1},{1,0},{2,3},{3,2},{4,5},{5,4},{6,7},{7,6},{8,9},{9,8},{10,11... | collective-permute-start | bytes 393224 | tf_op jit(solution)/shard_map/ppermute | solution.py:655
  4.1 9.9 %collective-permute-start.1 = (f32[32,8,128]{2,1,0:T(8,128)S(1)}, f32[32,8,128]{2,1,0:T(8,128)S(1)}, u32[]{:S(2)}, u32[]{:S(2)}) collective-permute-start(f32[32,8,128]{2,1,0:T(8,128)S(1)} %get-tuple-element.48), channel_id=1, source_target_pairs={{0,31},{1,2},{2,1},{3,4},{4,3},{5,6},{6,5},{7,8},{8,7},{9,10},{10,... | collective-permute-start | bytes 393224 | tf_op jit(solution)/shard_map/ppermute | solution.py:655
  7.1 17.8 %collective-permute-start.2 = (f32[80,8,128]{2,1,0:T(8,128)S(1)}, f32[80,8,128]{2,1,0:T(8,128)S(1)}, u32[]{:S(2)}, u32[]{:S(2)}) collective-permute-start(f32[80,8,128]{2,1,0:T(8,128)S(1)} %get-tuple-element.52), channel_id=1, source_target_pairs={{0,32},{32,0},{64,96},{96,64},{128,160},{160,128},{192,224},{224,1... | collective-permute-start | bytes 983048 | tf_op jit(solution)/shard_map/ppermute | solution.py:655
  9.0 8.7 %copy-start.1 = (f32[64,8,128]{2,1,0:T(8,128)S(1)}, f32[64,8,128]{2,1,0:T(8,128)}, u32[]{:S(2)}) copy-start(f32[64,8,128]{2,1,0:T(8,128)} %f.1) | copy-start | bytes 786436
  9.1 15.9 %collective-permute-start.3 = (f32[80,8,128]{2,1,0:T(8,128)S(1)}, f32[80,8,128]{2,1,0:T(8,128)S(1)}, u32[]{:S(2)}, u32[]{:S(2)}) collective-permute-start(f32[80,8,128]{2,1,0:T(8,128)S(1)} %get-tuple-element.53), channel_id=1, source_target_pairs={{0,224},{32,64},{64,32},{96,128},{128,96},{160,192},{192,160},{224... | collective-permute-start | bytes 983048 | tf_op jit(solution)/shard_map/ppermute | solution.py:655
  14.1 5.2 %collective-permute-start.4 = (f32[32,8,128]{2,1,0:T(8,128)S(1)}, f32[32,8,128]{2,1,0:T(8,128)S(1)}, u32[]{:S(2)}, u32[]{:S(2)}) collective-permute-start(f32[32,8,128]{2,1,0:T(8,128)S(1)} %get-tuple-element.54), channel_id=1, source_target_pairs={{0,32},{32,0},{64,96},{96,64},{128,160},{160,128},{192,224},{224,1... | collective-permute-start | bytes 393224 | tf_op jit(solution)/shard_map/ppermute | solution.py:655
  14.2 10.8 %collective-permute-start.5 = (f32[32,8,128]{2,1,0:T(8,128)S(1)}, f32[32,8,128]{2,1,0:T(8,128)S(1)}, u32[]{:S(2)}, u32[]{:S(2)}) collective-permute-start(f32[32,8,128]{2,1,0:T(8,128)S(1)} %get-tuple-element.55), channel_id=1, source_target_pairs={{0,224},{32,64},{64,32},{96,128},{128,96},{160,192},{192,160},{224... | collective-permute-start | bytes 393224 | tf_op jit(solution)/shard_map/ppermute | solution.py:655
  19.2 13.2 %collective-permute-start.8 = (f32[20,8,128]{2,1,0:T(8,128)S(1)}, f32[20,8,128]{2,1,0:T(8,128)S(1)}, u32[]{:S(2)}, u32[]{:S(2)}) collective-permute-start(f32[20,8,128]{2,1,0:T(8,128)S(1)} %get-tuple-element.59), channel_id=1, source_target_pairs={{0,32},{32,0},{64,96},{96,64},{128,160},{160,128},{192,224},{224,1... | collective-permute-start | bytes 245768 | tf_op jit(solution)/shard_map/ppermute | solution.py:655
  19.3 13.1 %collective-permute-start.9 = (f32[20,8,128]{2,1,0:T(8,128)S(1)}, f32[20,8,128]{2,1,0:T(8,128)S(1)}, u32[]{:S(2)}, u32[]{:S(2)}) collective-permute-start(f32[20,8,128]{2,1,0:T(8,128)S(1)} %get-tuple-element.59), channel_id=1, source_target_pairs={{0,224},{32,64},{64,32},{96,128},{128,96},{160,192},{192,160},{224... | collective-permute-start | bytes 245768 | tf_op jit(solution)/shard_map/ppermute | solution.py:655
  30.0 4.1 %collective-permute-start.6 = (f32[10,8,128]{2,1,0:T(8,128)S(1)}, f32[10,8,128]{2,1,0:T(8,128)S(1)}, u32[]{:S(2)}, u32[]{:S(2)}) collective-permute-start(f32[10,8,128]{2,1,0:T(8,128)S(1)} %get-tuple-element.57), channel_id=1, source_target_pairs={{0,32},{32,0},{64,96},{96,64},{128,160},{160,128},{192,224},{224,1... | collective-permute-start | bytes 122888 | tf_op jit(solution)/shard_map/ppermute | solution.py:655
  30.1 5.3 %collective-permute-start.7 = (f32[10,8,128]{2,1,0:T(8,128)S(1)}, f32[10,8,128]{2,1,0:T(8,128)S(1)}, u32[]{:S(2)}, u32[]{:S(2)}) collective-permute-start(f32[10,8,128]{2,1,0:T(8,128)S(1)} %get-tuple-element.57), channel_id=1, source_target_pairs={{0,224},{32,64},{64,32},{96,128},{128,96},{160,192},{192,160},{224... | collective-permute-start | bytes 122888 | tf_op jit(solution)/shard_map/ppermute | solution.py:655
  50.6 3.6 %collective-permute-start.10 = (f32[24,8,128]{2,1,0:T(8,128)S(1)}, f32[24,8,128]{2,1,0:T(8,128)S(1)}, u32[]{:S(2)}, u32[]{:S(2)}) collective-permute-start(f32[24,8,128]{2,1,0:T(8,128)S(1)} %all_to_all.5.own._), channel_id=1, source_target_pairs={{0,1},{1,0},{2,3},{3,2},{4,5},{5,4},{6,7},{7,6},{8,9},{9,8},{10,11... | collective-permute-start | bytes 294920 | tf_op jit(solution)/shard_map/ppermute | solution.py:655
  50.6 6.2 %collective-permute-start.11 = (f32[24,8,128]{2,1,0:T(8,128)S(1)}, f32[24,8,128]{2,1,0:T(8,128)S(1)}, u32[]{:S(2)}, u32[]{:S(2)}) collective-permute-start(f32[24,8,128]{2,1,0:T(8,128)S(1)} %all_to_all.5.own._), channel_id=1, source_target_pairs={{0,31},{1,2},{2,1},{3,4},{4,3},{5,6},{6,5},{7,8},{8,7},{9,10},{10,... | collective-permute-start | bytes 294920 | tf_op jit(solution)/shard_map/ppermute | solution.py:655
  53.2 6.0 %collective-permute-start.12 = (f32[46,8,128]{2,1,0:T(8,128)S(1)}, f32[46,8,128]{2,1,0:T(8,128)S(1)}, u32[]{:S(2)}, u32[]{:S(2)}) collective-permute-start(f32[46,8,128]{2,1,0:T(8,128)S(1)} %get-tuple-element.66), channel_id=1, source_target_pairs={{0,32},{32,0},{64,96},{96,64},{128,160},{160,128},{192,224},{224,1... | collective-permute-start | bytes 565256 | tf_op jit(solution)/shard_map/ppermute | solution.py:655
  53.8 6.8 %collective-permute-start.13 = (f32[46,8,128]{2,1,0:T(8,128)S(1)}, f32[46,8,128]{2,1,0:T(8,128)S(1)}, u32[]{:S(2)}, u32[]{:S(2)}) collective-permute-start(f32[46,8,128]{2,1,0:T(8,128)S(1)} %get-tuple-element.67), channel_id=1, source_target_pairs={{0,224},{32,64},{64,32},{96,128},{128,96},{160,192},{192,160},{224... | collective-permute-start | bytes 565256 | tf_op jit(solution)/shard_map/ppermute | solution.py:655

commit v7 on v6

--- a/solution.py
+++ b/solution.py
@@ -205,7 +205,7 @@
             out[z] = jnp.where(here, value, before[old][z]) if before else only(here, value)
         return carry
 
-    lax.fori_loop(0, 32, y_step, 0, unroll=8)
+    lax.fori_loop(0, 32, y_step, 0, unroll=16)
 
     def x_step(q, carry):
         extra_low = extra_high = jnp.zeros((8, 128), F32)
@@ -224,7 +224,7 @@
             xb[64 + q] = either(even_x, extra_low, extra_high)
         return carry
 
-    lax.fori_loop(0, 16, x_step, 0, unroll=4)
+    lax.fori_loop(0, 16, x_step, 0, unroll=8)
 
 
 def corner_kernel(ya, yb, ca, cb):

time: 68.1 us -> 68 us (level)
  no operation moved by 1% of the time
where the time goes in v7:
time: 68 us; the launch traced here: 67.8 us
  starting transfers between devices  24.9 us (37%)
  Pallas kernels  19.8 us (29%)
  blocking collectives  13.1 us (19%)
  waiting for transfers between devices  6.99 us (10%)
  local copies, waits for them, and re-layouts  2.23 us (3%)
  between operations  0.79 us (1%)
    ppermute x14, starting transfers between devices, swap(): return (lax.ppermute(a, axis, first), lax.ppermute(b, axis, second))  24.9 us
    all_to_all x1, blocking collectives, body(): own = lax.all_to_all(copies, 'gx', 0, 0, tiled=True)  13.1 us
    pallas_call x1, Pallas kernels, body(): call(up_kernel, [tiles(64), tiles(64)], [(65, 16, 256)] * 2 + level(32, 1...  7.04 us
    ppermute x14, waiting for transfers between devices, swap(): return (lax.ppermute(a, axis, first), lax.ppermute(b, axis, second))  6.99 us
    pallas_call x1, Pallas kernels, body(): call(fine_down_kernel, [tiles(16), tiles(10), more, top] + [full] * 5, [t...  5 us
    pallas_call x1, Pallas kernels, body(): call(bottom_kernel, [(16, 16, 128)], level(16, 16, 128) + level(8, 8, 128...  2.33 us
    unnamed x8, local copies, waits for them, and re-layouts  2.23 us
    pallas_call x1, Pallas kernels, body(): call(middle_down_kernel, [tiles(24), full, full, more, more], [full, full...  2.19 us
  transfers between devices with their start and end apart: 14, of which 4 were waited for; matrix products, arithmetic and copies ran while one was open for 0% of the time, Pallas kernels for 14%

profile of v7, /device:TPU:24, one launch (start us, length us, event | category | flops | bytes accessed | tf_op | source)
XLA Modules:
  0.0 67.8 jit_solution(14604144396133796508)
XLA Ops:
  0.6 0.9 %copy-done = f32[64,8,128]{2,1,0:T(8,128)S(1)} copy-done((f32[64,8,128]{2,1,0:T(8,128)S(1)}, f32[64,8,128]{2,1,0:T(8,128)}, u32[]{:S(2)}) %copy-start) | copy-done | bytes 262168
  1.9 0.7 copy-done.2
  2.5 0.3 shard_map.51
  2.9 0.6 copy-done.3
  3.5 0.4 shard_map.52
  3.9 3.0 %collective-permute-start.1 = (f32[32,8,128]{2,1,0:T(8,128)S(1)}, f32[32,8,128]{2,1,0:T(8,128)S(1)}, u32[]{:S(2)}, u32[]{:S(2)}) collective-permute-start(f32[32,8,128]{2,1,0:T(8,128)S(1)} %get-tuple-element.48), channel_id=1, source_target_pairs={{0,31},{1,2},{2,1},{3,4},{4,3},{5,6},{6,5},{7,8},{8,7},{9,10},{10,... | collective-permute-start | bytes 393224 | tf_op jit(solution)/shard_map/ppermute | solution.py:655
  7.0 1.9 %collective-permute-start.2 = (f32[80,8,128]{2,1,0:T(8,128)S(1)}, f32[80,8,128]{2,1,0:T(8,128)S(1)}, u32[]{:S(2)}, u32[]{:S(2)}) collective-permute-start(f32[80,8,128]{2,1,0:T(8,128)S(1)} %get-tuple-element.52), channel_id=1, source_target_pairs={{0,32},{32,0},{64,96},{96,64},{128,160},{160,128},{192,224},{224,1... | collective-permute-start | bytes 983048 | tf_op jit(solution)/shard_map/ppermute | solution.py:655
  8.9 4.9 %collective-permute-start.3 = (f32[80,8,128]{2,1,0:T(8,128)S(1)}, f32[80,8,128]{2,1,0:T(8,128)S(1)}, u32[]{:S(2)}, u32[]{:S(2)}) collective-permute-start(f32[80,8,128]{2,1,0:T(8,128)S(1)} %get-tuple-element.53), channel_id=1, source_target_pairs={{0,224},{32,64},{64,32},{96,128},{128,96},{160,192},{192,160},{224... | collective-permute-start | bytes 983048 | tf_op jit(solution)/shard_map/ppermute | solution.py:655
  14.0 3.5 %collective-permute-start.5 = (f32[32,8,128]{2,1,0:T(8,128)S(1)}, f32[32,8,128]{2,1,0:T(8,128)S(1)}, u32[]{:S(2)}, u32[]{:S(2)}) collective-permute-start(f32[32,8,128]{2,1,0:T(8,128)S(1)} %get-tuple-element.55), channel_id=1, source_target_pairs={{0,224},{32,64},{64,32},{96,128},{128,96},{160,192},{192,160},{224... | collective-permute-start | bytes 393224 | tf_op jit(solution)/shard_map/ppermute | solution.py:655
  17.6 1.5 %shard_map.53 = (f32[64,8,256]{2,1,0:T(8,128)S(1)}, f32[64,8,256]{2,1,0:T(8,128)S(1)}, f32[65,8,256]{2,1,0:T(8,128)S(1)}, f32[32,8,128]{2,1,0:T(8,128)S(1)}, f32[20,8,128]{2,1,0:T(8,128)S(1)}) custom-call(f32[64,8,128]{2,1,0:T(8,128)S(1)} %copy-done.1, f32[64,8,128]{2,1,0:T(8,128)S(1)} %copy-done.2, f32[64,8,128]{2,1,0:T(8,128)S(1)} %copy-done.3, ...), custom_call_target="tpu_custom_call" | custom-call | flops 3000000000 | bytes 9000000 | tf_op jit(solution)/shard_map/pallas_call | solution.py:673
  19.1 5.7 %collective-permute-start.9 = (f32[20,8,128]{2,1,0:T(8,128)S(1)}, f32[20,8,128]{2,1,0:T(8,128)S(1)}, u32[]{:S(2)}, u32[]{:S(2)}) collective-permute-start(f32[20,8,128]{2,1,0:T(8,128)S(1)} %get-tuple-element.59), channel_id=1, source_target_pairs={{0,224},{32,64},{64,32},{96,128},{128,96},{160,192},{192,160},{224... | collective-permute-start | bytes 245768 | tf_op jit(solution)/shard_map/ppermute | solution.py:655
  24.8 5.0 %shard_map.55 = (f32[16,8,128]{2,1,0:T(8,128)S(1)}, f32[10,8,128]{2,1,0:T(8,128)S(1)}, f32[65,16,256]{2,1,0:T(8,128)S(1)}, f32[64,8,256]{2,1,0:T(8,128)S(1)}, f3...) custom-call(f32[64,8,256]{2,1,0:T(8,128)S(1)} %get-tuple-element.49., ...), custom_call_target="tpu_custom_call" | custom-call | flops 49999998976 | bytes 150000000 | tf_op jit(solution)/shard_map/pallas_call | solution.py:679
  29.9 2.0 %collective-permute-start.7 = (f32[10,8,128]{2,1,0:T(8,128)S(1)}, f32[10,8,128]{2,1,0:T(8,128)S(1)}, u32[]{:S(2)}, u32[]{:S(2)}) collective-permute-start(f32[10,8,128]{2,1,0:T(8,128)S(1)} %get-tuple-element.57), channel_id=1, source_target_pairs={{0,224},{32,64},{64,32},{96,128},{128,96},{160,192},{192,160},{224... | collective-permute-start | bytes 122888 | tf_op jit(solution)/shard_map/ppermute | solution.py:655
  32.2 1.7 %collective-permute-done.6.ga = f32[10,8,128]{2,1,0:T(8,128)S(1)} collective-permute-done((f32[10,8,128]{2,1,0:T(8,128)S(1)}, f32[10,8,128]{2,1,0:T(8,128)S(1)}, u32[]{:S(2)}, u32[]{:S(2)}) %collective-permute-start.6) | collective-permute-done | bytes 40992 | tf_op jit(solution)/shard_map/ppermute | solution.py:655
  33.9 1.3 %collective-permute-done.7.gb = f32[10,8,128]{2,1,0:T(8,128)S(1)} collective-permute-done((f32[10,8,128]{2,1,0:T(8,128)S(1)}, f32[10,8,128]{2,1,0:T(8,128)S(1)}, u32[]{:S(2)}, u32[]{:S(2)}) %collective-permute-start.7) | collective-permute-done | bytes 40992 | tf_op jit(solution)/shard_map/ppermute | solution.py:655
  35.2 2.2 %shard_map.57 = (f32[24,8,128]{2,1,0:T(8,128)S(1)}, f32[32,16,128]{2,1,0:T(8,128)S(1)}, f32[32,16,128]{2,1,0:T(8,128)S(1)}, f32[33,16,128]{2,1,0:T(8,128)S(1)}, f32[33,16,128]{2,1,0:T(8,128)S(1)}) custom-call(f32[16,8,128]{2,1,0:T(8,128)S(1)} %get-tuple-element.56.source_in, f32[10,8,128]{2,1,0:T(8,128)S(1)} %collective-permute-done.6.ga, ...), custom_call_target="tpu_custom_call" | custom-call | flops 49999998976 | bytes 150000000 | tf_op jit(solution)/shard_map/pallas_call | solution.py:690
  37.4 13.1 %all_to_all.5.own._ = f32[24,8,128]{2,1,0:T(8,128)S(1)} all-to-all(f32[24,8,128]{2,1,0:T(8,128)S(1)} %get-tuple-element.63), channel_id=1, replica_groups=mesh['gx'=8,'gy'=32] {'gx'}, dimensions={0} | all-to-all | bytes 196608 | tf_op jit(solution)/shard_map/all_to_all | solution.py:697
  50.5 2.3 %collective-permute-start.11 = (f32[24,8,128]{2,1,0:T(8,128)S(1)}, f32[24,8,128]{2,1,0:T(8,128)S(1)}, u32[]{:S(2)}, u32[]{:S(2)}) collective-permute-start(f32[24,8,128]{2,1,0:T(8,128)S(1)} %all_to_all.5.own._), channel_id=1, source_target_pairs={{0,31},{1,2},{2,1},{3,4},{4,3},{5,6},{6,5},{7,8},{8,7},{9,10},{10,... | collective-permute-start | bytes 294920 | tf_op jit(solution)/shard_map/ppermute | solution.py:655
  53.0 0.7 collective-permute-start.12
  53.7 0.4 collective-permute-start.13
  54.1 2.5 %collective-permute-done.11.yb = f32[24,8,128]{2,1,0:T(8,128)S(1)} collective-permute-done((f32[24,8,128]{2,1,0:T(8,128)S(1)}, f32[24,8,128]{2,1,0:T(8,128)S(1)}, u32[]{:S(2)}, u32[]{:S(2)}) %collective-permute-start.11) | collective-permute-done | bytes 98336 | tf_op jit(solution)/shard_map/ppermute | solution.py:655
  56.6 2.3 %shard_map.58.v2 = f32[16,16,128]{2,1,0:T(8,128)S(1)} custom-call(f32[24,8,128]{2,1,0:T(8,128)S(1)} %all_to_all.5.own._, f32[24,8,128]{2,1,0:T(8,128)S(1)} %collective-permute-done.10.ya, f32[24,8,128]{2,1,0:T(8,128)S(1)} %collective-permute-done.11.yb), custom_call_target="tpu_custom_call" | custom-call | flops 49999998976 | bytes 150000000 | tf_op jit(solution)/shard_map/pallas_call | solution.py:707
  59.0 1.5 %collective-permute-done.13.xb = f32[46,8,128]{2,1,0:T(8,128)S(1)} collective-permute-done((f32[46,8,128]{2,1,0:T(8,128)S(1)}, f32[46,8,128]{2,1,0:T(8,128)S(1)}, u32[]{:S(2)}, u32[]{:S(2)}) %collective-permute-start.13) | collective-permute-done | bytes 188448 | tf_op jit(solution)/shard_map/ppermute | solution.py:655
  60.7 7.0 %shard_map.61 = (f32[64,8,128]{2,1,0:T(8,128)}, f32[64,8,128]{2,1,0:T(8,128)}) custom-call(f32[16,16,128]{2,1,0:T(8,128)S(1)} %shard_map.58.v2, f32[46,8,128]{2,1,0:T(8,128)S(1)} %collective-permute-done.12.xa, f32[46,8,128]{2,1,0:T(8,128)S(1)} %collective-permute-done.13.xb, f32[32,16,128]{2,1,0:T(8,128)S(1)} %get-tuple-element.68.f1, ...), custom_call_target="tpu_custom_call" | custom-call | flops 1000000000 | bytes 3000000 | tf_op jit(solution)/shard_map/pallas_call | solution.py:715
  (25 shorter events, 1.5 us)
Async XLA Ops:
  0.6 1.0 %copy-start = (f32[64,8,128]{2,1,0:T(8,128)S(1)}, f32[64,8,128]{2,1,0:T(8,128)}, u32[]{:S(2)}) copy-start(f32[64,8,128]{2,1,0:T(8,128)} %f.1) | copy-start | bytes 786436
  1.6 0.9 %copy-start.2 = (f32[64,8,128]{2,1,0:T(8,128)S(1)}, f32[64,8,128]{2,1,0:T(8,128)}, u32[]{:S(2)}) copy-start(f32[64,8,128]{2,1,0:T(8,128)} %a.1) | copy-start | bytes 786436
  2.5 0.9 %copy-start.3 = (f32[64,8,128]{2,1,0:T(8,128)S(1)}, f32[64,8,128]{2,1,0:T(8,128)}, u32[]{:S(2)}) copy-start(f32[64,8,128]{2,1,0:T(8,128)} %b.1) | copy-start | bytes 786436
  3.8 10.0 %collective-permute-start = (f32[32,8,128]{2,1,0:T(8,128)S(1)}, f32[32,8,128]{2,1,0:T(8,128)S(1)}, u32[]{:S(2)}, u32[]{:S(2)}) collective-permute-start(f32[32,8,128]{2,1,0:T(8,128)S(1)} %get-tuple-element.47), channel_id=1, source_target_pairs={{0,1},{1,0},{2,3},{3,2},{4,5},{5,4},{6,7},{7,6},{8,9},{9,8},{10,11... | collective-permute-start | bytes 393224 | tf_op jit(solution)/shard_map/ppermute | solution.py:655
  3.9 9.9 %collective-permute-start.1 = (f32[32,8,128]{2,1,0:T(8,128)S(1)}, f32[32,8,128]{2,1,0:T(8,128)S(1)}, u32[]{:S(2)}, u32[]{:S(2)}) collective-permute-start(f32[32,8,128]{2,1,0:T(8,128)S(1)} %get-tuple-element.48), channel_id=1, source_target_pairs={{0,31},{1,2},{2,1},{3,4},{4,3},{5,6},{6,5},{7,8},{8,7},{9,10},{10,... | collective-permute-start | bytes 393224 | tf_op jit(solution)/shard_map/ppermute | solution.py:655
  7.0 17.8 %collective-permute-start.2 = (f32[80,8,128]{2,1,0:T(8,128)S(1)}, f32[80,8,128]{2,1,0:T(8,128)S(1)}, u32[]{:S(2)}, u32[]{:S(2)}) collective-permute-start(f32[80,8,128]{2,1,0:T(8,128)S(1)} %get-tuple-element.52), channel_id=1, source_target_pairs={{0,32},{32,0},{64,96},{96,64},{128,160},{160,128},{192,224},{224,1... | collective-permute-start | bytes 983048 | tf_op jit(solution)/shard_map/ppermute | solution.py:655
  8.9 8.7 %copy-start.1 = (f32[64,8,128]{2,1,0:T(8,128)S(1)}, f32[64,8,128]{2,1,0:T(8,128)}, u32[]{:S(2)}) copy-start(f32[64,8,128]{2,1,0:T(8,128)} %f.1) | copy-start | bytes 786436
  8.9 15.9 %collective-permute-start.3 = (f32[80,8,128]{2,1,0:T(8,128)S(1)}, f32[80,8,128]{2,1,0:T(8,128)S(1)}, u32[]{:S(2)}, u32[]{:S(2)}) collective-permute-start(f32[80,8,128]{2,1,0:T(8,128)S(1)} %get-tuple-element.53), channel_id=1, source_target_pairs={{0,224},{32,64},{64,32},{96,128},{128,96},{160,192},{192,160},{224... | collective-permute-start | bytes 983048 | tf_op jit(solution)/shard_map/ppermute | solution.py:655
  13.9 5.2 %collective-permute-start.4 = (f32[32,8,128]{2,1,0:T(8,128)S(1)}, f32[32,8,128]{2,1,0:T(8,128)S(1)}, u32[]{:S(2)}, u32[]{:S(2)}) collective-permute-start(f32[32,8,128]{2,1,0:T(8,128)S(1)} %get-tuple-element.54), channel_id=1, source_target_pairs={{0,32},{32,0},{64,96},{96,64},{128,160},{160,128},{192,224},{224,1... | collective-permute-start | bytes 393224 | tf_op jit(solution)/shard_map/ppermute | solution.py:655
  14.0 10.8 %collective-permute-start.5 = (f32[32,8,128]{2,1,0:T(8,128)S(1)}, f32[32,8,128]{2,1,0:T(8,128)S(1)}, u32[]{:S(2)}, u32[]{:S(2)}) collective-permute-start(f32[32,8,128]{2,1,0:T(8,128)S(1)} %get-tuple-element.55), channel_id=1, source_target_pairs={{0,224},{32,64},{64,32},{96,128},{128,96},{160,192},{192,160},{224... | collective-permute-start | bytes 393224 | tf_op jit(solution)/shard_map/ppermute | solution.py:655
  19.0 13.2 %collective-permute-start.8 = (f32[20,8,128]{2,1,0:T(8,128)S(1)}, f32[20,8,128]{2,1,0:T(8,128)S(1)}, u32[]{:S(2)}, u32[]{:S(2)}) collective-permute-start(f32[20,8,128]{2,1,0:T(8,128)S(1)} %get-tuple-element.59), channel_id=1, source_target_pairs={{0,32},{32,0},{64,96},{96,64},{128,160},{160,128},{192,224},{224,1... | collective-permute-start | bytes 245768 | tf_op jit(solution)/shard_map/ppermute | solution.py:655
  19.1 13.1 %collective-permute-start.9 = (f32[20,8,128]{2,1,0:T(8,128)S(1)}, f32[20,8,128]{2,1,0:T(8,128)S(1)}, u32[]{:S(2)}, u32[]{:S(2)}) collective-permute-start(f32[20,8,128]{2,1,0:T(8,128)S(1)} %get-tuple-element.59), channel_id=1, source_target_pairs={{0,224},{32,64},{64,32},{96,128},{128,96},{160,192},{192,160},{224... | collective-permute-start | bytes 245768 | tf_op jit(solution)/shard_map/ppermute | solution.py:655
  29.8 4.1 %collective-permute-start.6 = (f32[10,8,128]{2,1,0:T(8,128)S(1)}, f32[10,8,128]{2,1,0:T(8,128)S(1)}, u32[]{:S(2)}, u32[]{:S(2)}) collective-permute-start(f32[10,8,128]{2,1,0:T(8,128)S(1)} %get-tuple-element.57), channel_id=1, source_target_pairs={{0,32},{32,0},{64,96},{96,64},{128,160},{160,128},{192,224},{224,1... | collective-permute-start | bytes 122888 | tf_op jit(solution)/shard_map/ppermute | solution.py:655
  29.9 5.3 %collective-permute-start.7 = (f32[10,8,128]{2,1,0:T(8,128)S(1)}, f32[10,8,128]{2,1,0:T(8,128)S(1)}, u32[]{:S(2)}, u32[]{:S(2)}) collective-permute-start(f32[10,8,128]{2,1,0:T(8,128)S(1)} %get-tuple-element.57), channel_id=1, source_target_pairs={{0,224},{32,64},{64,32},{96,128},{128,96},{160,192},{192,160},{224... | collective-permute-start | bytes 122888 | tf_op jit(solution)/shard_map/ppermute | solution.py:655
  50.5 3.6 %collective-permute-start.10 = (f32[24,8,128]{2,1,0:T(8,128)S(1)}, f32[24,8,128]{2,1,0:T(8,128)S(1)}, u32[]{:S(2)}, u32[]{:S(2)}) collective-permute-start(f32[24,8,128]{2,1,0:T(8,128)S(1)} %all_to_all.5.own._), channel_id=1, source_target_pairs={{0,1},{1,0},{2,3},{3,2},{4,5},{5,4},{6,7},{7,6},{8,9},{9,8},{10,11... | collective-permute-start | bytes 294920 | tf_op jit(solution)/shard_map/ppermute | solution.py:655
  50.5 6.2 %collective-permute-start.11 = (f32[24,8,128]{2,1,0:T(8,128)S(1)}, f32[24,8,128]{2,1,0:T(8,128)S(1)}, u32[]{:S(2)}, u32[]{:S(2)}) collective-permute-start(f32[24,8,128]{2,1,0:T(8,128)S(1)} %all_to_all.5.own._), channel_id=1, source_target_pairs={{0,31},{1,2},{2,1},{3,4},{4,3},{5,6},{6,5},{7,8},{8,7},{9,10},{10,... | collective-permute-start | bytes 294920 | tf_op jit(solution)/shard_map/ppermute | solution.py:655
  53.0 6.0 %collective-permute-start.12 = (f32[46,8,128]{2,1,0:T(8,128)S(1)}, f32[46,8,128]{2,1,0:T(8,128)S(1)}, u32[]{:S(2)}, u32[]{:S(2)}) collective-permute-start(f32[46,8,128]{2,1,0:T(8,128)S(1)} %get-tuple-element.66), channel_id=1, source_target_pairs={{0,32},{32,0},{64,96},{96,64},{128,160},{160,128},{192,224},{224,1... | collective-permute-start | bytes 565256 | tf_op jit(solution)/shard_map/ppermute | solution.py:655
  53.7 6.8 %collective-permute-start.13 = (f32[46,8,128]{2,1,0:T(8,128)S(1)}, f32[46,8,128]{2,1,0:T(8,128)S(1)}, u32[]{:S(2)}, u32[]{:S(2)}) collective-permute-start(f32[46,8,128]{2,1,0:T(8,128)S(1)} %get-tuple-element.67), channel_id=1, source_target_pairs={{0,224},{32,64},{64,32},{96,128},{128,96},{160,192},{192,160},{224... | collective-permute-start | bytes 565256 | tf_op jit(solution)/shard_map/ppermute | solution.py:655
